TPU v7x, 128 devices: a whole 4x4x4 slice. The times are simulated.
128 devices in a mesh: curve: 16 (over x, z), sub: 8 (over y, core).
Axes of the slice: x: 4, y: 4, z: 4, core: 2. Of those that a mesh axis runs over, the one named last changes fastest.
Arguments:
- coefficients: float32 [5, 512, 16384], P(None, None, ('curve', 'sub')), may hold values from -6 to 6
- old_degree: int32 [16384], P(('curve', 'sub')), may hold values from 3 to 7
- new_degree: int32 [16384], P(('curve', 'sub')), may hold values from 3 to 7
- destination: int32 [16384], P(('curve', 'sub')), may hold values from 0 to 16383, as said below
- metric: float32 [3, 16384], P(None, ('curve', 'sub')), may hold values from 0.5 to 2
- neighbours: int32 [4, 16384], P(None, ('curve', 'sub')), may hold values from 0 to 128, as said below
- mortar_up: int32 [2, 18432], P(None, ('curve', 'sub')), may hold values from 0 to 127, as said below
- mortar_low: int32 [2, 18432], P(None, ('curve', 'sub')), may hold values from 0 to 127, as said below
Outputs:
- advanced: float32 [5, 512, 16384], P(None, None, ('curve', 'sub'))
Inputs may be any that keep to these rules, and one draw needn't show every extreme that they name: A permutation of 0..16383; the new owner of element g is destination[g] // 128. Each device sends exactly 2 elements to each of 64 distinct devices and none to the others, and receives exactly 2 from each of 64 devices. `neighbours`: local index, on the element's own device, of the element across its +x, -x, +z, -z face, or 128 at the far field; mutual: b is across a's +x face exactly when a is across b's -x face, and likewise for z. `mortar_up`: row 0: local element whose +y face the mortar touches; row 1: 0 if the mortar covers that face whole, 1 or 2 if it covers its lower or upper half along x. Entries of device q are positions q * 144 onward. Every element of a device appears in its list; on each side of each interface 128 // 8 faces are split between two mortars with codes 1 and 2, whose two partners are whole faces. `mortar_low`: as mortar_up for the -y faces of the device's lower interface; mortar m here meets mortar m of the upper interface of the device below.
All inputs are finite; a program needn't handle non-finite values.
Results may differ from a plain program's by a relative error of at most 0.0001.
Values sent between devices are 32-bit elements; how exact they have to be, the bound alone decides.
No kernel may reach another device: no remote copies, remote signals or barrier semaphores. Data moves between devices by JAX's collectives and lax.ppermute only.
A program may use at most 128 MiB of HBM per device.

v0:
```python
import functools
import math

import jax
import jax.numpy as jnp
import numpy as np
from jax import lax
from jax.experimental import pallas as pl
from jax.experimental.pallas import tpu as pltpu
from jax.sharding import PartitionSpec as P

NV = 5
N = 8
MODES = N * N * N
ROWS = NV * MODES
FACE = NV * N * N
E = 128
BLOCK = 41
STEP = 0.006
ALPHA = (0.0, 0.75, 1.0 / 3.0)
BETA = (1.0, 0.25, 2.0 / 3.0)
PAY = FACE + 8
LIMIT = 24 * 1024 * 1024
F32 = jnp.float32
BF16 = jnp.bfloat16

VMEM = pl.BlockSpec(memory_space=pltpu.VMEM)
PARAMS = pltpu.CompilerParams(vmem_limit_bytes=LIMIT)


def legendre_pair(degree_n, points):
    points = np.asarray(points) + 0.0
    value_before = points * 0.0
    value_now = points * 0.0 + 1.0
    for order in range(1, degree_n + 1):
        value_next = ((2 * order - 1) * points * value_now - (order - 1) * value_before) / order
        value_before = value_now
        value_now = value_next
    return (value_now, value_before)


def half_table():
    nodes, weights = np.polynomial.legendre.leggauss(2 * N + 2)
    table = np.zeros((N, N))
    for a in range(N):
        for b in range(a, N):
            fa = math.sqrt((2 * a + 1) / 2.0) * legendre_pair(a, nodes)[0]
            fb = math.sqrt((2 * b + 1) / 2.0) * legendre_pair(b, (nodes - 1.0) / 2.0)[0]
            table[a, b] = np.sum(weights * fa * fb)
    return table


HALF = half_table()
RESTRICT = [[float(HALF[a, b] * math.sqrt((2 * a + 1) / (2 * b + 1))) for b in range(N)] for a in range(N)]
PROJECT = [[float(0.5 * HALF[a, b] * math.sqrt((2 * b + 1) / (2 * a + 1))) for a in range(N)] for b in range(N)]


def z_table():
    out = np.zeros((320, 256))
    for col in range(256):
        line, k = divmod(col, N)
        out[line, col] = 1.0
        out[32 + line, col] = (-1.0) ** k
        for a in range(k):
            if (k - a) % 2 == 1:
                out[64 + line * N + a, col] = 1.0
    return out


def iota(shape, axis):
    return lax.broadcasted_iota(jnp.int32, shape, axis)


def split(x):
    high = x.astype(BF16)
    return high, (x - high.astype(F32)).astype(BF16)


def dot(a, b):
    return lax.dot_general(a, b, (((1,), (0,)), ((), ())), preferred_element_type=F32)


def dot_nt(a, b):
    return lax.dot_general(a, b, (((1,), (1,)), ((), ())), preferred_element_type=F32)


def onehot(flag):
    return jnp.where(flag, 1.0, 0.0)


def pack_kernel(coef, old, new, dest, out):
    row = iota((E, E), 0)
    col = iota((E, E), 1)
    new_row = new[...]
    kept = jnp.minimum(old[...], new_row)
    target = lax.shift_right_logical(dest[...], 7)
    slot = dest[...] & (E - 1)
    target_f = jnp.broadcast_to(target.astype(F32), (E, E))
    same = target_f == target_f.T
    rank = jnp.sum(onehot(same & (row < col)), axis=0, keepdims=True)
    here = jnp.broadcast_to(target, (E, E)) == row
    pick0 = onehot(here & (rank < 0.5)).astype(BF16)
    pick1 = onehot(here & (rank > 0.5)).astype(BF16)
    slot_f = jnp.broadcast_to((slot - E).astype(F32), (E, E))
    new_f = jnp.broadcast_to(new_row.astype(F32), (E, E))
    tags0 = jnp.where(row == 0, slot_f, jnp.where(row == 1, new_f, 0.0)).astype(BF16)
    tags1 = jnp.where(row == 2, slot_f, jnp.where(row == 3, new_f, 0.0)).astype(BF16)
    tags = dot_nt(pick0, tags0) + dot_nt(pick1, tags1)
    tags = tags + jnp.where((col == 0) | (col == 2), float(E), 0.0)
    out[pl.ds(40, E, stride=BLOCK), :] = tags
    pick = jnp.concatenate([pick0, pick1], axis=0)
    pick = jnp.concatenate([pick, pick], axis=1)
    for q in range(4):
        mode = row + E * q
        i = lax.shift_right_logical(mode, 6)
        j = lax.shift_right_logical(mode, 3) & 7
        k = mode & 7
        live = jnp.maximum(jnp.maximum(i, j), k) <= kept
        weight = ((2 * i + 1) * (2 * j + 1) * (2 * k + 1)).astype(F32)
        weight = jnp.where(live, jnp.sqrt(weight), 0.0)
        for v in range(NV):
            g = 4 * v + q
            high, low = split(coef[v, E * q : E * (q + 1), :] * weight)
            moved = dot_nt(pick, jnp.concatenate([high, low], axis=1))
            out[pl.ds(g, E, stride=BLOCK), :] = moved[:E]
            out[pl.ds(20 + g, E, stride=BLOCK), :] = moved[E:]


def write_traces(even, odd, upper, lower, v, i):
    rows = slice((v * N + i) * N, (v * N + i) * N + N)
    upper[rows, :] = even + odd
    lower[rows, :] = even - odd


def unpack_kernel(got, mortar_up, mortar_low, solution, degree, upper, lower):
    row = iota((E, E), 0)
    tags = got[pl.ds(40, E, stride=BLOCK), :].T
    place0 = onehot(row.astype(F32) == tags[0:1, :]).astype(BF16)
    place1 = onehot(row.astype(F32) == tags[2:3, :]).astype(BF16)
    place = jnp.concatenate([place0, place1], axis=1)
    degrees = jnp.concatenate([tags[1:2, :], tags[3:4, :]], axis=1)
    degrees = jnp.broadcast_to(degrees, (16, 2 * E)).astype(BF16)
    degree[...] = dot_nt(degrees, place)[:8, :]
    for g in range(20):
        both = jnp.concatenate(
            [got[pl.ds(g, E, stride=BLOCK), :], got[pl.ds(20 + g, E, stride=BLOCK), :]], axis=0
        )
        high, low = split(both)
        moved = dot(place, jnp.concatenate([high, low], axis=1))
        solution[E * g : E * (g + 1), :] = (moved[:, :E] + moved[:, E:]).T
    for v in range(NV):
        for i in range(N):
            base = v * MODES + i * 64
            line = [solution[base + 8 * j : base + 8 * j + 8, :] for j in range(N)]
            even = (line[0] + line[2]) + (line[4] + line[6])
            odd = (line[1] + line[3]) + (line[5] + line[7])
            write_traces(even, odd, upper, lower, v, i)
    for table, face in ((mortar_up, upper), (mortar_low, lower)):
        face[FACE:PAY, :] = jnp.full((PAY - FACE, E), -1.0, F32)
        face[FACE : FACE + 2, :] = table[:, 0:E].astype(F32)
        face[FACE + 2 : FACE + 4, 0:16] = table[:, E : E + 16].astype(F32)


def couple(d, first, k):
    half = [(0.5 * k) * d[v] for v in range(NV)]
    vel, pres = 0.5 * d[first], 0.5 * d[4]
    half[0] = half[0] + vel
    half[first] = half[first] + pres
    half[4] = half[4] + vel
    return half


def halves_of(plus, minus):
    return [p - m for p, m in zip(plus, minus)], [p + m for p, m in zip(plus, minus)]


def volume_kernel(alpha, beta, *refs):
    if alpha:
        first, *refs = refs
    (state, upper, lower, metric, near, ztab, out, xsum, zsum, xp, xm, zp, zm, xl, zl, cat) = refs
    row = iota((E, E), 0)
    gather = []
    for d in range(4):
        pick = onehot(row == near[d : d + 1, :]).astype(BF16)
        gather.append(jnp.concatenate([pick, pick], axis=0))
    for v in range(NV):
        for h in range(2):
            base = v * MODES + 256 * h
            high, low = split(state[base : base + 256, :])
            both = jnp.concatenate([high, low], axis=1)
            count = 320 if v >= 3 else 64
            sums = dot(ztab[0:count, :], both)
            sums = sums[:, :E] + sums[:, E:]
            zp[v * 64 + 32 * h : v * 64 + 32 * h + 32, :] = sums[0:32]
            zm[v * 64 + 32 * h : v * 64 + 32 * h + 32, :] = sums[32:64]
            if v >= 3:
                zsum[(v - 3) * MODES + 256 * h : (v - 3) * MODES + 256 * h + 256, :] = sums[64:]
    for v in range(NV):
        for j in range(N):
            line = [state[v * MODES + 64 * i + 8 * j : v * MODES + 64 * i + 8 * j + 8, :] for i in range(N)]
            even = (line[0] + line[2]) + (line[4] + line[6])
            odd = (line[1] + line[3]) + (line[5] + line[7])
            write_traces(even, odd, xp, xm, v, j)

    def outer(face, pick):
        for v in range(NV):
            high, low = split(face[64 * v : 64 * v + 64, :])
            cat[64 * v : 64 * v + 64, 0:E] = high
            cat[64 * v : 64 * v + 64, E : 2 * E] = low
        return dot(cat[...], pick)

    def by_variable(x):
        return [x[64 * v : 64 * v + 64] for v in range(NV)]

    for plus, minus, where, first_v, k_minus, scale, result in (
        (xp, xm, (0, 1), 1, 2.0, 1.0, xl),
        (zp, zm, (2, 3), 3, 1.0, 0.5, zl),
    ):
        d_plus = by_variable(outer(minus, gather[where[0]]) - plus[...])
        d_minus = by_variable(outer(plus, gather[where[1]]) - minus[...])
        even, odd = halves_of(couple(d_plus, first_v, -1.0), couple(d_minus, first_v, k_minus))
        for v in range(NV):
            result[64 * v : 64 * v + 64, :] = scale * even[v] if scale != 1.0 else even[v]
            result[FACE + 64 * v : FACE + 64 * v + 64, :] = scale * odd[v] if scale != 1.0 else odd[v]

    full = [jnp.broadcast_to(metric[d : d + 1, :], (8, E)) for d in range(3)]
    kx = [full[0] * (-0.5 * beta * STEP * (2 * a + 1)) for a in range(N)]
    ky = [full[1] * (-0.05 * beta * STEP * (2 * a + 1)) for a in range(N)]
    kz = full[2] * (-beta * STEP) * (2 * iota((8, E), 0) + 1).astype(F32)
    odd_k = (iota((8, E), 0) & 1) == 1

    def at(ref, start):
        return ref[pl.ds(pl.multiple_of(start, 8), 8), :]

    def x_pass(j, carry):
        s = [
            [at(xl, 64 * v + 8 * j) for v in range(NV)],
            [at(xl, FACE + 64 * v + 8 * j) for v in range(NV)],
        ]
        for i in range(N - 1, -1, -1):
            rows = [v * MODES + 64 * i + 8 * j for v in range(NV)]
            now = s[i % 2]
            for v in range(NV):
                xsum[pl.ds(pl.multiple_of(rows[v], 8), 8), :] = kx[i] * now[v]
            if i:
                r, u, y, w, p = [at(state, rows[v]) for v in range(NV)]
                twice = u + u
                f = [r + twice, u + (p + p), y, w, p + twice]
                s[(i + 1) % 2] = [a + b for a, b in zip(s[(i + 1) % 2], f)]
        return carry

    lax.fori_loop(0, N, x_pass, 0)

    def y_pass(i, carry):
        d_plus = [-at(upper, 64 * v + 8 * i) for v in range(NV)]
        d_minus = [-at(lower, 64 * v + 8 * i) for v in range(NV)]
        even, odd = halves_of(couple(d_plus, 2, -1.0), couple(d_minus, 2, 1.1))
        s = [[10.0 * x for x in even], [10.0 * x for x in odd]]
        z_even = [at(zl, 64 * v + 8 * i) for v in range(NV)]
        z_odd = [at(zl, FACE + 64 * v + 8 * i) for v in range(NV)]
        for j in range(N - 1, -1, -1):
            inner = 64 * i + 8 * j
            rows = [v * MODES + inner for v in range(NV)]
            c = [at(state, rows[v]) for v in range(NV)]
            sw, sp = at(zsum, inner), at(zsum, MODES + inner)
            zs = (sw, None, None, sp, sw)
            now = s[j % 2]
            for v in range(NV):
                lift = jnp.where(
                    odd_k,
                    jnp.broadcast_to(z_odd[v][j : j + 1, :], (8, E)),
                    jnp.broadcast_to(z_even[v][j : j + 1, :], (8, E)),
                )
                if zs[v] is not None:
                    lift = lift + zs[v]
                total = at(xsum, rows[v]) + ky[j] * now[v] + kz * lift
                if alpha:
                    total = total + (alpha * at(first, rows[v]) + beta * c[v])
                else:
                    total = total + c[v]
                out[pl.ds(pl.multiple_of(rows[v], 8), 8), :] = total
            if j:
                r, u, y, w, p = c
                y20 = 20.0 * y
                f = [r + y20, u, y + 20.0 * p, w, p + y20]
                s[(j + 1) % 2] = [a + b for a, b in zip(s[(j + 1) % 2], f)]
        return carry

    lax.fori_loop(0, N, y_pass, 0)


def build_routes(pay, table):
    wide = iota((E, 2 * E), 0).astype(F32)
    pad = jnp.full((1, E - 16), -1.0, F32)

    def own(r):
        return jnp.concatenate([table[r : r + 1, 0:E].astype(F32), table[r : r + 1, E : E + 16].astype(F32), pad], axis=1)

    far_elem = jnp.concatenate([pay[FACE : FACE + 1, :], pay[FACE + 2 : FACE + 3, :]], axis=1)
    far_half = jnp.concatenate([pay[FACE + 1 : FACE + 2, :], pay[FACE + 3 : FACE + 4, :]], axis=1)
    own_elem, own_half = own(0), own(1)
    far_pick = onehot(wide == far_elem)
    own_pick = onehot(wide == own_elem).astype(BF16)
    far_whole, own_whole = onehot(far_half == 0.0), onehot(own_half == 0.0)
    far_1, far_2 = onehot(far_half == 1.0), onehot(far_half == 2.0)
    own_1, own_2 = onehot(own_half == 1.0), onehot(own_half == 2.0)
    weights = (
        far_whole * own_whole,
        own_whole * (far_1 + far_2),
        own_whole * (far_1 - far_2),
        far_whole * (own_1 + own_2),
        far_whole * (own_1 - own_2),
    )
    return [dot_nt((far_pick * w).astype(BF16), own_pick).astype(BF16) for w in weights]


def post_kernel(stage, *refs):
    beta = BETA[stage]
    if stage == 0:
        (partial, above, below, metric, degree, table_up, table_low, out, upper, lower, routes, cat_up, cat_low) = refs
        for side, (pay, table) in enumerate(((above, table_up), (below, table_low))):
            for n, route in enumerate(build_routes(pay, table)):
                for part in range(2):
                    start = side * 10 * E + part * 5 * E + n * E
                    routes[start : start + E, :] = route
    elif stage == 1:
        (partial, above, below, metric, degree, routes, out, upper, lower, cat_up, cat_low) = refs
    else:
        (partial, above, below, metric, degree, routes, out, cat_up, cat_low) = refs

    def mix(line, table, parity, transposed):
        result = []
        for a in range(N):
            total = None
            for b in range(N):
                if (a + b) % 2 != parity or (b > a if transposed else b < a):
                    continue
                term = table[a][b] * line[b]
                total = term if total is None else total + term
            result.append(jnp.zeros_like(line[0]) if total is None else total)
        return jnp.concatenate(result, axis=0)

    far = []
    for side, (face, cat) in enumerate(((above, cat_up), (below, cat_low))):
        for v in range(NV):
            whole = face[64 * v : 64 * v + 64, :]
            line = [whole[8 * i : 8 * i + 8] for i in range(N)]
            kinds = (
                whole,
                mix(line, RESTRICT, 0, False),
                mix(line, RESTRICT, 1, False),
                mix(line, PROJECT, 0, True),
                mix(line, PROJECT, 1, True),
            )
            for n, kind in enumerate(kinds):
                high, low = split(kind)
                cat[64 * v : 64 * v + 64, n * E : n * E + E] = high
                cat[64 * v : 64 * v + 64, (n + 5) * E : (n + 5) * E + E] = low
        far.append(dot(cat[...], routes[side * 10 * E : (side + 1) * 10 * E, :]))
    far_up, far_low = far
    k_row = iota((8, E), 0)
    deg = degree[...]
    masks = [onehot(jnp.maximum(k_row, n).astype(F32) <= deg) for n in range(N)]
    if stage == 2:
        back = 1.0 / jnp.sqrt((2 * k_row + 1).astype(F32))
        masks = [m * back for m in masks]
    full = jnp.broadcast_to(metric[1:2, :], (8, E))
    ky = [full * (-0.5 * beta * STEP * (2 * a + 1)) for a in range(N)]
    for i in range(N):
        up = [far_up[64 * v + 8 * i : 64 * v + 8 * i + 8] for v in range(NV)]
        low = [far_low[64 * v + 8 * i : 64 * v + 8 * i + 8] for v in range(NV)]
        lift = halves_of(couple(up, 2, -1.0), couple(low, 2, 1.1))
        for v in range(NV):
            sums = [None, None]
            for j in range(N):
                start = v * MODES + 64 * i + 8 * j
                value = masks[max(i, j)] * (partial[start : start + 8, :] + ky[j] * lift[j % 2][v])
                if stage == 2:
                    value = value * (1.0 / math.sqrt((2 * i + 1) * (2 * j + 1)))
                else:
                    sums[j % 2] = value if sums[j % 2] is None else sums[j % 2] + value
                out[start : start + 8, :] = value
            if stage < 2:
                write_traces(sums[0], sums[1], upper, lower, v, i)


def call(kernel, outs, scratch, args):
    return pl.pallas_call(
        kernel,
        out_shape=outs,
        in_specs=[VMEM] * len(args),
        out_specs=jax.tree.map(lambda _: VMEM, outs),
        scratch_shapes=scratch,
        compiler_params=PARAMS,
    )(*args)


def f32(*shape):
    return jax.ShapeDtypeStruct(shape, F32)


def swap(upper, lower):
    count = lax.axis_size("sub")
    below = lax.ppermute(upper, "sub", [(i, i + 1) for i in range(count - 1)])
    above = lax.ppermute(lower, "sub", [(i + 1, i) for i in range(count - 1)])
    return above, below


def shards(coefficients, old_degree, new_degree, destination, metric, near, mortar_up, mortar_low):
    ztab = jnp.asarray(z_table(), BF16)
    packed = call(
        pack_kernel,
        f32(E * BLOCK, E),
        [],
        (coefficients, old_degree.reshape(1, E), new_degree.reshape(1, E), destination.reshape(1, E)),
    )
    packed = packed.reshape(E, 1, BLOCK * E)
    got = lax.all_to_all(packed, ("curve", "sub"), split_axis=0, concat_axis=0, tiled=True)
    got = got.reshape(E * BLOCK, E)
    first, degree, upper, lower = call(
        unpack_kernel, (f32(ROWS, E), f32(8, E), f32(PAY, E), f32(PAY, E)), [], (got, mortar_up, mortar_low)
    )
    state = first
    routes = None
    for stage in range(3):
        above, below = swap(upper, lower)
        given = (state, upper, lower, metric, near, ztab)
        partial = call(
            functools.partial(volume_kernel, ALPHA[stage], BETA[stage]),
            f32(ROWS, E),
            [pltpu.VMEM((ROWS, E), F32), pltpu.VMEM((2 * MODES, E), F32)]
            + [pltpu.VMEM((FACE, E), F32)] * 4
            + [pltpu.VMEM((2 * FACE, E), F32)] * 2
            + [pltpu.VMEM((FACE, 2 * E), BF16)],
            (first,) + given if stage else given,
        )
        cats = [pltpu.VMEM((FACE, 10 * E), BF16)] * 2
        body = functools.partial(post_kernel, stage)
        faces = (f32(FACE, E), f32(FACE, E))
        if stage == 0:
            state, upper, lower, routes = call(
                body,
                (f32(ROWS, E),) + faces + (jax.ShapeDtypeStruct((20 * E, E), BF16),),
                cats,
                (partial, above, below, metric, degree, mortar_up, mortar_low),
            )
        elif stage == 1:
            state, upper, lower = call(
                body, (f32(ROWS, E),) + faces, cats, (partial, above, below, metric, degree, routes)
            )
        else:
            state = call(body, f32(ROWS, E), cats, (partial, above, below, metric, degree, routes))
    return state.reshape(NV, MODES, E)


def solution(mesh):
    lanes = P(None, ("curve", "sub"))
    rank = P(("curve", "sub"))
    cube = P(None, None, ("curve", "sub"))
    return jax.shard_map(
        shards,
        mesh=mesh,
        in_specs=(cube, rank, rank, rank, lanes, lanes, lanes, lanes),
        out_specs=cube,
        check_vma=False,
    )
```

profile of v0, /device:TPU:1, one launch (start us, length us, event | category | flops | bytes accessed | tf_op | source)
XLA Modules:
  0.0 83.7 jit_solution(3431476976240631651)
XLA Ops:
  0.0 0.0 copy-start.1
  0.0 1.3 %copy-done.1 = f32[5,512,128]{2,1,0:T(8,128)S(1)} copy-done((f32[5,512,128]{2,1,0:T(8,128)S(1)}, f32[5,512,128]{2,1,0:T(8,128)}, u32[]{:S(2)}) %copy-start.1) | copy-done | bytes 1310744
  1.3 0.0 copy-start.6
  1.3 0.7 copy-done.6
  2.0 0.0 copy-start.7
  2.0 0.7 copy-done.7
  2.6 0.0 copy-start.8
  2.6 0.7 copy-done.8
  3.3 1.0 %shard_map.91 = f32[5248,128]{1,0:T(8,128)S(1)} custom-call(f32[5,512,128]{2,1,0:T(8,128)S(1)} %copy-done.1, s32[1,128]{1,0:T(1,128)S(1)} %bitcast.8, s32[1,128]{1,0:T(1,128)S(1)} %bitcast.9, s32[1,128]{1,0:T(1,128)S(1)} %bitcast.10), custom_call_target="tpu_custom_call" | custom-call | tf_op jit(solution)/shard_map/pallas_call | solution.py:388
  4.3 0.0 copy-start.4
  4.3 0.0 copy-start.5
  4.3 48.1 %all_to_all.5 = f32[128,1,5248]{2,1,0:T(1,128)S(1)} all-to-all(f32[128,1,5248]{2,1,0:T(1,128)S(1)} %bitcast.7), channel_id=1, replica_groups=mesh['curve'=16,'sub'=8] {'curve','sub'}, dimensions={0} | all-to-all | bytes 5373952 | tf_op jit(solution)/shard_map/all_to_all | solution.py:418
  52.4 0.0 copy-done.4
  52.4 0.0 copy-done.5
  52.4 0.0 copy-start
  52.4 0.0 copy-start.2
  52.4 0.0 copy-start.3
  52.4 0.7 shard_map.92
  53.1 2.8 %collective-permute-start.1 = (f32[328,128]{1,0:T(8,128)S(1)}, f32[328,128]{1,0:T(8,128)S(1)}, u32[]{:S(2)}, u32[]{:S(2)}) collective-permute-start(f32[328,128]{1,0:T(8,128)S(1)} %get-tuple-element.17.refs_1_), channel_id=1, source_target_pairs={{0,1},{1,2},{2,3},{3,4},{4,5},{5,6},{6,7},{8,9},{9,10},{10,11},{11... | collective-permute-start | bytes 503816 | tf_op jit(solution)/shard_map/ppermute | solution.py:404
  56.0 1.9 %collective-permute-start = (f32[328,128]{1,0:T(8,128)S(1)}, f32[328,128]{1,0:T(8,128)S(1)}, u32[]{:S(2)}, u32[]{:S(2)}) collective-permute-start(f32[328,128]{1,0:T(8,128)S(1)} %get-tuple-element.18.refs_2_), channel_id=1, source_target_pairs={{1,0},{2,1},{3,2},{4,3},{5,4},{6,5},{7,6},{9,8},{10,9},{11,10},{12... | collective-permute-start | bytes 503816 | tf_op jit(solution)/shard_map/ppermute | solution.py:405
  57.9 0.0 copy-done
  57.9 0.0 copy-done.2
  57.9 0.0 copy-done.3
  57.9 1.6 %shard_map.93.refs_0_ = f32[2560,128]{1,0:T(8,128)S(1)} custom-call(f32[2560,128]{1,0:T(8,128)S(1)} %get-tuple-element.16.refs_0_, f32[328,128]{1,0:T(8,128)S(1)} %get-tuple-element.17.refs_1_, f32[328,128]{1,0:T(8,128)S(1)} %get-tuple-element.18.refs_2_, f32[3,128]{1,0:T(4,128)S(1)} %copy-done.2, s32[4,128]{1,0:T(4,128)S(1)} %copy-done.3, ...), custom_call_target="tpu_custom_call" | custom-call | tf_op jit(solution)/shard_map/pallas_call | solution.py:388
  59.5 0.0 collective-permute-done.1.refs_2_
  59.5 3.1 %collective-permute-done.refs_1_ = f32[328,128]{1,0:T(8,128)S(1)} collective-permute-done((f32[328,128]{1,0:T(8,128)S(1)}, f32[328,128]{1,0:T(8,128)S(1)}, u32[]{:S(2)}, u32[]{:S(2)}) %collective-permute-start) | collective-permute-done | bytes 167968 | tf_op jit(solution)/shard_map/ppermute | solution.py:405
  62.6 1.1 %shard_map.94 = (f32[2560,128]{1,0:T(8,128)S(1)}, f32[320,128]{1,0:T(8,128)S(1)}, f32[320,128]{1,0:T(8,128)S(1)}, bf16[2560,128]{1,0:T(8,128)(2,1)S(1)}) custom-call(f32[2560,128]{1,0:T(8,128)S(1)} %shard_map.93.refs_0_, f32[328,128]{1,0:T(8,128)S(1)} %collective-permute-done.refs_1_, f32[328,128]{1,0:T(8,128)S(1)} %collective-permute-done.1.refs_2_, ...), custom_call_target="tpu_custom_call" | custom-call | tf_op jit(solution)/shard_map/pallas_call | solution.py:388
  63.8 1.9 %collective-permute-start.3 = (f32[320,128]{1,0:T(8,128)S(1)}, f32[320,128]{1,0:T(8,128)S(1)}, u32[]{:S(2)}, u32[]{:S(2)}) collective-permute-start(f32[320,128]{1,0:T(8,128)S(1)} %get-tuple-element.21.refs_2_), channel_id=1, source_target_pairs={{0,1},{1,2},{2,3},{3,4},{4,5},{5,6},{6,7},{8,9},{9,10},{10,11},{11... | collective-permute-start | bytes 491528 | tf_op jit(solution)/shard_map/ppermute | solution.py:404
  65.7 2.4 %collective-permute-start.2 = (f32[320,128]{1,0:T(8,128)S(1)}, f32[320,128]{1,0:T(8,128)S(1)}, u32[]{:S(2)}, u32[]{:S(2)}) collective-permute-start(f32[320,128]{1,0:T(8,128)S(1)} %get-tuple-element.22.refs_3_), channel_id=1, source_target_pairs={{1,0},{2,1},{3,2},{4,3},{5,4},{6,5},{7,6},{9,8},{10,9},{11,10},{12... | collective-permute-start | bytes 491528 | tf_op jit(solution)/shard_map/ppermute | solution.py:405
  68.1 1.7 %shard_map.95.refs_0_ = f32[2560,128]{1,0:T(8,128)S(1)} custom-call(f32[2560,128]{1,0:T(8,128)S(1)} %get-tuple-element.16.refs_0_, f32[2560,128]{1,0:T(8,128)S(1)} %get-tuple-element.20.refs_1_, f32[320,128]{1,0:T(8,128)S(1)} %get-tuple-element.21.refs_2_, f32[320,128]{1,0:T(8,128)S(1)} %get-tuple-element.22.refs_3_, f32[3,128]{1,0:T(4,128)S(1)} %copy-done.2, ...), custom_call_target="tpu_custom_call" | custom-call | tf_op jit(solution)/shard_map/pallas_call | solution.py:388
  69.9 0.0 collective-permute-done.3.refs_2_
  69.9 2.5 %collective-permute-done.2.refs_1_ = f32[320,128]{1,0:T(8,128)S(1)} collective-permute-done((f32[320,128]{1,0:T(8,128)S(1)}, f32[320,128]{1,0:T(8,128)S(1)}, u32[]{:S(2)}, u32[]{:S(2)}) %collective-permute-start.2) | collective-permute-done | bytes 163872 | tf_op jit(solution)/shard_map/ppermute | solution.py:405
  72.3 0.9 %shard_map.96 = (f32[2560,128]{1,0:T(8,128)S(1)}, f32[320,128]{1,0:T(8,128)S(1)}, f32[320,128]{1,0:T(8,128)S(1)}) custom-call(f32[2560,128]{1,0:T(8,128)S(1)} %shard_map.95.refs_0_, f32[320,128]{1,0:T(8,128)S(1)} %collective-permute-done.2.refs_1_, f32[320,128]{1,0:T(8,128)S(1)} %collective-permute-done.3.refs_2_, f32[3,128]{1,0:T(4,128)S(1)} %copy-done.2, ...), custom_call_target="tpu_custom_call" | custom-call | tf_op jit(solution)/shard_map/pallas_call | solution.py:388
  73.2 1.9 %collective-permute-start.5 = (f32[320,128]{1,0:T(8,128)S(1)}, f32[320,128]{1,0:T(8,128)S(1)}, u32[]{:S(2)}, u32[]{:S(2)}) collective-permute-start(f32[320,128]{1,0:T(8,128)S(1)} %get-tuple-element.25.refs_2_), channel_id=1, source_target_pairs={{0,1},{1,2},{2,3},{3,4},{4,5},{5,6},{6,7},{8,9},{9,10},{10,11},{11... | collective-permute-start | bytes 491528 | tf_op jit(solution)/shard_map/ppermute | solution.py:404
  75.1 2.4 %collective-permute-start.4 = (f32[320,128]{1,0:T(8,128)S(1)}, f32[320,128]{1,0:T(8,128)S(1)}, u32[]{:S(2)}, u32[]{:S(2)}) collective-permute-start(f32[320,128]{1,0:T(8,128)S(1)} %get-tuple-element.26.refs_3_), channel_id=1, source_target_pairs={{1,0},{2,1},{3,2},{4,3},{5,4},{6,5},{7,6},{9,8},{10,9},{11,10},{12... | collective-permute-start | bytes 491528 | tf_op jit(solution)/shard_map/ppermute | solution.py:405
  77.6 1.7 %shard_map.97.refs_0_ = f32[2560,128]{1,0:T(8,128)S(1)} custom-call(f32[2560,128]{1,0:T(8,128)S(1)} %get-tuple-element.16.refs_0_, f32[2560,128]{1,0:T(8,128)S(1)} %get-tuple-element.24.refs_1_, f32[320,128]{1,0:T(8,128)S(1)} %get-tuple-element.25.refs_2_, f32[320,128]{1,0:T(8,128)S(1)} %get-tuple-element.26.refs_3_, f32[3,128]{1,0:T(4,128)S(1)} %copy-done.2, ...), custom_call_target="tpu_custom_call" | custom-call | tf_op jit(solution)/shard_map/pallas_call | solution.py:388
  79.3 0.0 collective-permute-done.5.refs_2_
  79.3 2.5 %collective-permute-done.4.refs_1_ = f32[320,128]{1,0:T(8,128)S(1)} collective-permute-done((f32[320,128]{1,0:T(8,128)S(1)}, f32[320,128]{1,0:T(8,128)S(1)}, u32[]{:S(2)}, u32[]{:S(2)}) %collective-permute-start.4) | collective-permute-done | bytes 163872 | tf_op jit(solution)/shard_map/ppermute | solution.py:405
  81.8 1.9 %shard_map.98 = f32[2560,128]{1,0:T(8,128)} custom-call(f32[2560,128]{1,0:T(8,128)S(1)} %shard_map.97.refs_0_, f32[320,128]{1,0:T(8,128)S(1)} %collective-permute-done.4.refs_1_, f32[320,128]{1,0:T(8,128)S(1)} %collective-permute-done.5.refs_2_, f32[3,128]{1,0:T(4,128)S(1)} %copy-done.2, f32[8,128]{1,0:T(8,128)S(1)} %get-tuple-element.19.refs_4_, ...), custom_call_target="tpu_custom_call" | custom-call | tf_op jit(solution)/shard_map/pallas_call | solution.py:388
Async XLA Ops:
  0.0 1.3 %copy-start.1 = (f32[5,512,128]{2,1,0:T(8,128)S(1)}, f32[5,512,128]{2,1,0:T(8,128)}, u32[]{:S(2)}) copy-start(f32[5,512,128]{2,1,0:T(8,128)} %coef.1) | copy-start | bytes 3932164
  1.3 0.7 copy-start.6
  2.0 0.7 copy-start.7
  2.6 0.7 copy-start.8
  4.3 48.1 %copy-start.4 = (s32[2,144]{1,0:T(2,128)S(1)}, s32[2,144]{1,0:T(2,128)}, u32[]{:S(2)}) copy-start(s32[2,144]{1,0:T(2,128)} %refs_5_.4) | copy-start | bytes 3460
  4.3 48.1 %copy-start.5 = (s32[2,144]{1,0:T(2,128)S(1)}, s32[2,144]{1,0:T(2,128)}, u32[]{:S(2)}) copy-start(s32[2,144]{1,0:T(2,128)} %refs_6_.3) | copy-start | bytes 3460
  52.4 5.5 %copy-start = (bf16[320,256]{1,0:T(8,128)(2,1)S(1)}, bf16[320,256]{1,0:T(8,128)(2,1)}, u32[]{:S(2)}) copy-start(bf16[320,256]{1,0:T(8,128)(2,1)} %constant.2.clone.refs_5_.refs_6_) | copy-start | bytes 491524
  52.4 5.5 %copy-start.2 = (f32[3,128]{1,0:T(4,128)S(1)}, f32[3,128]{1,0:T(4,128)}, u32[]{:S(2)}) copy-start(f32[3,128]{1,0:T(4,128)} %refs_3_.7) | copy-start | bytes 4612
  52.4 5.5 %copy-start.3 = (s32[4,128]{1,0:T(4,128)S(1)}, s32[4,128]{1,0:T(4,128)}, u32[]{:S(2)}) copy-start(s32[4,128]{1,0:T(4,128)} %refs_5_.6) | copy-start | bytes 6148
  53.1 6.4 %collective-permute-start.1 = (f32[328,128]{1,0:T(8,128)S(1)}, f32[328,128]{1,0:T(8,128)S(1)}, u32[]{:S(2)}, u32[]{:S(2)}) collective-permute-start(f32[328,128]{1,0:T(8,128)S(1)} %get-tuple-element.17.refs_1_), channel_id=1, source_target_pairs={{0,1},{1,2},{2,3},{3,4},{4,5},{5,6},{6,7},{8,9},{9,10},{10,11},{11... | collective-permute-start | bytes 503816 | tf_op jit(solution)/shard_map/ppermute | solution.py:404
  56.0 6.7 %collective-permute-start = (f32[328,128]{1,0:T(8,128)S(1)}, f32[328,128]{1,0:T(8,128)S(1)}, u32[]{:S(2)}, u32[]{:S(2)}) collective-permute-start(f32[328,128]{1,0:T(8,128)S(1)} %get-tuple-element.18.refs_2_), channel_id=1, source_target_pairs={{1,0},{2,1},{3,2},{4,3},{5,4},{6,5},{7,6},{9,8},{10,9},{11,10},{12... | collective-permute-start | bytes 503816 | tf_op jit(solution)/shard_map/ppermute | solution.py:405
  63.8 6.1 %collective-permute-start.3 = (f32[320,128]{1,0:T(8,128)S(1)}, f32[320,128]{1,0:T(8,128)S(1)}, u32[]{:S(2)}, u32[]{:S(2)}) collective-permute-start(f32[320,128]{1,0:T(8,128)S(1)} %get-tuple-element.21.refs_2_), channel_id=1, source_target_pairs={{0,1},{1,2},{2,3},{3,4},{4,5},{5,6},{6,7},{8,9},{9,10},{10,11},{11... | collective-permute-start | bytes 491528 | tf_op jit(solution)/shard_map/ppermute | solution.py:404
  65.7 6.6 %collective-permute-start.2 = (f32[320,128]{1,0:T(8,128)S(1)}, f32[320,128]{1,0:T(8,128)S(1)}, u32[]{:S(2)}, u32[]{:S(2)}) collective-permute-start(f32[320,128]{1,0:T(8,128)S(1)} %get-tuple-element.22.refs_3_), channel_id=1, source_target_pairs={{1,0},{2,1},{3,2},{4,3},{5,4},{6,5},{7,6},{9,8},{10,9},{11,10},{12... | collective-permute-start | bytes 491528 | tf_op jit(solution)/shard_map/ppermute | solution.py:405
  73.2 6.1 %collective-permute-start.5 = (f32[320,128]{1,0:T(8,128)S(1)}, f32[320,128]{1,0:T(8,128)S(1)}, u32[]{:S(2)}, u32[]{:S(2)}) collective-permute-start(f32[320,128]{1,0:T(8,128)S(1)} %get-tuple-element.25.refs_2_), channel_id=1, source_target_pairs={{0,1},{1,2},{2,3},{3,4},{4,5},{5,6},{6,7},{8,9},{9,10},{10,11},{11... | collective-permute-start | bytes 491528 | tf_op jit(solution)/shard_map/ppermute | solution.py:404
  75.1 6.6 %collective-permute-start.4 = (f32[320,128]{1,0:T(8,128)S(1)}, f32[320,128]{1,0:T(8,128)S(1)}, u32[]{:S(2)}, u32[]{:S(2)}) collective-permute-start(f32[320,128]{1,0:T(8,128)S(1)} %get-tuple-element.26.refs_3_), channel_id=1, source_target_pairs={{1,0},{2,1},{3,2},{4,3},{5,4},{6,5},{7,6},{9,8},{10,9},{11,10},{12... | collective-permute-start | bytes 491528 | tf_op jit(solution)/shard_map/ppermute | solution.py:405
where the time goes:
time: 84.1 us; the launch traced here: 83.7 us
  blocking collectives  48.1 us (57%)
  starting transfers between devices  13.4 us (16%)
  Pallas kernels  10.7 us (13%)
  waiting for transfers between devices  8.04 us (10%)
  local copies, waits for them, and re-layouts  3.31 us (4%)
    all_to_all x1, blocking collectives, shards(): lax.all_to_all(packed, ('curve', 'sub'), split_axis=0, concat_axis=0, til...  48.1 us
    pallas_call x8, Pallas kernels, call(): pl.pallas_call(kernel, out_shape=outs, in_specs=[VMEM] * len(args), out_s...  10.7 us
    ppermute x3, waiting for transfers between devices, swap(): above = lax.ppermute(lower, 'sub', [(i + 1, i) for i in range(count - 1)])  8.03 us
    ppermute x3, starting transfers between devices, swap(): above = lax.ppermute(lower, 'sub', [(i + 1, i) for i in range(count - 1)])  6.74 us
    ppermute x3, starting transfers between devices, swap(): below = lax.ppermute(upper, 'sub', [(i, i + 1) for i in range(count - 1)])  6.69 us
    unnamed x18, local copies, waits for them, and re-layouts  3.31 us
  transfers between devices with their start and end apart: 6, of which 3 were waited for; matrix products, arithmetic and copies ran while one was open for 0% of the time, Pallas kernels for 6%

commit v1 on v0

--- a/solution.py
+++ b/solution.py
@@ -25,6 +25,7 @@
 BF16 = jnp.bfloat16
 
 VMEM = pl.BlockSpec(memory_space=pltpu.VMEM)
+HBM = pl.BlockSpec(memory_space=pltpu.HBM)
 PARAMS = pltpu.CompilerParams(vmem_limit_bytes=LIMIT)
 
 
@@ -88,13 +89,13 @@
     return jnp.where(flag, 1.0, 0.0)
 
 
-def pack_kernel(coef, old, new, dest, out):
+def pack_kernel(coef, index, out):
     row = iota((E, E), 0)
     col = iota((E, E), 1)
-    new_row = new[...]
-    kept = jnp.minimum(old[...], new_row)
-    target = lax.shift_right_logical(dest[...], 7)
-    slot = dest[...] & (E - 1)
+    old, new_row, dest = index[0:1, :], index[1:2, :], index[2:3, :]
+    kept = jnp.minimum(old, new_row)
+    target = lax.shift_right_logical(dest, 7)
+    slot = dest & (E - 1)
     target_f = jnp.broadcast_to(target.astype(F32), (E, E))
     same = target_f == target_f.T
     rank = jnp.sum(onehot(same & (row < col)), axis=0, keepdims=True)
@@ -289,7 +290,7 @@
     lax.fori_loop(0, N, y_pass, 0)
 
 
-def build_routes(pay, table):
+def build_routes(pay, table, inside):
     wide = iota((E, 2 * E), 0).astype(F32)
     pad = jnp.full((1, E - 16), -1.0, F32)
 
@@ -299,7 +300,7 @@
     far_elem = jnp.concatenate([pay[FACE : FACE + 1, :], pay[FACE + 2 : FACE + 3, :]], axis=1)
     far_half = jnp.concatenate([pay[FACE + 1 : FACE + 2, :], pay[FACE + 3 : FACE + 4, :]], axis=1)
     own_elem, own_half = own(0), own(1)
-    far_pick = onehot(wide == far_elem)
+    far_pick = jnp.where(wide == far_elem, inside, 0.0)
     own_pick = onehot(wide == own_elem).astype(BF16)
     far_whole, own_whole = onehot(far_half == 0.0), onehot(own_half == 0.0)
     far_1, far_2 = onehot(far_half == 1.0), onehot(far_half == 2.0)
@@ -318,15 +319,18 @@
     beta = BETA[stage]
     if stage == 0:
         (partial, above, below, metric, degree, table_up, table_low, out, upper, lower, routes, cat_up, cat_low) = refs
+        place = lax.axis_index("sub")
+        last = lax.axis_size("sub") - 1
+        inside = (jnp.where(place < last, 1.0, 0.0), jnp.where(place > 0, 1.0, 0.0))
         for side, (pay, table) in enumerate(((above, table_up), (below, table_low))):
-            for n, route in enumerate(build_routes(pay, table)):
+            for n, route in enumerate(build_routes(pay, table, inside[side])):
                 for part in range(2):
                     start = side * 10 * E + part * 5 * E + n * E
                     routes[start : start + E, :] = route
     elif stage == 1:
         (partial, above, below, metric, degree, routes, out, upper, lower, cat_up, cat_low) = refs
     else:
-        (partial, above, below, metric, degree, routes, out, cat_up, cat_low) = refs
+        (partial, above, below, metric, degree, routes, final, cat_up, cat_low, out, sems) = refs
 
     def mix(line, table, parity, transposed):
         result = []
@@ -366,6 +370,7 @@
         masks = [m * back for m in masks]
     full = jnp.broadcast_to(metric[1:2, :], (8, E))
     ky = [full * (-0.5 * beta * STEP * (2 * a + 1)) for a in range(N)]
+    sent = []
     for i in range(N):
         up = [far_up[64 * v + 8 * i : 64 * v + 8 * i + 8] for v in range(NV)]
         low = [far_low[64 * v + 8 * i : 64 * v + 8 * i + 8] for v in range(NV)]
@@ -379,17 +384,26 @@
                     value = value * (1.0 / math.sqrt((2 * i + 1) * (2 * j + 1)))
                 else:
                     sums[j % 2] = value if sums[j % 2] is None else sums[j % 2] + value
-                out[start : start + 8, :] = value
+                if stage == 2:
+                    out[v, 64 * i + 8 * j : 64 * i + 8 * j + 8, :] = value
+                else:
+                    out[start : start + 8, :] = value
             if stage < 2:
                 write_traces(sums[0], sums[1], upper, lower, v, i)
-
-
-def call(kernel, outs, scratch, args):
+        if stage == 2:
+            part = pl.ds(64 * i, 64)
+            sent.append(pltpu.make_async_copy(out.at[:, part, :], final.at[:, part, :], sems.at[i]))
+            sent[i].start()
+    for copy in sent:
+        copy.wait()
+
+
+def call(kernel, outs, scratch, args, result=VMEM):
     return pl.pallas_call(
         kernel,
         out_shape=outs,
         in_specs=[VMEM] * len(args),
-        out_specs=jax.tree.map(lambda _: VMEM, outs),
+        out_specs=jax.tree.map(lambda _: result, outs),
         scratch_shapes=scratch,
         compiler_params=PARAMS,
     )(*args)
@@ -401,8 +415,8 @@
 
 def swap(upper, lower):
     count = lax.axis_size("sub")
-    below = lax.ppermute(upper, "sub", [(i, i + 1) for i in range(count - 1)])
-    above = lax.ppermute(lower, "sub", [(i + 1, i) for i in range(count - 1)])
+    below = lax.ppermute(upper, "sub", [(i, (i + 1) % count) for i in range(count)])
+    above = lax.ppermute(lower, "sub", [((i + 1) % count, i) for i in range(count)])
     return above, below
 
 
@@ -412,7 +426,7 @@
         pack_kernel,
         f32(E * BLOCK, E),
         [],
-        (coefficients, old_degree.reshape(1, E), new_degree.reshape(1, E), destination.reshape(1, E)),
+        (coefficients, jnp.stack([old_degree, new_degree, destination])),
     )
     packed = packed.reshape(E, 1, BLOCK * E)
     got = lax.all_to_all(packed, ("curve", "sub"), split_axis=0, concat_axis=0, tiled=True)
@@ -449,8 +463,10 @@
                 body, (f32(ROWS, E),) + faces, cats, (partial, above, below, metric, degree, routes)
             )
         else:
-            state = call(body, f32(ROWS, E), cats, (partial, above, below, metric, degree, routes))
-    return state.reshape(NV, MODES, E)
+            cats = cats + [pltpu.VMEM((NV, MODES, E), F32), pltpu.SemaphoreType.DMA((N,))]
+            args = (partial, above, below, metric, degree, routes)
+            state = call(body, f32(NV, MODES, E), cats, args, result=HBM)
+    return state
 
 
 def solution(mesh):

time: 84.1 us -> 73.9 us (0.88)
  the two profiles are of different devices: /device:TPU:1 before, /device:TPU:0 now
where the time goes in v1:
time: 73.9 us; the launch traced here: 73.3 us
  blocking collectives  47.7 us (65%)
  Pallas kernels  10.6 us (14%)
  starting transfers between devices  8.93 us (12%)
  waiting for transfers between devices  3.9 us (5%)
  local copies, waits for them, and re-layouts  1.34 us (2%)
    all_to_all x1, blocking collectives, shards(): lax.all_to_all(packed, ('curve', 'sub'), split_axis=0, concat_axis=0, til...  47.7 us
    pallas_call x8, Pallas kernels, call(): pl.pallas_call(kernel, out_shape=outs, in_specs=[VMEM] * len(args), out_s...  10.6 us
    ppermute x3, starting transfers between devices, swap(): lax.ppermute(lower, 'sub', [((i + 1) % count, i) for i in range(count)])  8.88 us
    ppermute x3, waiting for transfers between devices, swap(): lax.ppermute(upper, 'sub', [(i, (i + 1) % count) for i in range(count)])  3.89 us
  transfers between devices with their start and end apart: 6, of which 3 were waited for; matrix products, arithmetic and copies ran while one was open for 0% of the time, Pallas kernels for 7%

profile of v1, /device:TPU:0, one launch (start us, length us, event | category | flops | bytes accessed | tf_op | source)
XLA Modules:
  0.0 73.3 jit_solution(15116494893804717184)
XLA Ops:
  0.0 0.7 pad_add_fusion.index
  0.7 0.0 copy-start.1
  0.7 1.3 %copy-done.1 = f32[5,512,128]{2,1,0:T(8,128)S(1)} copy-done((f32[5,512,128]{2,1,0:T(8,128)S(1)}, f32[5,512,128]{2,1,0:T(8,128)}, u32[]{:S(2)}) %copy-start.1) | copy-done | bytes 1310744
  2.0 1.0 %shard_map.91 = f32[5248,128]{1,0:T(8,128)S(1)} custom-call(f32[5,512,128]{2,1,0:T(8,128)S(1)} %copy-done.1, s32[3,128]{1,0:T(4,128)S(1)} %pad_add_fusion.index), custom_call_target="tpu_custom_call" | custom-call | tf_op jit(solution)/shard_map/pallas_call | solution.py:402
  3.0 0.0 copy-start.4
  3.0 0.0 copy-start.5
  3.0 47.7 %all_to_all.5 = f32[128,1,5248]{2,1,0:T(1,128)S(1)} all-to-all(f32[128,1,5248]{2,1,0:T(1,128)S(1)} %bitcast.6), channel_id=1, replica_groups=mesh['curve'=16,'sub'=8] {'curve','sub'}, dimensions={0} | all-to-all | bytes 5373952 | tf_op jit(solution)/shard_map/all_to_all | solution.py:432
  50.7 0.0 copy-done.4
  50.7 0.0 copy-done.5
  50.8 0.0 copy-start
  50.8 0.0 copy-start.2
  50.8 0.0 copy-start.3
  50.8 0.7 shard_map.92
  51.5 0.0 collective-permute-start.1
  51.5 2.9 %collective-permute-start = (f32[328,128]{1,0:T(8,128)S(1)}, f32[328,128]{1,0:T(8,128)S(1)}, u32[]{:S(2)}, u32[]{:S(2)}) collective-permute-start(f32[328,128]{1,0:T(8,128)S(1)} %get-tuple-element.18.refs_2_), channel_id=1, source_target_pairs={{1,0},{2,1},{3,2},{4,3},{5,4},{6,5},{7,6},{0,7},{9,8},{10,9},{11,1... | collective-permute-start | bytes 503816 | tf_op jit(solution)/shard_map/ppermute | solution.py:419
  54.4 0.0 copy-done
  54.4 0.0 copy-done.2
  54.4 0.0 copy-done.3
  54.4 1.6 %shard_map.93.refs_0_ = f32[2560,128]{1,0:T(8,128)S(1)} custom-call(f32[2560,128]{1,0:T(8,128)S(1)} %get-tuple-element.16.refs_0_, f32[328,128]{1,0:T(8,128)S(1)} %get-tuple-element.17.refs_1_, f32[328,128]{1,0:T(8,128)S(1)} %get-tuple-element.18.refs_2_, f32[3,128]{1,0:T(4,128)S(1)} %copy-done.2, s32[4,128]{1,0:T(4,128)S(1)} %copy-done.3, ...), custom_call_target="tpu_custom_call" | custom-call | tf_op jit(solution)/shard_map/pallas_call | solution.py:402
  56.0 1.4 %collective-permute-done.1.refs_2_ = f32[328,128]{1,0:T(8,128)S(1)} collective-permute-done((f32[328,128]{1,0:T(8,128)S(1)}, f32[328,128]{1,0:T(8,128)S(1)}, u32[]{:S(2)}, u32[]{:S(2)}) %collective-permute-start.1) | collective-permute-done | bytes 167968 | tf_op jit(solution)/shard_map/ppermute | solution.py:418
  57.5 0.0 collective-permute-done.refs_1_
  57.5 1.1 %shard_map.94 = (f32[2560,128]{1,0:T(8,128)S(1)}, f32[320,128]{1,0:T(8,128)S(1)}, f32[320,128]{1,0:T(8,128)S(1)}, bf16[2560,128]{1,0:T(8,128)(2,1)S(1)}) custom-call(f32[2560,128]{1,0:T(8,128)S(1)} %shard_map.93.refs_0_, f32[328,128]{1,0:T(8,128)S(1)} %collective-permute-done.refs_1_, f32[328,128]{1,0:T(8,128)S(1)} %collective-permute-done.1.refs_2_, ...), custom_call_target="tpu_custom_call" | custom-call | tf_op jit(solution)/shard_map/pallas_call | solution.py:402
  58.6 0.0 collective-permute-start.3
  58.6 3.0 %collective-permute-start.2 = (f32[320,128]{1,0:T(8,128)S(1)}, f32[320,128]{1,0:T(8,128)S(1)}, u32[]{:S(2)}, u32[]{:S(2)}) collective-permute-start(f32[320,128]{1,0:T(8,128)S(1)} %get-tuple-element.22.refs_3_), channel_id=1, source_target_pairs={{1,0},{2,1},{3,2},{4,3},{5,4},{6,5},{7,6},{0,7},{9,8},{10,9},{11,1... | collective-permute-start | bytes 491528 | tf_op jit(solution)/shard_map/ppermute | solution.py:419
  61.6 1.7 %shard_map.95.refs_0_ = f32[2560,128]{1,0:T(8,128)S(1)} custom-call(f32[2560,128]{1,0:T(8,128)S(1)} %get-tuple-element.16.refs_0_, f32[2560,128]{1,0:T(8,128)S(1)} %get-tuple-element.20.refs_1_, f32[320,128]{1,0:T(8,128)S(1)} %get-tuple-element.21.refs_2_, f32[320,128]{1,0:T(8,128)S(1)} %get-tuple-element.22.refs_3_, f32[3,128]{1,0:T(4,128)S(1)} %copy-done.2, ...), custom_call_target="tpu_custom_call" | custom-call | tf_op jit(solution)/shard_map/pallas_call | solution.py:402
  63.4 1.2 %collective-permute-done.3.refs_2_ = f32[320,128]{1,0:T(8,128)S(1)} collective-permute-done((f32[320,128]{1,0:T(8,128)S(1)}, f32[320,128]{1,0:T(8,128)S(1)}, u32[]{:S(2)}, u32[]{:S(2)}) %collective-permute-start.3) | collective-permute-done | bytes 163872 | tf_op jit(solution)/shard_map/ppermute | solution.py:418
  64.6 0.0 collective-permute-done.2.refs_1_
  64.6 0.9 %shard_map.96 = (f32[2560,128]{1,0:T(8,128)S(1)}, f32[320,128]{1,0:T(8,128)S(1)}, f32[320,128]{1,0:T(8,128)S(1)}) custom-call(f32[2560,128]{1,0:T(8,128)S(1)} %shard_map.95.refs_0_, f32[320,128]{1,0:T(8,128)S(1)} %collective-permute-done.2.refs_1_, f32[320,128]{1,0:T(8,128)S(1)} %collective-permute-done.3.refs_2_, f32[3,128]{1,0:T(4,128)S(1)} %copy-done.2, ...), custom_call_target="tpu_custom_call" | custom-call | tf_op jit(solution)/shard_map/pallas_call | solution.py:402
  65.5 0.0 collective-permute-start.5
  65.5 3.0 %collective-permute-start.4 = (f32[320,128]{1,0:T(8,128)S(1)}, f32[320,128]{1,0:T(8,128)S(1)}, u32[]{:S(2)}, u32[]{:S(2)}) collective-permute-start(f32[320,128]{1,0:T(8,128)S(1)} %get-tuple-element.26.refs_3_), channel_id=1, source_target_pairs={{1,0},{2,1},{3,2},{4,3},{5,4},{6,5},{7,6},{0,7},{9,8},{10,9},{11,1... | collective-permute-start | bytes 491528 | tf_op jit(solution)/shard_map/ppermute | solution.py:419
  68.5 1.7 %shard_map.97.refs_0_ = f32[2560,128]{1,0:T(8,128)S(1)} custom-call(f32[2560,128]{1,0:T(8,128)S(1)} %get-tuple-element.16.refs_0_, f32[2560,128]{1,0:T(8,128)S(1)} %get-tuple-element.24.refs_1_, f32[320,128]{1,0:T(8,128)S(1)} %get-tuple-element.25.refs_2_, f32[320,128]{1,0:T(8,128)S(1)} %get-tuple-element.26.refs_3_, f32[3,128]{1,0:T(4,128)S(1)} %copy-done.2, ...), custom_call_target="tpu_custom_call" | custom-call | tf_op jit(solution)/shard_map/pallas_call | solution.py:402
  70.2 1.2 %collective-permute-done.5.refs_2_ = f32[320,128]{1,0:T(8,128)S(1)} collective-permute-done((f32[320,128]{1,0:T(8,128)S(1)}, f32[320,128]{1,0:T(8,128)S(1)}, u32[]{:S(2)}, u32[]{:S(2)}) %collective-permute-start.5) | collective-permute-done | bytes 163872 | tf_op jit(solution)/shard_map/ppermute | solution.py:418
  71.4 0.0 collective-permute-done.4.refs_1_
  71.4 1.9 %shard_map.98 = f32[5,512,128]{2,1,0:T(8,128)} custom-call(f32[2560,128]{1,0:T(8,128)S(1)} %shard_map.97.refs_0_, f32[320,128]{1,0:T(8,128)S(1)} %collective-permute-done.4.refs_1_, f32[320,128]{1,0:T(8,128)S(1)} %collective-permute-done.5.refs_2_, f32[3,128]{1,0:T(4,128)S(1)} %copy-done.2, f32[8,128]{1,0:T(8,128)S(1)} %get-tuple-element.19.refs_4_, ...), custom_call_target="tpu_custom_call" | custom-call | tf_op jit(solution)/shard_map/pallas_call | solution.py:402
Async XLA Ops:
  0.7 1.3 %copy-start.1 = (f32[5,512,128]{2,1,0:T(8,128)S(1)}, f32[5,512,128]{2,1,0:T(8,128)}, u32[]{:S(2)}) copy-start(f32[5,512,128]{2,1,0:T(8,128)} %coef.1) | copy-start | bytes 3932164
  3.0 47.8 %copy-start.4 = (s32[2,144]{1,0:T(2,128)S(1)}, s32[2,144]{1,0:T(2,128)}, u32[]{:S(2)}) copy-start(s32[2,144]{1,0:T(2,128)} %refs_5_.4) | copy-start | bytes 3460
  3.0 47.7 %copy-start.5 = (s32[2,144]{1,0:T(2,128)S(1)}, s32[2,144]{1,0:T(2,128)}, u32[]{:S(2)}) copy-start(s32[2,144]{1,0:T(2,128)} %refs_6_.3) | copy-start | bytes 3460
  50.8 3.7 %copy-start = (bf16[320,256]{1,0:T(8,128)(2,1)S(1)}, bf16[320,256]{1,0:T(8,128)(2,1)}, u32[]{:S(2)}) copy-start(bf16[320,256]{1,0:T(8,128)(2,1)} %constant.2.clone.refs_5_.refs_6_) | copy-start | bytes 491524
  50.8 3.7 %copy-start.2 = (f32[3,128]{1,0:T(4,128)S(1)}, f32[3,128]{1,0:T(4,128)}, u32[]{:S(2)}) copy-start(f32[3,128]{1,0:T(4,128)} %refs_3_.7) | copy-start | bytes 4612
  50.8 3.7 %copy-start.3 = (s32[4,128]{1,0:T(4,128)S(1)}, s32[4,128]{1,0:T(4,128)}, u32[]{:S(2)}) copy-start(s32[4,128]{1,0:T(4,128)} %refs_5_.6) | copy-start | bytes 6148
  51.5 6.0 %collective-permute-start.1 = (f32[328,128]{1,0:T(8,128)S(1)}, f32[328,128]{1,0:T(8,128)S(1)}, u32[]{:S(2)}, u32[]{:S(2)}) collective-permute-start(f32[328,128]{1,0:T(8,128)S(1)} %get-tuple-element.17.refs_1_), channel_id=1, source_target_pairs={{0,1},{1,2},{2,3},{3,4},{4,5},{5,6},{6,7},{7,0},{8,9},{9,10},{10,1... | collective-permute-start | bytes 503816 | tf_op jit(solution)/shard_map/ppermute | solution.py:418
  51.5 6.0 %collective-permute-start = (f32[328,128]{1,0:T(8,128)S(1)}, f32[328,128]{1,0:T(8,128)S(1)}, u32[]{:S(2)}, u32[]{:S(2)}) collective-permute-start(f32[328,128]{1,0:T(8,128)S(1)} %get-tuple-element.18.refs_2_), channel_id=1, source_target_pairs={{1,0},{2,1},{3,2},{4,3},{5,4},{6,5},{7,6},{0,7},{9,8},{10,9},{11,1... | collective-permute-start | bytes 503816 | tf_op jit(solution)/shard_map/ppermute | solution.py:419
  58.6 6.0 %collective-permute-start.3 = (f32[320,128]{1,0:T(8,128)S(1)}, f32[320,128]{1,0:T(8,128)S(1)}, u32[]{:S(2)}, u32[]{:S(2)}) collective-permute-start(f32[320,128]{1,0:T(8,128)S(1)} %get-tuple-element.21.refs_2_), channel_id=1, source_target_pairs={{0,1},{1,2},{2,3},{3,4},{4,5},{5,6},{6,7},{7,0},{8,9},{9,10},{10,1... | collective-permute-start | bytes 491528 | tf_op jit(solution)/shard_map/ppermute | solution.py:418
  58.6 5.9 %collective-permute-start.2 = (f32[320,128]{1,0:T(8,128)S(1)}, f32[320,128]{1,0:T(8,128)S(1)}, u32[]{:S(2)}, u32[]{:S(2)}) collective-permute-start(f32[320,128]{1,0:T(8,128)S(1)} %get-tuple-element.22.refs_3_), channel_id=1, source_target_pairs={{1,0},{2,1},{3,2},{4,3},{5,4},{6,5},{7,6},{0,7},{9,8},{10,9},{11,1... | collective-permute-start | bytes 491528 | tf_op jit(solution)/shard_map/ppermute | solution.py:419
  65.5 6.0 %collective-permute-start.5 = (f32[320,128]{1,0:T(8,128)S(1)}, f32[320,128]{1,0:T(8,128)S(1)}, u32[]{:S(2)}, u32[]{:S(2)}) collective-permute-start(f32[320,128]{1,0:T(8,128)S(1)} %get-tuple-element.25.refs_2_), channel_id=1, source_target_pairs={{0,1},{1,2},{2,3},{3,4},{4,5},{5,6},{6,7},{7,0},{8,9},{9,10},{10,1... | collective-permute-start | bytes 491528 | tf_op jit(solution)/shard_map/ppermute | solution.py:418
  65.5 6.0 %collective-permute-start.4 = (f32[320,128]{1,0:T(8,128)S(1)}, f32[320,128]{1,0:T(8,128)S(1)}, u32[]{:S(2)}, u32[]{:S(2)}) collective-permute-start(f32[320,128]{1,0:T(8,128)S(1)} %get-tuple-element.26.refs_3_), channel_id=1, source_target_pairs={{1,0},{2,1},{3,2},{4,3},{5,4},{6,5},{7,6},{0,7},{9,8},{10,9},{11,1... | collective-permute-start | bytes 491528 | tf_op jit(solution)/shard_map/ppermute | solution.py:419

commit v2 on v1

--- a/solution.py
+++ b/solution.py
@@ -175,11 +175,39 @@
     return [p - m for p, m in zip(plus, minus)], [p + m for p, m in zip(plus, minus)]
 
 
-def volume_kernel(alpha, beta, *refs):
-    if alpha:
+def degree_masks(degree):
+    k_row = iota((8, E), 0)
+    return [onehot(jnp.maximum(k_row, n).astype(F32) <= degree[...]) for n in range(N)]
+
+
+def lift_weights(metric, stage):
+    full = jnp.broadcast_to(metric[1:2, :], (8, E))
+    return [full * (-0.5 * BETA[stage] * STEP * (2 * a + 1)) for a in range(N)]
+
+
+def volume_kernel(stage, *refs):
+    alpha, beta = ALPHA[stage], BETA[stage]
+    if stage:
+        first, before, lifts, *refs, state = refs
+    else:
         first, *refs = refs
-    (state, upper, lower, metric, near, ztab, out, xsum, zsum, xp, xm, zp, zm, xl, zl, cat) = refs
+        state = first
+    if stage < 2:
+        sums_out = refs.pop(7)
+    (degree, upper, lower, metric, near, ztab, out, xsum, zsum, xp, xm, zp, zm, xl, zl, cat, live) = refs
     row = iota((E, E), 0)
+    masks = degree_masks(degree)
+    for n in range(N):
+        live[8 * n : 8 * n + 8, :] = masks[n]
+    if stage:
+        kq = lift_weights(metric, stage - 1)
+        for v in range(NV):
+            for i in range(N):
+                face = 64 * v + 8 * i
+                lift = (lifts[face : face + 8, :], lifts[FACE + face : FACE + face + 8, :])
+                for j in range(N):
+                    start = v * MODES + 64 * i + 8 * j
+                    state[start : start + 8, :] = masks[max(i, j)] * (before[start : start + 8, :] + kq[j] * lift[j % 2])
     gather = []
     for d in range(4):
         pick = onehot(row == near[d : d + 1, :]).astype(BF16)
@@ -259,6 +287,7 @@
         s = [[10.0 * x for x in even], [10.0 * x for x in odd]]
         z_even = [at(zl, 64 * v + 8 * i) for v in range(NV)]
         z_odd = [at(zl, FACE + 64 * v + 8 * i) for v in range(NV)]
+        sums = [[None] * NV, [None] * NV]
         for j in range(N - 1, -1, -1):
             inner = 64 * i + 8 * j
             rows = [v * MODES + inner for v in range(NV)]
@@ -266,6 +295,7 @@
             sw, sp = at(zsum, inner), at(zsum, MODES + inner)
             zs = (sw, None, None, sp, sw)
             now = s[j % 2]
+            mask = at(live, 8 * jnp.maximum(i, j))
             for v in range(NV):
                 lift = jnp.where(
                     odd_k,
@@ -279,12 +309,19 @@
                     total = total + (alpha * at(first, rows[v]) + beta * c[v])
                 else:
                     total = total + c[v]
+                total = mask * total
                 out[pl.ds(pl.multiple_of(rows[v], 8), 8), :] = total
+                held = sums[j % 2]
+                held[v] = total if held[v] is None else held[v] + total
             if j:
                 r, u, y, w, p = c
                 y20 = 20.0 * y
                 f = [r + y20, u, y + 20.0 * p, w, p + y20]
                 s[(j + 1) % 2] = [a + b for a, b in zip(s[(j + 1) % 2], f)]
+        for parity in range(2):
+            for v in range(NV if stage < 2 else 0):
+                start = FACE * parity + 64 * v + 8 * i
+                sums_out[pl.ds(pl.multiple_of(start, 8), 8), :] = sums[parity][v]
         return carry
 
     lax.fori_loop(0, N, y_pass, 0)
@@ -315,85 +352,85 @@
     return [dot_nt((far_pick * w).astype(BF16), own_pick).astype(BF16) for w in weights]
 
 
-def post_kernel(stage, *refs):
-    beta = BETA[stage]
+def far_side(face, cat, routes):
+    for v in range(NV):
+        high, low = split(face[64 * v : 64 * v + 64, :])
+        cat[64 * v : 64 * v + 64, 0:E] = high
+        cat[64 * v : 64 * v + 64, E : 2 * E] = low
+    picked = dot(cat[...], routes)
+    result = []
+    for v in range(NV):
+        lines = [
+            [picked[64 * v + 8 * a : 64 * v + 8 * a + 8, E * n : E * n + E] for a in range(N)] for n in range(5)
+        ]
+        totals = []
+        for a in range(N):
+            total = lines[0][a]
+            for b in range(a, N):
+                total = total + RESTRICT[a][b] * lines[1 + (a + b) % 2][b]
+            for b in range(a + 1):
+                total = total + PROJECT[a][b] * lines[3 + (a + b) % 2][b]
+            totals.append(total)
+        result.append(totals)
+    return result
+
+
+def far_lifts(above, below, cat_up, cat_low, routes):
+    up = far_side(above, cat_up, routes[0 : 2 * E, :])
+    low = far_side(below, cat_low, routes[2 * E : 4 * E, :])
+    result = []
+    for i in range(N):
+        plus = couple([up[v][i] for v in range(NV)], 2, -1.0)
+        minus = couple([low[v][i] for v in range(NV)], 2, 1.1)
+        result.append(halves_of(plus, minus))
+    return result
+
+
+def trace_kernel(stage, *refs):
     if stage == 0:
-        (partial, above, below, metric, degree, table_up, table_low, out, upper, lower, routes, cat_up, cat_low) = refs
+        (sums, above, below, metric, degree, table_up, table_low, upper, lower, lifts, routes, cat_up, cat_low) = refs
         place = lax.axis_index("sub")
         last = lax.axis_size("sub") - 1
         inside = (jnp.where(place < last, 1.0, 0.0), jnp.where(place > 0, 1.0, 0.0))
         for side, (pay, table) in enumerate(((above, table_up), (below, table_low))):
             for n, route in enumerate(build_routes(pay, table, inside[side])):
                 for part in range(2):
-                    start = side * 10 * E + part * 5 * E + n * E
-                    routes[start : start + E, :] = route
-    elif stage == 1:
-        (partial, above, below, metric, degree, routes, out, upper, lower, cat_up, cat_low) = refs
+                    start = (side * 2 + part) * E
+                    routes[start : start + E, E * n : E * n + E] = route
     else:
-        (partial, above, below, metric, degree, routes, final, cat_up, cat_low, out, sems) = refs
-
-    def mix(line, table, parity, transposed):
-        result = []
-        for a in range(N):
-            total = None
-            for b in range(N):
-                if (a + b) % 2 != parity or (b > a if transposed else b < a):
-                    continue
-                term = table[a][b] * line[b]
-                total = term if total is None else total + term
-            result.append(jnp.zeros_like(line[0]) if total is None else total)
-        return jnp.concatenate(result, axis=0)
-
-    far = []
-    for side, (face, cat) in enumerate(((above, cat_up), (below, cat_low))):
+        (sums, above, below, metric, degree, routes, upper, lower, lifts, cat_up, cat_low) = refs
+    masks = degree_masks(degree)
+    kq = lift_weights(metric, stage)
+    far = far_lifts(above, below, cat_up, cat_low, routes)
+    for i in range(N):
+        weight = [sum(masks[max(i, j)] * kq[j] for j in range(p, N, 2)) for p in range(2)]
         for v in range(NV):
-            whole = face[64 * v : 64 * v + 64, :]
-            line = [whole[8 * i : 8 * i + 8] for i in range(N)]
-            kinds = (
-                whole,
-                mix(line, RESTRICT, 0, False),
-                mix(line, RESTRICT, 1, False),
-                mix(line, PROJECT, 0, True),
-                mix(line, PROJECT, 1, True),
-            )
-            for n, kind in enumerate(kinds):
-                high, low = split(kind)
-                cat[64 * v : 64 * v + 64, n * E : n * E + E] = high
-                cat[64 * v : 64 * v + 64, (n + 5) * E : (n + 5) * E + E] = low
-        far.append(dot(cat[...], routes[side * 10 * E : (side + 1) * 10 * E, :]))
-    far_up, far_low = far
-    k_row = iota((8, E), 0)
-    deg = degree[...]
-    masks = [onehot(jnp.maximum(k_row, n).astype(F32) <= deg) for n in range(N)]
-    if stage == 2:
-        back = 1.0 / jnp.sqrt((2 * k_row + 1).astype(F32))
-        masks = [m * back for m in masks]
-    full = jnp.broadcast_to(metric[1:2, :], (8, E))
-    ky = [full * (-0.5 * beta * STEP * (2 * a + 1)) for a in range(N)]
+            rows = slice(64 * v + 8 * i, 64 * v + 8 * i + 8)
+            odd_rows = slice(FACE + 64 * v + 8 * i, FACE + 64 * v + 8 * i + 8)
+            lifts[rows, :] = far[i][0][v]
+            lifts[odd_rows, :] = far[i][1][v]
+            even = sums[rows, :] + weight[0] * far[i][0][v]
+            odd = sums[odd_rows, :] + weight[1] * far[i][1][v]
+            write_traces(even, odd, upper, lower, v, i)
+
+
+def final_kernel(partial, above, below, metric, degree, routes, final, cat_up, cat_low, out, sems):
+    back = 1.0 / jnp.sqrt((2 * iota((8, E), 0) + 1).astype(F32))
+    masks = [m * back for m in degree_masks(degree)]
+    kq = lift_weights(metric, 2)
+    far = far_lifts(above, below, cat_up, cat_low, routes)
     sent = []
     for i in range(N):
-        up = [far_up[64 * v + 8 * i : 64 * v + 8 * i + 8] for v in range(NV)]
-        low = [far_low[64 * v + 8 * i : 64 * v + 8 * i + 8] for v in range(NV)]
-        lift = halves_of(couple(up, 2, -1.0), couple(low, 2, 1.1))
         for v in range(NV):
-            sums = [None, None]
             for j in range(N):
-                start = v * MODES + 64 * i + 8 * j
-                value = masks[max(i, j)] * (partial[start : start + 8, :] + ky[j] * lift[j % 2][v])
-                if stage == 2:
-                    value = value * (1.0 / math.sqrt((2 * i + 1) * (2 * j + 1)))
-                else:
-                    sums[j % 2] = value if sums[j % 2] is None else sums[j % 2] + value
-                if stage == 2:
-                    out[v, 64 * i + 8 * j : 64 * i + 8 * j + 8, :] = value
-                else:
-                    out[start : start + 8, :] = value
-            if stage < 2:
-                write_traces(sums[0], sums[1], upper, lower, v, i)
-        if stage == 2:
+                start = 64 * i + 8 * j
+                value = partial[v * MODES + start : v * MODES + start + 8, :] + kq[j] * far[i][j % 2][v]
+                value = (masks[max(i, j)] * (1.0 / math.sqrt((2 * i + 1) * (2 * j + 1)))) * value
+                out[v, start : start + 8, :] = value
             part = pl.ds(64 * i, 64)
-            sent.append(pltpu.make_async_copy(out.at[:, part, :], final.at[:, part, :], sems.at[i]))
-            sent[i].start()
+            copy = pltpu.make_async_copy(out.at[v, part, :], final.at[v, part, :], sems.at[v * N + i])
+            copy.start()
+            sent.append(copy)
     for copy in sent:
         copy.wait()
 
@@ -434,39 +471,36 @@
     first, degree, upper, lower = call(
         unpack_kernel, (f32(ROWS, E), f32(8, E), f32(PAY, E), f32(PAY, E)), [], (got, mortar_up, mortar_low)
     )
-    state = first
-    routes = None
+    faces = (f32(FACE, E), f32(FACE, E))
+    cats = [pltpu.VMEM((FACE, 2 * E), BF16)] * 2
     for stage in range(3):
         above, below = swap(upper, lower)
-        given = (state, upper, lower, metric, near, ztab)
-        partial = call(
-            functools.partial(volume_kernel, ALPHA[stage], BETA[stage]),
-            f32(ROWS, E),
+        given = (first,) if stage == 0 else (first, partial, lifts)
+        partial, *sums = call(
+            functools.partial(volume_kernel, stage),
+            (f32(ROWS, E), f32(2 * FACE, E))[: 2 if stage < 2 else 1],
             [pltpu.VMEM((ROWS, E), F32), pltpu.VMEM((2 * MODES, E), F32)]
             + [pltpu.VMEM((FACE, E), F32)] * 4
             + [pltpu.VMEM((2 * FACE, E), F32)] * 2
-            + [pltpu.VMEM((FACE, 2 * E), BF16)],
-            (first,) + given if stage else given,
+            + [pltpu.VMEM((FACE, 2 * E), BF16), pltpu.VMEM((8 * N, E), F32)]
+            + ([pltpu.VMEM((ROWS, E), F32)] if stage else []),
+            given + (degree, upper, lower, metric, near, ztab),
         )
-        cats = [pltpu.VMEM((FACE, 10 * E), BF16)] * 2
-        body = functools.partial(post_kernel, stage)
-        faces = (f32(FACE, E), f32(FACE, E))
+        body = functools.partial(trace_kernel, stage)
+        outs = faces + (f32(2 * FACE, E),)
         if stage == 0:
-            state, upper, lower, routes = call(
+            upper, lower, lifts, routes = call(
                 body,
-                (f32(ROWS, E),) + faces + (jax.ShapeDtypeStruct((20 * E, E), BF16),),
+                outs + (jax.ShapeDtypeStruct((4 * E, 5 * E), BF16),),
                 cats,
-                (partial, above, below, metric, degree, mortar_up, mortar_low),
+                (*sums, above, below, metric, degree, mortar_up, mortar_low),
             )
         elif stage == 1:
-            state, upper, lower = call(
-                body, (f32(ROWS, E),) + faces, cats, (partial, above, below, metric, degree, routes)
-            )
+            upper, lower, lifts = call(body, outs, cats, (*sums, above, below, metric, degree, routes))
         else:
-            cats = cats + [pltpu.VMEM((NV, MODES, E), F32), pltpu.SemaphoreType.DMA((N,))]
+            scratch = cats + [pltpu.VMEM((NV, MODES, E), F32), pltpu.SemaphoreType.DMA((NV * N,))]
             args = (partial, above, below, metric, degree, routes)
-            state = call(body, f32(NV, MODES, E), cats, args, result=HBM)
-    return state
+            return call(final_kernel, f32(NV, MODES, E), scratch, args, result=HBM)
 
 
 def solution(mesh):

time: 73.9 us -> 73.3 us (level)
  transfers between devices with their start and end apart: 6 -> 6, of which waited for: 3 -> 3; matrix products, arithmetic and copies ran while one was open for 0% -> 0% of each run, Pallas kernels for 7% -> 8%
where the time goes in v2:
time: 73.3 us; the launch traced here: 72.7 us
  blocking collectives  47.7 us (65%)
  Pallas kernels  10.6 us (14%)
  starting transfers between devices  8.95 us (12%)
  waiting for transfers between devices  3.31 us (5%)
  local copies, waits for them, and re-layouts  1.34 us (2%)
    all_to_all x1, blocking collectives, shards(): lax.all_to_all(packed, ('curve', 'sub'), split_axis=0, concat_axis=0, til...  47.7 us
    pallas_call x8, Pallas kernels, call(): pl.pallas_call(kernel, out_shape=outs, in_specs=[VMEM] * len(args), out_s...  10.6 us
    ppermute x3, starting transfers between devices, swap(): lax.ppermute(lower, 'sub', [((i + 1) % count, i) for i in range(count)])  8.89 us
    ppermute x3, waiting for transfers between devices, swap(): lax.ppermute(upper, 'sub', [(i, (i + 1) % count) for i in range(count)])  3.3 us
  transfers between devices with their start and end apart: 6, of which 3 were waited for; matrix products, arithmetic and copies ran while one was open for 0% of the time, Pallas kernels for 8%

profile of v2, /device:TPU:0, one launch (start us, length us, event | category | flops | bytes accessed | tf_op | source)
XLA Modules:
  0.0 72.7 jit_solution(15715985925131891003)
XLA Ops:
  0.0 0.7 pad_add_fusion.index
  0.7 0.0 copy-start.1
  0.7 1.3 %copy-done.1 = f32[5,512,128]{2,1,0:T(8,128)S(1)} copy-done((f32[5,512,128]{2,1,0:T(8,128)S(1)}, f32[5,512,128]{2,1,0:T(8,128)}, u32[]{:S(2)}) %copy-start.1) | copy-done | bytes 1310744
  2.0 1.0 %shard_map.91 = f32[5248,128]{1,0:T(8,128)S(1)} custom-call(f32[5,512,128]{2,1,0:T(8,128)S(1)} %copy-done.1, s32[3,128]{1,0:T(4,128)S(1)} %pad_add_fusion.index), custom_call_target="tpu_custom_call" | custom-call | tf_op jit(solution)/shard_map/pallas_call | solution.py:439
  3.0 0.0 copy-start.4
  3.0 0.0 copy-start.5
  3.0 47.7 %all_to_all.5 = f32[128,1,5248]{2,1,0:T(1,128)S(1)} all-to-all(f32[128,1,5248]{2,1,0:T(1,128)S(1)} %bitcast.6), channel_id=1, replica_groups=mesh['curve'=16,'sub'=8] {'curve','sub'}, dimensions={0} | all-to-all | bytes 5373952 | tf_op jit(solution)/shard_map/all_to_all | solution.py:469
  50.7 0.0 copy-done.4
  50.7 0.0 copy-done.5
  50.8 0.0 copy-start
  50.8 0.0 copy-start.2
  50.8 0.0 copy-start.3
  50.8 0.7 shard_map.92
  51.5 0.0 collective-permute-start.1
  51.5 2.9 %collective-permute-start = (f32[328,128]{1,0:T(8,128)S(1)}, f32[328,128]{1,0:T(8,128)S(1)}, u32[]{:S(2)}, u32[]{:S(2)}) collective-permute-start(f32[328,128]{1,0:T(8,128)S(1)} %get-tuple-element.23.refs_3_), channel_id=1, source_target_pairs={{1,0},{2,1},{3,2},{4,3},{5,4},{6,5},{7,6},{0,7},{9,8},{10,9},{11,1... | collective-permute-start | bytes 503816 | tf_op jit(solution)/shard_map/ppermute | solution.py:456
  54.4 0.0 copy-done
  54.4 0.0 copy-done.2
  54.4 0.0 copy-done.3
  54.4 1.7 %shard_map.93 = (f32[2560,128]{1,0:T(8,128)S(1)}, f32[640,128]{1,0:T(8,128)S(1)}) custom-call(f32[2560,128]{1,0:T(8,128)S(1)} %get-tuple-element.20.refs_0_, f32[8,128]{1,0:T(8,128)S(1)} %get-tuple-element.21.refs_1_.refs_4_.refs_3_.degree, f32[328,128]{1,0:T(8,128)S(1)} %get-tuple-element.22.refs_2_, f32[328,128]{1,0:T(8,128)S(1)} %get-tuple-element.23.refs_3_, ...), custom_call_target="tpu_custom_call" | custom-call | tf_op jit(solution)/shard_map/pallas_call | solution.py:439
  56.1 1.4 %collective-permute-done.1.refs_2_ = f32[328,128]{1,0:T(8,128)S(1)} collective-permute-done((f32[328,128]{1,0:T(8,128)S(1)}, f32[328,128]{1,0:T(8,128)S(1)}, u32[]{:S(2)}, u32[]{:S(2)}) %collective-permute-start.1) | collective-permute-done | bytes 167968 | tf_op jit(solution)/shard_map/ppermute | solution.py:455
  57.5 0.0 collective-permute-done.refs_1_
  57.5 0.8 %shard_map.94 = (f32[320,128]{1,0:T(8,128)S(1)}, f32[320,128]{1,0:T(8,128)S(1)}, f32[640,128]{1,0:T(8,128)S(1)}, bf16[512,640]{1,0:T(8,128)(2,1)S(1)}) custom-call(f32[640,128]{1,0:T(8,128)S(1)} %get-tuple-element.25.refs_0_, f32[328,128]{1,0:T(8,128)S(1)} %collective-permute-done.refs_1_, f32[328,128]{1,0:T(8,128)S(1)} %collective-permute-done.1.refs_2_, ...), custom_call_target="tpu_custom_call" | custom-call | tf_op jit(solution)/shard_map/pallas_call | solution.py:439
  58.2 0.0 collective-permute-start.3
  58.3 3.0 %collective-permute-start.2 = (f32[320,128]{1,0:T(8,128)S(1)}, f32[320,128]{1,0:T(8,128)S(1)}, u32[]{:S(2)}, u32[]{:S(2)}) collective-permute-start(f32[320,128]{1,0:T(8,128)S(1)} %get-tuple-element.28.refs_5_), channel_id=1, source_target_pairs={{1,0},{2,1},{3,2},{4,3},{5,4},{6,5},{7,6},{0,7},{9,8},{10,9},{11,1... | collective-permute-start | bytes 491528 | tf_op jit(solution)/shard_map/ppermute | solution.py:456
  61.2 2.0 %shard_map.95 = (f32[2560,128]{1,0:T(8,128)S(1)}, f32[640,128]{1,0:T(8,128)S(1)}) custom-call(f32[2560,128]{1,0:T(8,128)S(1)} %get-tuple-element.20.refs_0_, f32[2560,128]{1,0:T(8,128)S(1)} %get-tuple-element.24.refs_1_, f32[640,128]{1,0:T(8,128)S(1)} %get-tuple-element.26.refs_2_, f32[8,128]{1,0:T(8,128)S(1)} %get-tuple-element.21.refs_1_.refs_4_.refs_3_.degree, ...), custom_call_target="tpu_custom_call" | custom-call | tf_op jit(solution)/shard_map/pallas_call | solution.py:439
  63.3 0.9 %collective-permute-done.3.refs_2_ = f32[320,128]{1,0:T(8,128)S(1)} collective-permute-done((f32[320,128]{1,0:T(8,128)S(1)}, f32[320,128]{1,0:T(8,128)S(1)}, u32[]{:S(2)}, u32[]{:S(2)}) %collective-permute-start.3) | collective-permute-done | bytes 163872 | tf_op jit(solution)/shard_map/ppermute | solution.py:455
  64.2 0.0 collective-permute-done.2.refs_1_
  64.2 0.5 shard_map.96
  64.7 0.0 collective-permute-start.5
  64.8 3.0 %collective-permute-start.4 = (f32[320,128]{1,0:T(8,128)S(1)}, f32[320,128]{1,0:T(8,128)S(1)}, u32[]{:S(2)}, u32[]{:S(2)}) collective-permute-start(f32[320,128]{1,0:T(8,128)S(1)} %get-tuple-element.34.refs_5_), channel_id=1, source_target_pairs={{1,0},{2,1},{3,2},{4,3},{5,4},{6,5},{7,6},{0,7},{9,8},{10,9},{11,1... | collective-permute-start | bytes 491528 | tf_op jit(solution)/shard_map/ppermute | solution.py:456
  67.8 2.0 %shard_map.97.partial = f32[2560,128]{1,0:T(8,128)S(1)} custom-call(f32[2560,128]{1,0:T(8,128)S(1)} %get-tuple-element.20.refs_0_, f32[2560,128]{1,0:T(8,128)S(1)} %get-tuple-element.29.refs_1_, f32[640,128]{1,0:T(8,128)S(1)} %get-tuple-element.32.refs_2_, f32[8,128]{1,0:T(8,128)S(1)} %get-tuple-element.21.refs_1_.refs_4_.refs_3_.degree, ...), custom_call_target="tpu_custom_call" | custom-call | tf_op jit(solution)/shard_map/pallas_call | solution.py:439
  69.7 1.0 %collective-permute-done.5.below = f32[320,128]{1,0:T(8,128)S(1)} collective-permute-done((f32[320,128]{1,0:T(8,128)S(1)}, f32[320,128]{1,0:T(8,128)S(1)}, u32[]{:S(2)}, u32[]{:S(2)}) %collective-permute-start.5) | collective-permute-done | bytes 163872 | tf_op jit(solution)/shard_map/ppermute | solution.py:455
  70.7 0.0 collective-permute-done.4.above
  70.7 2.0 %shard_map.98 = f32[5,512,128]{2,1,0:T(8,128)} custom-call(f32[2560,128]{1,0:T(8,128)S(1)} %shard_map.97.partial, f32[320,128]{1,0:T(8,128)S(1)} %collective-permute-done.4.above, f32[320,128]{1,0:T(8,128)S(1)} %collective-permute-done.5.below, f32[3,128]{1,0:T(4,128)S(1)} %copy-done.2, f32[8,128]{1,0:T(8,128)S(1)} %get-tuple-element.21.refs_1_.refs_4_.refs_3_.degree, ...), custom_call_target="tpu_custom_call" | custom-call | tf_op jit(solution)/shard_map/pallas_call | solution.py:439
Async XLA Ops:
  0.7 1.3 %copy-start.1 = (f32[5,512,128]{2,1,0:T(8,128)S(1)}, f32[5,512,128]{2,1,0:T(8,128)}, u32[]{:S(2)}) copy-start(f32[5,512,128]{2,1,0:T(8,128)} %coef.1) | copy-start | bytes 3932164
  3.0 47.8 %copy-start.4 = (s32[2,144]{1,0:T(2,128)S(1)}, s32[2,144]{1,0:T(2,128)}, u32[]{:S(2)}) copy-start(s32[2,144]{1,0:T(2,128)} %refs_5_.3) | copy-start | bytes 3460
  3.0 47.7 %copy-start.5 = (s32[2,144]{1,0:T(2,128)S(1)}, s32[2,144]{1,0:T(2,128)}, u32[]{:S(2)}) copy-start(s32[2,144]{1,0:T(2,128)} %refs_6_.4) | copy-start | bytes 3460
  50.8 3.7 %copy-start = (bf16[320,256]{1,0:T(8,128)(2,1)S(1)}, bf16[320,256]{1,0:T(8,128)(2,1)}, u32[]{:S(2)}) copy-start(bf16[320,256]{1,0:T(8,128)(2,1)} %constant.2.clone.refs_6_.refs_8_) | copy-start | bytes 491524
  50.8 3.7 %copy-start.2 = (f32[3,128]{1,0:T(4,128)S(1)}, f32[3,128]{1,0:T(4,128)}, u32[]{:S(2)}) copy-start(f32[3,128]{1,0:T(4,128)} %metric.1) | copy-start | bytes 4612
  50.8 3.7 %copy-start.3 = (s32[4,128]{1,0:T(4,128)S(1)}, s32[4,128]{1,0:T(4,128)}, u32[]{:S(2)}) copy-start(s32[4,128]{1,0:T(4,128)} %refs_7_.3) | copy-start | bytes 6148
  51.5 6.0 %collective-permute-start.1 = (f32[328,128]{1,0:T(8,128)S(1)}, f32[328,128]{1,0:T(8,128)S(1)}, u32[]{:S(2)}, u32[]{:S(2)}) collective-permute-start(f32[328,128]{1,0:T(8,128)S(1)} %get-tuple-element.22.refs_2_), channel_id=1, source_target_pairs={{0,1},{1,2},{2,3},{3,4},{4,5},{5,6},{6,7},{7,0},{8,9},{9,10},{10,1... | collective-permute-start | bytes 503816 | tf_op jit(solution)/shard_map/ppermute | solution.py:455
  51.5 6.0 %collective-permute-start = (f32[328,128]{1,0:T(8,128)S(1)}, f32[328,128]{1,0:T(8,128)S(1)}, u32[]{:S(2)}, u32[]{:S(2)}) collective-permute-start(f32[328,128]{1,0:T(8,128)S(1)} %get-tuple-element.23.refs_3_), channel_id=1, source_target_pairs={{1,0},{2,1},{3,2},{4,3},{5,4},{6,5},{7,6},{0,7},{9,8},{10,9},{11,1... | collective-permute-start | bytes 503816 | tf_op jit(solution)/shard_map/ppermute | solution.py:456
  58.2 6.0 %collective-permute-start.3 = (f32[320,128]{1,0:T(8,128)S(1)}, f32[320,128]{1,0:T(8,128)S(1)}, u32[]{:S(2)}, u32[]{:S(2)}) collective-permute-start(f32[320,128]{1,0:T(8,128)S(1)} %get-tuple-element.27.refs_4_), channel_id=1, source_target_pairs={{0,1},{1,2},{2,3},{3,4},{4,5},{5,6},{6,7},{7,0},{8,9},{9,10},{10,1... | collective-permute-start | bytes 491528 | tf_op jit(solution)/shard_map/ppermute | solution.py:455
  58.3 5.9 %collective-permute-start.2 = (f32[320,128]{1,0:T(8,128)S(1)}, f32[320,128]{1,0:T(8,128)S(1)}, u32[]{:S(2)}, u32[]{:S(2)}) collective-permute-start(f32[320,128]{1,0:T(8,128)S(1)} %get-tuple-element.28.refs_5_), channel_id=1, source_target_pairs={{1,0},{2,1},{3,2},{4,3},{5,4},{6,5},{7,6},{0,7},{9,8},{10,9},{11,1... | collective-permute-start | bytes 491528 | tf_op jit(solution)/shard_map/ppermute | solution.py:456
  64.7 6.0 %collective-permute-start.5 = (f32[320,128]{1,0:T(8,128)S(1)}, f32[320,128]{1,0:T(8,128)S(1)}, u32[]{:S(2)}, u32[]{:S(2)}) collective-permute-start(f32[320,128]{1,0:T(8,128)S(1)} %get-tuple-element.33.refs_4_), channel_id=1, source_target_pairs={{0,1},{1,2},{2,3},{3,4},{4,5},{5,6},{6,7},{7,0},{8,9},{9,10},{10,1... | collective-permute-start | bytes 491528 | tf_op jit(solution)/shard_map/ppermute | solution.py:455
  64.8 6.0 %collective-permute-start.4 = (f32[320,128]{1,0:T(8,128)S(1)}, f32[320,128]{1,0:T(8,128)S(1)}, u32[]{:S(2)}, u32[]{:S(2)}) collective-permute-start(f32[320,128]{1,0:T(8,128)S(1)} %get-tuple-element.34.refs_5_), channel_id=1, source_target_pairs={{1,0},{2,1},{3,2},{4,3},{5,4},{6,5},{7,6},{0,7},{9,8},{10,9},{11,1... | collective-permute-start | bytes 491528 | tf_op jit(solution)/shard_map/ppermute | solution.py:456

commit v3 on v2

--- a/solution.py
+++ b/solution.py
@@ -89,7 +89,7 @@
     return jnp.where(flag, 1.0, 0.0)
 
 
-def pack_kernel(coef, index, out):
+def setup_kernel(index, pick, weights, tags_out):
     row = iota((E, E), 0)
     col = iota((E, E), 1)
     old, new_row, dest = index[0:1, :], index[1:2, :], index[2:3, :]
@@ -107,10 +107,9 @@
     tags0 = jnp.where(row == 0, slot_f, jnp.where(row == 1, new_f, 0.0)).astype(BF16)
     tags1 = jnp.where(row == 2, slot_f, jnp.where(row == 3, new_f, 0.0)).astype(BF16)
     tags = dot_nt(pick0, tags0) + dot_nt(pick1, tags1)
-    tags = tags + jnp.where((col == 0) | (col == 2), float(E), 0.0)
-    out[pl.ds(40, E, stride=BLOCK), :] = tags
-    pick = jnp.concatenate([pick0, pick1], axis=0)
-    pick = jnp.concatenate([pick, pick], axis=1)
+    tags_out[...] = tags + jnp.where((col == 0) | (col == 2), float(E), 0.0)
+    half = jnp.concatenate([pick0, pick1], axis=0)
+    pick[...] = jnp.concatenate([half, half], axis=1)
     for q in range(4):
         mode = row + E * q
         i = lax.shift_right_logical(mode, 6)
@@ -118,13 +117,25 @@
         k = mode & 7
         live = jnp.maximum(jnp.maximum(i, j), k) <= kept
         weight = ((2 * i + 1) * (2 * j + 1) * (2 * k + 1)).astype(F32)
-        weight = jnp.where(live, jnp.sqrt(weight), 0.0)
-        for v in range(NV):
-            g = 4 * v + q
-            high, low = split(coef[v, E * q : E * (q + 1), :] * weight)
-            moved = dot_nt(pick, jnp.concatenate([high, low], axis=1))
-            out[pl.ds(g, E, stride=BLOCK), :] = moved[:E]
-            out[pl.ds(20 + g, E, stride=BLOCK), :] = moved[E:]
+        weights[E * q : E * (q + 1), :] = jnp.where(live, jnp.sqrt(weight), 0.0)
+
+
+def pack_kernel(coef, pick, weights, tags, out):
+    out[pl.ds(40, E, stride=BLOCK), :] = tags[...]
+
+    def send(group, rows):
+        high, low = split(rows)
+        moved = dot_nt(pick[...], jnp.concatenate([high, low], axis=1))
+        out[pl.ds(group, E, stride=BLOCK), :] = moved[:E]
+        out[pl.ds(20 + group, E, stride=BLOCK), :] = moved[E:]
+
+    for v in range(NV):
+        x = (coef[v] * weights[...]).reshape(N, N, N, E)
+        sums = [(x[:, p] + x[:, p + 2]) + (x[:, p + 4] + x[:, p + 6]) for p in range(2)]
+        send(v, jnp.concatenate([part.reshape(64, E) for part in sums], axis=0))
+        rest = x[:, 2:].reshape(3 * E, E)
+        for n in range(3):
+            send(NV + 3 * v + n, rest[E * n : E * (n + 1)])
 
 
 def write_traces(even, odd, upper, lower, v, i):
@@ -133,42 +144,64 @@
     lower[rows, :] = even - odd
 
 
-def unpack_kernel(got, mortar_up, mortar_low, solution, degree, upper, lower):
+def placed(got, place, group):
+    both = jnp.concatenate(
+        [got[pl.ds(group, E, stride=BLOCK), :], got[pl.ds(20 + group, E, stride=BLOCK), :]], axis=0
+    )
+    high, low = split(both)
+    moved = dot(place, jnp.concatenate([high, low], axis=1))
+    return (moved[:, :E] + moved[:, E:]).T
+
+
+def unpack_kernel(got, mortar_up, mortar_low, place_out, degree, upper, lower):
     row = iota((E, E), 0)
     tags = got[pl.ds(40, E, stride=BLOCK), :].T
     place0 = onehot(row.astype(F32) == tags[0:1, :]).astype(BF16)
     place1 = onehot(row.astype(F32) == tags[2:3, :]).astype(BF16)
     place = jnp.concatenate([place0, place1], axis=1)
+    place_out[...] = place
     degrees = jnp.concatenate([tags[1:2, :], tags[3:4, :]], axis=1)
     degrees = jnp.broadcast_to(degrees, (16, 2 * E)).astype(BF16)
     degree[...] = dot_nt(degrees, place)[:8, :]
-    for g in range(20):
-        both = jnp.concatenate(
-            [got[pl.ds(g, E, stride=BLOCK), :], got[pl.ds(20 + g, E, stride=BLOCK), :]], axis=0
-        )
-        high, low = split(both)
-        moved = dot(place, jnp.concatenate([high, low], axis=1))
-        solution[E * g : E * (g + 1), :] = (moved[:, :E] + moved[:, E:]).T
     for v in range(NV):
-        for i in range(N):
-            base = v * MODES + i * 64
-            line = [solution[base + 8 * j : base + 8 * j + 8, :] for j in range(N)]
-            even = (line[0] + line[2]) + (line[4] + line[6])
-            odd = (line[1] + line[3]) + (line[5] + line[7])
-            write_traces(even, odd, upper, lower, v, i)
+        sums = placed(got, place, v)
+        upper[64 * v : 64 * v + 64, :] = sums[:64] + sums[64:]
+        lower[64 * v : 64 * v + 64, :] = sums[:64] - sums[64:]
     for table, face in ((mortar_up, upper), (mortar_low, lower)):
         face[FACE:PAY, :] = jnp.full((PAY - FACE, E), -1.0, F32)
         face[FACE : FACE + 2, :] = table[:, 0:E].astype(F32)
         face[FACE + 2 : FACE + 4, 0:16] = table[:, E : E + 16].astype(F32)
 
 
+def unpack_rest(got, place, upper, lower, state):
+    pick = place[...]
+    for v in range(NV):
+        for n in range(3):
+            rows = placed(got, pick, NV + 3 * v + n)
+            for m in range(16):
+                i, j = divmod(16 * n + m, 6)
+                start = v * MODES + 64 * i + 8 * j + 16
+                state[start : start + 8, :] = rows[8 * m : 8 * m + 8]
+        for i in range(N):
+            base = v * MODES + 64 * i
+            face = slice(64 * v + 8 * i, 64 * v + 8 * i + 8)
+            line = [state[base + 8 * j : base + 8 * j + 8, :] for j in range(2, N)]
+            up, low = 0.5 * upper[face, :], 0.5 * lower[face, :]
+            state[base : base + 8, :] = (up + low) - (line[0] + line[2] + line[4])
+            state[base + 8 : base + 16, :] = (up - low) - (line[1] + line[3] + line[5])
+
+
+def couple_one(d, v, first, k):
+    half = (0.5 * k) * d[v]
+    if v in (0, 4):
+        half = half + 0.5 * d[first]
+    if v == first:
+        half = half + 0.5 * d[4]
+    return half
+
+
 def couple(d, first, k):
-    half = [(0.5 * k) * d[v] for v in range(NV)]
-    vel, pres = 0.5 * d[first], 0.5 * d[4]
-    half[0] = half[0] + vel
-    half[first] = half[first] + pres
-    half[4] = half[4] + vel
-    return half
+    return [couple_one(d, v, first, k) for v in range(NV)]
 
 
 def halves_of(plus, minus):
@@ -190,13 +223,15 @@
     if stage:
         first, before, lifts, *refs, state = refs
     else:
-        first, *refs = refs
-        state = first
+        got, place, *refs = refs
+        state = refs.pop(8)
     if stage < 2:
         sums_out = refs.pop(7)
     (degree, upper, lower, metric, near, ztab, out, xsum, zsum, xp, xm, zp, zm, xl, zl, cat, live) = refs
     row = iota((E, E), 0)
     masks = degree_masks(degree)
+    if stage == 0:
+        unpack_rest(got, place, upper, lower, state)
     for n in range(N):
         live[8 * n : 8 * n + 8, :] = masks[n]
     if stage:
@@ -357,33 +392,37 @@
         high, low = split(face[64 * v : 64 * v + 64, :])
         cat[64 * v : 64 * v + 64, 0:E] = high
         cat[64 * v : 64 * v + 64, E : 2 * E] = low
-    picked = dot(cat[...], routes)
-    result = []
-    for v in range(NV):
-        lines = [
-            [picked[64 * v + 8 * a : 64 * v + 8 * a + 8, E * n : E * n + E] for a in range(N)] for n in range(5)
-        ]
-        totals = []
-        for a in range(N):
-            total = lines[0][a]
-            for b in range(a, N):
-                total = total + RESTRICT[a][b] * lines[1 + (a + b) % 2][b]
-            for b in range(a + 1):
-                total = total + PROJECT[a][b] * lines[3 + (a + b) % 2][b]
-            totals.append(total)
-        result.append(totals)
-    return result
+    return dot(cat[...], routes)
+
+
+def mixed(picked, v):
+    lines = [[picked[64 * v + 8 * a : 64 * v + 8 * a + 8, E * n : E * n + E] for a in range(N)] for n in range(5)]
+    totals = []
+    for a in range(N):
+        total = lines[0][a]
+        for b in range(a, N):
+            total = total + RESTRICT[a][b] * lines[1 + (a + b) % 2][b]
+        for b in range(a + 1):
+            total = total + PROJECT[a][b] * lines[3 + (a + b) % 2][b]
+        totals.append(total)
+    return totals
 
 
 def far_lifts(above, below, cat_up, cat_low, routes):
-    up = far_side(above, cat_up, routes[0 : 2 * E, :])
-    low = far_side(below, cat_low, routes[2 * E : 4 * E, :])
-    result = []
-    for i in range(N):
-        plus = couple([up[v][i] for v in range(NV)], 2, -1.0)
-        minus = couple([low[v][i] for v in range(NV)], 2, 1.1)
-        result.append(halves_of(plus, minus))
-    return result
+    picked_up = far_side(above, cat_up, routes[0 : 2 * E, :])
+    picked_low = far_side(below, cat_low, routes[2 * E : 4 * E, :])
+    up, low = {}, {}
+    for v in (1, 3, 2, 4, 0):
+        for n in (2, 4) if v == 2 else (v,):
+            if n not in up:
+                up[n], low[n] = mixed(picked_up, n), mixed(picked_low, n)
+        even, odd = [], []
+        for i in range(N):
+            plus = couple_one({n: x[i] for n, x in up.items()}, v, 2, -1.0)
+            minus = couple_one({n: x[i] for n, x in low.items()}, v, 2, 1.1)
+            even.append(plus - minus)
+            odd.append(plus + minus)
+        yield v, even, odd
 
 
 def trace_kernel(stage, *refs):
@@ -401,16 +440,15 @@
         (sums, above, below, metric, degree, routes, upper, lower, lifts, cat_up, cat_low) = refs
     masks = degree_masks(degree)
     kq = lift_weights(metric, stage)
-    far = far_lifts(above, below, cat_up, cat_low, routes)
-    for i in range(N):
-        weight = [sum(masks[max(i, j)] * kq[j] for j in range(p, N, 2)) for p in range(2)]
-        for v in range(NV):
+    weights = [[sum(masks[max(i, j)] * kq[j] for j in range(p, N, 2)) for p in range(2)] for i in range(N)]
+    for v, lift_even, lift_odd in far_lifts(above, below, cat_up, cat_low, routes):
+        for i in range(N):
             rows = slice(64 * v + 8 * i, 64 * v + 8 * i + 8)
             odd_rows = slice(FACE + 64 * v + 8 * i, FACE + 64 * v + 8 * i + 8)
-            lifts[rows, :] = far[i][0][v]
-            lifts[odd_rows, :] = far[i][1][v]
-            even = sums[rows, :] + weight[0] * far[i][0][v]
-            odd = sums[odd_rows, :] + weight[1] * far[i][1][v]
+            lifts[rows, :] = lift_even[i]
+            lifts[odd_rows, :] = lift_odd[i]
+            even = sums[rows, :] + weights[i][0] * lift_even[i]
+            odd = sums[odd_rows, :] + weights[i][1] * lift_odd[i]
             write_traces(even, odd, upper, lower, v, i)
 
 
@@ -418,13 +456,13 @@
     back = 1.0 / jnp.sqrt((2 * iota((8, E), 0) + 1).astype(F32))
     masks = [m * back for m in degree_masks(degree)]
     kq = lift_weights(metric, 2)
-    far = far_lifts(above, below, cat_up, cat_low, routes)
     sent = []
-    for i in range(N):
-        for v in range(NV):
+    for v, lift_even, lift_odd in far_lifts(above, below, cat_up, cat_low, routes):
+        for i in range(N):
             for j in range(N):
                 start = 64 * i + 8 * j
-                value = partial[v * MODES + start : v * MODES + start + 8, :] + kq[j] * far[i][j % 2][v]
+                lift = (lift_even, lift_odd)[j % 2][i]
+                value = partial[v * MODES + start : v * MODES + start + 8, :] + kq[j] * lift
                 value = (masks[max(i, j)] * (1.0 / math.sqrt((2 * i + 1) * (2 * j + 1)))) * value
                 out[v, start : start + 8, :] = value
             part = pl.ds(64 * i, 64)
@@ -435,7 +473,7 @@
         copy.wait()
 
 
-def call(kernel, outs, scratch, args, result=VMEM):
+def call(kernel, outs, scratch, args, result=VMEM, cost=None):
     return pl.pallas_call(
         kernel,
         out_shape=outs,
@@ -443,6 +481,7 @@
         out_specs=jax.tree.map(lambda _: result, outs),
         scratch_shapes=scratch,
         compiler_params=PARAMS,
+        cost_estimate=cost,
     )(*args)
 
 
@@ -459,26 +498,31 @@
 
 def shards(coefficients, old_degree, new_degree, destination, metric, near, mortar_up, mortar_low):
     ztab = jnp.asarray(z_table(), BF16)
-    packed = call(
-        pack_kernel,
-        f32(E * BLOCK, E),
+    chosen = call(
+        setup_kernel,
+        (jax.ShapeDtypeStruct((2 * E, 2 * E), BF16), f32(MODES, E), f32(E, E)),
         [],
-        (coefficients, jnp.stack([old_degree, new_degree, destination])),
+        (jnp.stack([old_degree, new_degree, destination]),),
+        cost=pl.CostEstimate(flops=400_000_000, bytes_accessed=1_000_000, transcendentals=0),
     )
+    packed = call(pack_kernel, f32(E * BLOCK, E), [], (coefficients, *chosen))
     packed = packed.reshape(E, 1, BLOCK * E)
     got = lax.all_to_all(packed, ("curve", "sub"), split_axis=0, concat_axis=0, tiled=True)
     got = got.reshape(E * BLOCK, E)
-    first, degree, upper, lower = call(
-        unpack_kernel, (f32(ROWS, E), f32(8, E), f32(PAY, E), f32(PAY, E)), [], (got, mortar_up, mortar_low)
+    place, degree, upper, lower = call(
+        unpack_kernel,
+        (jax.ShapeDtypeStruct((E, 2 * E), BF16), f32(8, E), f32(PAY, E), f32(PAY, E)),
+        [],
+        (got, mortar_up, mortar_low),
     )
     faces = (f32(FACE, E), f32(FACE, E))
     cats = [pltpu.VMEM((FACE, 2 * E), BF16)] * 2
     for stage in range(3):
         above, below = swap(upper, lower)
-        given = (first,) if stage == 0 else (first, partial, lifts)
+        given = (got, place) if stage == 0 else (first, partial, lifts)
         partial, *sums = call(
             functools.partial(volume_kernel, stage),
-            (f32(ROWS, E), f32(2 * FACE, E))[: 2 if stage < 2 else 1],
+            (f32(ROWS, E), f32(2 * FACE, E), f32(ROWS, E))[: 3 - stage],
             [pltpu.VMEM((ROWS, E), F32), pltpu.VMEM((2 * MODES, E), F32)]
             + [pltpu.VMEM((FACE, E), F32)] * 4
             + [pltpu.VMEM((2 * FACE, E), F32)] * 2
@@ -486,6 +530,8 @@
             + ([pltpu.VMEM((ROWS, E), F32)] if stage else []),
             given + (degree, upper, lower, metric, near, ztab),
         )
+        if stage == 0:
+            first = sums.pop()
         body = functools.partial(trace_kernel, stage)
         outs = faces + (f32(2 * FACE, E),)
         if stage == 0:

time: 73.3 us -> 71.7 us (0.978)
  starting transfers between devices: 8.95 us -> 1.54 us
  waiting for transfers between devices: 3.31 us -> 10.4 us
  local copies, waits for them, and re-layouts: 1.34 us -> 0.2 us
    ppermute x3, starting transfers between devices: 8.89 us -> 0.05 us  [swap(): lax.ppermute(lower, 'sub', [((i + 1) % count, i) for i in range(count)])]
    ppermute x3, waiting for transfers between devices: 3.3 us -> 9.41 us  [swap(): lax.ppermute(upper, 'sub', [(i, (i + 1) % count) for i in range(count)])]
    ppermute x3, starting transfers between devices: 0.05 us -> 1.49 us  [swap(): lax.ppermute(upper, 'sub', [(i, (i + 1) % count) for i in range(count)])]
    unnamed x12, local copies, waits for them, and re-layouts: 1.34 us -> 0.2 us
    ppermute x3, waiting for transfers between devices: 0.01 us -> 1.01 us  [swap(): lax.ppermute(lower, 'sub', [((i + 1) % count, i) for i in range(count)])]
    pallas_call x8 -> x9, Pallas kernels: 10.6 us -> 10.7 us  [call(): pl.pallas_call(kernel, out_shape=outs, in_specs=[VMEM] * len(args), out_s...]
  transfers between devices with their start and end apart: 6 -> 6, of which waited for: 3 -> 6; matrix products, arithmetic and copies ran while one was open for 0% -> 0% of each run, Pallas kernels for 8% -> 8%
where the time goes in v3:
time: 71.7 us; the launch traced here: 71.6 us
  blocking collectives  47.7 us (67%)
  Pallas kernels  10.7 us (15%)
  waiting for transfers between devices  10.4 us (15%)
  starting transfers between devices  1.54 us (2%)
  other arithmetic  0.8 us (1%)
    all_to_all x1, blocking collectives, shards(): lax.all_to_all(packed, ('curve', 'sub'), split_axis=0, concat_axis=0, til...  47.7 us
    pallas_call x9, Pallas kernels, call(): pl.pallas_call(kernel, out_shape=outs, in_specs=[VMEM] * len(args), out_s...  10.7 us
    ppermute x3, waiting for transfers between devices, swap(): lax.ppermute(upper, 'sub', [(i, (i + 1) % count) for i in range(count)])  9.41 us
    ppermute x3, starting transfers between devices, swap(): lax.ppermute(upper, 'sub', [(i, (i + 1) % count) for i in range(count)])  1.49 us
  transfers between devices with their start and end apart: 6, of which 6 were waited for; matrix products, arithmetic and copies ran while one was open for 0% of the time, Pallas kernels for 8%

profile of v3, /device:TPU:0, one launch (start us, length us, event | category | flops | bytes accessed | tf_op | source)
XLA Modules:
  0.0 71.6 jit_solution(1241191745934559915)
XLA Ops:
  0.0 0.0 copy-start.1
  0.0 0.8 %pad_add_fusion.index = s32[3,128]{1,0:T(4,128)S(1)} fusion(s32[1,128]{1,0:T(1,128)} %bitcast.8, s32[1,128]{1,0:T(1,128)} %bitcast.9, s32[1,128]{1,0:T(1,128)} %bitcast.10), kind=kLoop, calls=%fused_computation | loop fusion | flops 768 | bytes 3072 | tf_op jit(solution)/shard_map/stack | solution.py:505
  0.8 0.4 shard_map.91
  1.2 0.2 copy-done.1
  1.4 0.9 %shard_map.92 = f32[5248,128]{1,0:T(8,128)S(1)} custom-call(f32[5,512,128]{2,1,0:T(8,128)S(1)} %copy-done.1, bf16[256,256]{1,0:T(8,128)(2,1)S(1)} %get-tuple-element.24.pick, f32[512,128]{1,0:T(8,128)S(1)} %get-tuple-element.25.weights, f32[128,128]{1,0:T(8,128)S(1)} %get-tuple-element.26.tags), custom_call_target="tpu_custom_call" | custom-call | tf_op jit(solution)/shard_map/pallas_call | solution.py:477
  2.2 0.0 copy-start.4
  2.2 0.0 copy-start.5
  2.3 47.7 %all_to_all.5 = f32[128,1,5248]{2,1,0:T(1,128)S(1)} all-to-all(f32[128,1,5248]{2,1,0:T(1,128)S(1)} %bitcast.7), channel_id=1, replica_groups=mesh['curve'=16,'sub'=8] {'curve','sub'}, dimensions={0} | all-to-all | bytes 5373952 | tf_op jit(solution)/shard_map/all_to_all | solution.py:510
  50.0 0.0 copy-done.4
  50.0 0.0 copy-done.5
  50.0 0.0 copy-start
  50.0 0.0 copy-start.2
  50.0 0.0 copy-start.3
  50.0 0.4 shard_map.93
  50.4 0.0 collective-permute-start
  50.4 0.5 collective-permute-start.1
  50.9 0.0 copy-done
  50.9 0.0 copy-done.2
  50.9 0.0 copy-done.3
  50.9 2.0 %shard_map.94 = (f32[2560,128]{1,0:T(8,128)S(1)}, f32[640,128]{1,0:T(8,128)S(1)}, f32[2560,128]{1,0:T(8,128)S(1)}) custom-call(f32[5248,128]{1,0:T(8,128)S(1)} %bitcast.6, bf16[128,256]{1,0:T(8,128)(2,1)S(1)} %get-tuple-element.27.refs_1_, f32[8,128]{1,0:T(8,128)S(1)} %get-tuple-element.28.refs_2_.refs_4_.refs_3_.degree, ...), custom_call_target="tpu_custom_call" | custom-call | tf_op jit(solution)/shard_map/pallas_call | solution.py:477
  52.9 0.4 collective-permute-done.refs_1_
  53.3 3.1 %collective-permute-done.1.refs_2_ = f32[328,128]{1,0:T(8,128)S(1)} collective-permute-done((f32[328,128]{1,0:T(8,128)S(1)}, f32[328,128]{1,0:T(8,128)S(1)}, u32[]{:S(2)}, u32[]{:S(2)}) %collective-permute-start.1) | collective-permute-done | bytes 167968 | tf_op jit(solution)/shard_map/ppermute | solution.py:494
  56.5 0.8 %shard_map.95 = (f32[320,128]{1,0:T(8,128)S(1)}, f32[320,128]{1,0:T(8,128)S(1)}, f32[640,128]{1,0:T(8,128)S(1)}, bf16[512,640]{1,0:T(8,128)(2,1)S(1)}) custom-call(f32[640,128]{1,0:T(8,128)S(1)} %get-tuple-element.33.refs_0_, f32[328,128]{1,0:T(8,128)S(1)} %collective-permute-done.refs_1_, f32[328,128]{1,0:T(8,128)S(1)} %collective-permute-done.1.refs_2_, ...), custom_call_target="tpu_custom_call" | custom-call | tf_op jit(solution)/shard_map/pallas_call | solution.py:477
  57.2 0.0 collective-permute-start.2
  57.2 0.5 collective-permute-start.3
  57.7 2.0 %shard_map.96 = (f32[2560,128]{1,0:T(8,128)S(1)}, f32[640,128]{1,0:T(8,128)S(1)}) custom-call(f32[2560,128]{1,0:T(8,128)S(1)} %get-tuple-element.31.refs_0_, f32[2560,128]{1,0:T(8,128)S(1)} %get-tuple-element.32.refs_1_, f32[640,128]{1,0:T(8,128)S(1)} %get-tuple-element.34.refs_2_, f32[8,128]{1,0:T(8,128)S(1)} %get-tuple-element.28.refs_2_.refs_4_.refs_3_.degree, ...), custom_call_target="tpu_custom_call" | custom-call | tf_op jit(solution)/shard_map/pallas_call | solution.py:477
  59.8 0.3 collective-permute-done.2.refs_1_
  60.1 3.1 %collective-permute-done.3.refs_2_ = f32[320,128]{1,0:T(8,128)S(1)} collective-permute-done((f32[320,128]{1,0:T(8,128)S(1)}, f32[320,128]{1,0:T(8,128)S(1)}, u32[]{:S(2)}, u32[]{:S(2)}) %collective-permute-start.3) | collective-permute-done | bytes 163872 | tf_op jit(solution)/shard_map/ppermute | solution.py:494
  63.2 0.5 shard_map.97
  63.7 0.0 collective-permute-start.4
  63.7 0.5 collective-permute-start.5
  64.2 2.0 %shard_map.98.partial = f32[2560,128]{1,0:T(8,128)S(1)} custom-call(f32[2560,128]{1,0:T(8,128)S(1)} %get-tuple-element.31.refs_0_, f32[2560,128]{1,0:T(8,128)S(1)} %get-tuple-element.37.refs_1_, f32[640,128]{1,0:T(8,128)S(1)} %get-tuple-element.40.refs_2_, f32[8,128]{1,0:T(8,128)S(1)} %get-tuple-element.28.refs_2_.refs_4_.refs_3_.degree, ...), custom_call_target="tpu_custom_call" | custom-call | tf_op jit(solution)/shard_map/pallas_call | solution.py:477
  66.2 0.3 collective-permute-done.4.above
  66.6 3.1 %collective-permute-done.5.below = f32[320,128]{1,0:T(8,128)S(1)} collective-permute-done((f32[320,128]{1,0:T(8,128)S(1)}, f32[320,128]{1,0:T(8,128)S(1)}, u32[]{:S(2)}, u32[]{:S(2)}) %collective-permute-start.5) | collective-permute-done | bytes 163872 | tf_op jit(solution)/shard_map/ppermute | solution.py:494
  69.7 1.8 %shard_map.99 = f32[5,512,128]{2,1,0:T(8,128)} custom-call(f32[2560,128]{1,0:T(8,128)S(1)} %shard_map.98.partial, f32[320,128]{1,0:T(8,128)S(1)} %collective-permute-done.4.above, f32[320,128]{1,0:T(8,128)S(1)} %collective-permute-done.5.below, f32[3,128]{1,0:T(4,128)S(1)} %copy-done.2, f32[8,128]{1,0:T(8,128)S(1)} %get-tuple-element.28.refs_2_.refs_4_.refs_3_.degree, ...), custom_call_target="tpu_custom_call" | custom-call | tf_op jit(solution)/shard_map/pallas_call | solution.py:477
Async XLA Ops:
  0.0 1.4 %copy-start.1 = (f32[5,512,128]{2,1,0:T(8,128)S(1)}, f32[5,512,128]{2,1,0:T(8,128)}, u32[]{:S(2)}) copy-start(f32[5,512,128]{2,1,0:T(8,128)} %coef.1) | copy-start | bytes 3932164
  2.2 47.8 %copy-start.4 = (s32[2,144]{1,0:T(2,128)S(1)}, s32[2,144]{1,0:T(2,128)}, u32[]{:S(2)}) copy-start(s32[2,144]{1,0:T(2,128)} %refs_5_.3) | copy-start | bytes 3460
  2.2 47.7 %copy-start.5 = (s32[2,144]{1,0:T(2,128)S(1)}, s32[2,144]{1,0:T(2,128)}, u32[]{:S(2)}) copy-start(s32[2,144]{1,0:T(2,128)} %refs_6_.5) | copy-start | bytes 3460
  50.0 0.9 %copy-start = (bf16[320,256]{1,0:T(8,128)(2,1)S(1)}, bf16[320,256]{1,0:T(8,128)(2,1)}, u32[]{:S(2)}) copy-start(bf16[320,256]{1,0:T(8,128)(2,1)} %constant.2.clone.refs_7_.refs_8_) | copy-start | bytes 491524
  50.0 0.9 %copy-start.2 = (f32[3,128]{1,0:T(4,128)S(1)}, f32[3,128]{1,0:T(4,128)}, u32[]{:S(2)}) copy-start(f32[3,128]{1,0:T(4,128)} %metric.1) | copy-start | bytes 4612
  50.0 0.9 %copy-start.3 = (s32[4,128]{1,0:T(4,128)S(1)}, s32[4,128]{1,0:T(4,128)}, u32[]{:S(2)}) copy-start(s32[4,128]{1,0:T(4,128)} %refs_7_.4) | copy-start | bytes 6148
  50.4 2.9 %collective-permute-start = (f32[328,128]{1,0:T(8,128)S(1)}, f32[328,128]{1,0:T(8,128)S(1)}, u32[]{:S(2)}, u32[]{:S(2)}) collective-permute-start(f32[328,128]{1,0:T(8,128)S(1)} %get-tuple-element.30.refs_4_), channel_id=1, source_target_pairs={{1,0},{2,1},{3,2},{4,3},{5,4},{6,5},{7,6},{0,7},{9,8},{10,9},{11,1... | collective-permute-start | bytes 503816 | tf_op jit(solution)/shard_map/ppermute | solution.py:495
  50.4 6.0 %collective-permute-start.1 = (f32[328,128]{1,0:T(8,128)S(1)}, f32[328,128]{1,0:T(8,128)S(1)}, u32[]{:S(2)}, u32[]{:S(2)}) collective-permute-start(f32[328,128]{1,0:T(8,128)S(1)} %get-tuple-element.29.refs_3_), channel_id=1, source_target_pairs={{0,1},{1,2},{2,3},{3,4},{4,5},{5,6},{6,7},{7,0},{8,9},{9,10},{10,1... | collective-permute-start | bytes 503816 | tf_op jit(solution)/shard_map/ppermute | solution.py:494
  57.2 2.9 %collective-permute-start.2 = (f32[320,128]{1,0:T(8,128)S(1)}, f32[320,128]{1,0:T(8,128)S(1)}, u32[]{:S(2)}, u32[]{:S(2)}) collective-permute-start(f32[320,128]{1,0:T(8,128)S(1)} %get-tuple-element.36.refs_5_), channel_id=1, source_target_pairs={{1,0},{2,1},{3,2},{4,3},{5,4},{6,5},{7,6},{0,7},{9,8},{10,9},{11,1... | collective-permute-start | bytes 491528 | tf_op jit(solution)/shard_map/ppermute | solution.py:495
  57.2 6.0 %collective-permute-start.3 = (f32[320,128]{1,0:T(8,128)S(1)}, f32[320,128]{1,0:T(8,128)S(1)}, u32[]{:S(2)}, u32[]{:S(2)}) collective-permute-start(f32[320,128]{1,0:T(8,128)S(1)} %get-tuple-element.35.refs_4_), channel_id=1, source_target_pairs={{0,1},{1,2},{2,3},{3,4},{4,5},{5,6},{6,7},{7,0},{8,9},{9,10},{10,1... | collective-permute-start | bytes 491528 | tf_op jit(solution)/shard_map/ppermute | solution.py:494
  63.7 2.9 %collective-permute-start.4 = (f32[320,128]{1,0:T(8,128)S(1)}, f32[320,128]{1,0:T(8,128)S(1)}, u32[]{:S(2)}, u32[]{:S(2)}) collective-permute-start(f32[320,128]{1,0:T(8,128)S(1)} %get-tuple-element.42.refs_5_), channel_id=1, source_target_pairs={{1,0},{2,1},{3,2},{4,3},{5,4},{6,5},{7,6},{0,7},{9,8},{10,9},{11,1... | collective-permute-start | bytes 491528 | tf_op jit(solution)/shard_map/ppermute | solution.py:495
  63.7 6.0 %collective-permute-start.5 = (f32[320,128]{1,0:T(8,128)S(1)}, f32[320,128]{1,0:T(8,128)S(1)}, u32[]{:S(2)}, u32[]{:S(2)}) collective-permute-start(f32[320,128]{1,0:T(8,128)S(1)} %get-tuple-element.41.refs_4_), channel_id=1, source_target_pairs={{0,1},{1,2},{2,3},{3,4},{4,5},{5,6},{6,7},{7,0},{8,9},{9,10},{10,1... | collective-permute-start | bytes 491528 | tf_op jit(solution)/shard_map/ppermute | solution.py:494

commit v4 on v3

--- a/solution.py
+++ b/solution.py
@@ -123,19 +123,21 @@
 def pack_kernel(coef, pick, weights, tags, out):
     out[pl.ds(40, E, stride=BLOCK), :] = tags[...]
 
-    def send(group, rows):
+    def send(group_a, group_b, rows):
         high, low = split(rows)
         moved = dot_nt(pick[...], jnp.concatenate([high, low], axis=1))
-        out[pl.ds(group, E, stride=BLOCK), :] = moved[:E]
-        out[pl.ds(20 + group, E, stride=BLOCK), :] = moved[E:]
+        for n, group in enumerate((group_a, group_b)):
+            out[pl.ds(group, E, stride=BLOCK), :] = moved[:E, E * n : E * n + E]
+            out[pl.ds(20 + group, E, stride=BLOCK), :] = moved[E:, E * n : E * n + E]
 
     for v in range(NV):
         x = (coef[v] * weights[...]).reshape(N, N, N, E)
         sums = [(x[:, p] + x[:, p + 2]) + (x[:, p + 4] + x[:, p + 6]) for p in range(2)]
-        send(v, jnp.concatenate([part.reshape(64, E) for part in sums], axis=0))
+        sums = [part.reshape(64, E) for part in sums]
         rest = x[:, 2:].reshape(3 * E, E)
-        for n in range(3):
-            send(NV + 3 * v + n, rest[E * n : E * (n + 1)])
+        base = NV + 3 * v
+        send(v, base, jnp.concatenate(sums + [rest[:E]], axis=0))
+        send(base + 1, base + 2, rest[E:])
 
 
 def write_traces(even, odd, upper, lower, v, i):

time: 71.7 us -> 71.4 us (level)
  no operation moved by 1% of the time
where the time goes in v4:
time: 71.4 us; the launch traced here: 71.3 us
  blocking collectives  47.7 us (67%)
  Pallas kernels  10.4 us (15%)
  waiting for transfers between devices  10.4 us (15%)
  starting transfers between devices  1.54 us (2%)
  other arithmetic  0.8 us (1%)
    all_to_all x1, blocking collectives, shards(): lax.all_to_all(packed, ('curve', 'sub'), split_axis=0, concat_axis=0, til...  47.7 us
    pallas_call x9, Pallas kernels, call(): pl.pallas_call(kernel, out_shape=outs, in_specs=[VMEM] * len(args), out_s...  10.4 us
    ppermute x3, waiting for transfers between devices, swap(): lax.ppermute(upper, 'sub', [(i, (i + 1) % count) for i in range(count)])  9.41 us
    ppermute x3, starting transfers between devices, swap(): lax.ppermute(upper, 'sub', [(i, (i + 1) % count) for i in range(count)])  1.49 us
  transfers between devices with their start and end apart: 6, of which 6 were waited for; matrix products, arithmetic and copies ran while one was open for 0% of the time, Pallas kernels for 8%

profile of v4, /device:TPU:0, one launch (start us, length us, event | category | flops | bytes accessed | tf_op | source)
XLA Modules:
  0.0 71.3 jit_solution(4196833006451711178)
XLA Ops:
  0.0 0.0 copy-start.1
  0.0 0.8 %pad_add_fusion.index = s32[3,128]{1,0:T(4,128)S(1)} fusion(s32[1,128]{1,0:T(1,128)} %bitcast.8, s32[1,128]{1,0:T(1,128)} %bitcast.9, s32[1,128]{1,0:T(1,128)} %bitcast.10), kind=kLoop, calls=%fused_computation | loop fusion | flops 768 | bytes 3072 | tf_op jit(solution)/shard_map/stack | solution.py:507
  0.8 0.4 shard_map.91
  1.2 0.2 copy-done.1
  1.4 0.6 shard_map.92
  1.9 0.0 copy-start.4
  2.0 0.0 copy-start.5
  2.0 47.7 %all_to_all.5 = f32[128,1,5248]{2,1,0:T(1,128)S(1)} all-to-all(f32[128,1,5248]{2,1,0:T(1,128)S(1)} %bitcast.7), channel_id=1, replica_groups=mesh['curve'=16,'sub'=8] {'curve','sub'}, dimensions={0} | all-to-all | bytes 5373952 | tf_op jit(solution)/shard_map/all_to_all | solution.py:512
  49.7 0.0 copy-done.4
  49.7 0.0 copy-done.5
  49.7 0.0 copy-start
  49.7 0.0 copy-start.2
  49.7 0.0 copy-start.3
  49.7 0.4 shard_map.93
  50.1 0.0 collective-permute-start
  50.1 0.5 collective-permute-start.1
  50.6 0.0 copy-done
  50.6 0.0 copy-done.2
  50.6 0.0 copy-done.3
  50.6 2.0 %shard_map.94 = (f32[2560,128]{1,0:T(8,128)S(1)}, f32[640,128]{1,0:T(8,128)S(1)}, f32[2560,128]{1,0:T(8,128)S(1)}) custom-call(f32[5248,128]{1,0:T(8,128)S(1)} %bitcast.6, bf16[128,256]{1,0:T(8,128)(2,1)S(1)} %get-tuple-element.27.refs_1_, f32[8,128]{1,0:T(8,128)S(1)} %get-tuple-element.28.refs_2_.refs_4_.refs_3_.degree, ...), custom_call_target="tpu_custom_call" | custom-call | tf_op jit(solution)/shard_map/pallas_call | solution.py:479
  52.7 0.4 collective-permute-done.refs_1_
  53.0 3.1 %collective-permute-done.1.refs_2_ = f32[328,128]{1,0:T(8,128)S(1)} collective-permute-done((f32[328,128]{1,0:T(8,128)S(1)}, f32[328,128]{1,0:T(8,128)S(1)}, u32[]{:S(2)}, u32[]{:S(2)}) %collective-permute-start.1) | collective-permute-done | bytes 167968 | tf_op jit(solution)/shard_map/ppermute | solution.py:496
  56.2 0.8 %shard_map.95 = (f32[320,128]{1,0:T(8,128)S(1)}, f32[320,128]{1,0:T(8,128)S(1)}, f32[640,128]{1,0:T(8,128)S(1)}, bf16[512,640]{1,0:T(8,128)(2,1)S(1)}) custom-call(f32[640,128]{1,0:T(8,128)S(1)} %get-tuple-element.33.refs_0_, f32[328,128]{1,0:T(8,128)S(1)} %collective-permute-done.refs_1_, f32[328,128]{1,0:T(8,128)S(1)} %collective-permute-done.1.refs_2_, ...), custom_call_target="tpu_custom_call" | custom-call | tf_op jit(solution)/shard_map/pallas_call | solution.py:479
  56.9 0.0 collective-permute-start.2
  56.9 0.5 collective-permute-start.3
  57.4 2.0 %shard_map.96 = (f32[2560,128]{1,0:T(8,128)S(1)}, f32[640,128]{1,0:T(8,128)S(1)}) custom-call(f32[2560,128]{1,0:T(8,128)S(1)} %get-tuple-element.31.refs_0_, f32[2560,128]{1,0:T(8,128)S(1)} %get-tuple-element.32.refs_1_, f32[640,128]{1,0:T(8,128)S(1)} %get-tuple-element.34.refs_2_, f32[8,128]{1,0:T(8,128)S(1)} %get-tuple-element.28.refs_2_.refs_4_.refs_3_.degree, ...), custom_call_target="tpu_custom_call" | custom-call | tf_op jit(solution)/shard_map/pallas_call | solution.py:479
  59.5 0.3 collective-permute-done.2.refs_1_
  59.8 3.1 %collective-permute-done.3.refs_2_ = f32[320,128]{1,0:T(8,128)S(1)} collective-permute-done((f32[320,128]{1,0:T(8,128)S(1)}, f32[320,128]{1,0:T(8,128)S(1)}, u32[]{:S(2)}, u32[]{:S(2)}) %collective-permute-start.3) | collective-permute-done | bytes 163872 | tf_op jit(solution)/shard_map/ppermute | solution.py:496
  62.9 0.5 shard_map.97
  63.4 0.0 collective-permute-start.4
  63.5 0.5 collective-permute-start.5
  63.9 2.0 %shard_map.98.partial = f32[2560,128]{1,0:T(8,128)S(1)} custom-call(f32[2560,128]{1,0:T(8,128)S(1)} %get-tuple-element.31.refs_0_, f32[2560,128]{1,0:T(8,128)S(1)} %get-tuple-element.37.refs_1_, f32[640,128]{1,0:T(8,128)S(1)} %get-tuple-element.40.refs_2_, f32[8,128]{1,0:T(8,128)S(1)} %get-tuple-element.28.refs_2_.refs_4_.refs_3_.degree, ...), custom_call_target="tpu_custom_call" | custom-call | tf_op jit(solution)/shard_map/pallas_call | solution.py:479
  65.9 0.3 collective-permute-done.4.above
  66.3 3.1 %collective-permute-done.5.below = f32[320,128]{1,0:T(8,128)S(1)} collective-permute-done((f32[320,128]{1,0:T(8,128)S(1)}, f32[320,128]{1,0:T(8,128)S(1)}, u32[]{:S(2)}, u32[]{:S(2)}) %collective-permute-start.5) | collective-permute-done | bytes 163872 | tf_op jit(solution)/shard_map/ppermute | solution.py:496
  69.4 1.8 %shard_map.99 = f32[5,512,128]{2,1,0:T(8,128)} custom-call(f32[2560,128]{1,0:T(8,128)S(1)} %shard_map.98.partial, f32[320,128]{1,0:T(8,128)S(1)} %collective-permute-done.4.above, f32[320,128]{1,0:T(8,128)S(1)} %collective-permute-done.5.below, f32[3,128]{1,0:T(4,128)S(1)} %copy-done.2, f32[8,128]{1,0:T(8,128)S(1)} %get-tuple-element.28.refs_2_.refs_4_.refs_3_.degree, ...), custom_call_target="tpu_custom_call" | custom-call | tf_op jit(solution)/shard_map/pallas_call | solution.py:479
Async XLA Ops:
  0.0 1.4 %copy-start.1 = (f32[5,512,128]{2,1,0:T(8,128)S(1)}, f32[5,512,128]{2,1,0:T(8,128)}, u32[]{:S(2)}) copy-start(f32[5,512,128]{2,1,0:T(8,128)} %coef.1) | copy-start | bytes 3932164
  1.9 47.8 %copy-start.4 = (s32[2,144]{1,0:T(2,128)S(1)}, s32[2,144]{1,0:T(2,128)}, u32[]{:S(2)}) copy-start(s32[2,144]{1,0:T(2,128)} %refs_5_.3) | copy-start | bytes 3460
  2.0 47.7 %copy-start.5 = (s32[2,144]{1,0:T(2,128)S(1)}, s32[2,144]{1,0:T(2,128)}, u32[]{:S(2)}) copy-start(s32[2,144]{1,0:T(2,128)} %refs_6_.5) | copy-start | bytes 3460
  49.7 0.9 %copy-start = (bf16[320,256]{1,0:T(8,128)(2,1)S(1)}, bf16[320,256]{1,0:T(8,128)(2,1)}, u32[]{:S(2)}) copy-start(bf16[320,256]{1,0:T(8,128)(2,1)} %constant.2.clone.refs_7_.refs_8_) | copy-start | bytes 491524
  49.7 0.9 %copy-start.2 = (f32[3,128]{1,0:T(4,128)S(1)}, f32[3,128]{1,0:T(4,128)}, u32[]{:S(2)}) copy-start(f32[3,128]{1,0:T(4,128)} %metric.1) | copy-start | bytes 4612
  49.7 0.9 %copy-start.3 = (s32[4,128]{1,0:T(4,128)S(1)}, s32[4,128]{1,0:T(4,128)}, u32[]{:S(2)}) copy-start(s32[4,128]{1,0:T(4,128)} %refs_7_.4) | copy-start | bytes 6148
  50.1 2.9 %collective-permute-start = (f32[328,128]{1,0:T(8,128)S(1)}, f32[328,128]{1,0:T(8,128)S(1)}, u32[]{:S(2)}, u32[]{:S(2)}) collective-permute-start(f32[328,128]{1,0:T(8,128)S(1)} %get-tuple-element.30.refs_4_), channel_id=1, source_target_pairs={{1,0},{2,1},{3,2},{4,3},{5,4},{6,5},{7,6},{0,7},{9,8},{10,9},{11,1... | collective-permute-start | bytes 503816 | tf_op jit(solution)/shard_map/ppermute | solution.py:497
  50.1 6.0 %collective-permute-start.1 = (f32[328,128]{1,0:T(8,128)S(1)}, f32[328,128]{1,0:T(8,128)S(1)}, u32[]{:S(2)}, u32[]{:S(2)}) collective-permute-start(f32[328,128]{1,0:T(8,128)S(1)} %get-tuple-element.29.refs_3_), channel_id=1, source_target_pairs={{0,1},{1,2},{2,3},{3,4},{4,5},{5,6},{6,7},{7,0},{8,9},{9,10},{10,1... | collective-permute-start | bytes 503816 | tf_op jit(solution)/shard_map/ppermute | solution.py:496
  56.9 2.9 %collective-permute-start.2 = (f32[320,128]{1,0:T(8,128)S(1)}, f32[320,128]{1,0:T(8,128)S(1)}, u32[]{:S(2)}, u32[]{:S(2)}) collective-permute-start(f32[320,128]{1,0:T(8,128)S(1)} %get-tuple-element.36.refs_5_), channel_id=1, source_target_pairs={{1,0},{2,1},{3,2},{4,3},{5,4},{6,5},{7,6},{0,7},{9,8},{10,9},{11,1... | collective-permute-start | bytes 491528 | tf_op jit(solution)/shard_map/ppermute | solution.py:497
  56.9 6.0 %collective-permute-start.3 = (f32[320,128]{1,0:T(8,128)S(1)}, f32[320,128]{1,0:T(8,128)S(1)}, u32[]{:S(2)}, u32[]{:S(2)}) collective-permute-start(f32[320,128]{1,0:T(8,128)S(1)} %get-tuple-element.35.refs_4_), channel_id=1, source_target_pairs={{0,1},{1,2},{2,3},{3,4},{4,5},{5,6},{6,7},{7,0},{8,9},{9,10},{10,1... | collective-permute-start | bytes 491528 | tf_op jit(solution)/shard_map/ppermute | solution.py:496
  63.4 2.9 %collective-permute-start.4 = (f32[320,128]{1,0:T(8,128)S(1)}, f32[320,128]{1,0:T(8,128)S(1)}, u32[]{:S(2)}, u32[]{:S(2)}) collective-permute-start(f32[320,128]{1,0:T(8,128)S(1)} %get-tuple-element.42.refs_5_), channel_id=1, source_target_pairs={{1,0},{2,1},{3,2},{4,3},{5,4},{6,5},{7,6},{0,7},{9,8},{10,9},{11,1... | collective-permute-start | bytes 491528 | tf_op jit(solution)/shard_map/ppermute | solution.py:497
  63.5 6.0 %collective-permute-start.5 = (f32[320,128]{1,0:T(8,128)S(1)}, f32[320,128]{1,0:T(8,128)S(1)}, u32[]{:S(2)}, u32[]{:S(2)}) collective-permute-start(f32[320,128]{1,0:T(8,128)S(1)} %get-tuple-element.41.refs_4_), channel_id=1, source_target_pairs={{0,1},{1,2},{2,3},{3,4},{4,5},{5,6},{6,7},{7,0},{8,9},{9,10},{10,1... | collective-permute-start | bytes 491528 | tf_op jit(solution)/shard_map/ppermute | solution.py:496

commit v5 on v4

--- a/solution.py
+++ b/solution.py
@@ -140,6 +140,14 @@
         send(base + 1, base + 2, rest[E:])
 
 
+def is_even():
+    return (lax.axis_index("sub") & 1) == 0
+
+
+def odd_sign():
+    return jnp.where(is_even(), 1.0, -1.0)
+
+
 def write_traces(even, odd, upper, lower, v, i):
     rows = slice((v * N + i) * N, (v * N + i) * N + N)
     upper[rows, :] = even + odd
@@ -155,8 +163,9 @@
     return (moved[:, :E] + moved[:, E:]).T
 
 
-def unpack_kernel(got, mortar_up, mortar_low, place_out, degree, upper, lower):
+def unpack_kernel(got, mortar_up, mortar_low, place_out, degree, inner, outer):
     row = iota((E, E), 0)
+    sign = odd_sign()
     tags = got[pl.ds(40, E, stride=BLOCK), :].T
     place0 = onehot(row.astype(F32) == tags[0:1, :]).astype(BF16)
     place1 = onehot(row.astype(F32) == tags[2:3, :]).astype(BF16)
@@ -167,16 +176,19 @@
     degree[...] = dot_nt(degrees, place)[:8, :]
     for v in range(NV):
         sums = placed(got, place, v)
-        upper[64 * v : 64 * v + 64, :] = sums[:64] + sums[64:]
-        lower[64 * v : 64 * v + 64, :] = sums[:64] - sums[64:]
-    for table, face in ((mortar_up, upper), (mortar_low, lower)):
+        inner[64 * v : 64 * v + 64, :] = sums[:64] + sign * sums[64:]
+        outer[64 * v : 64 * v + 64, :] = sums[:64] - sign * sums[64:]
+    up, low = mortar_up[...].astype(F32), mortar_low[...].astype(F32)
+    even = is_even()
+    for table, face in ((jnp.where(even, up, low), inner), (jnp.where(even, low, up), outer)):
         face[FACE:PAY, :] = jnp.full((PAY - FACE, E), -1.0, F32)
-        face[FACE : FACE + 2, :] = table[:, 0:E].astype(F32)
-        face[FACE + 2 : FACE + 4, 0:16] = table[:, E : E + 16].astype(F32)
-
-
-def unpack_rest(got, place, upper, lower, state):
+        face[FACE : FACE + 2, :] = table[:, 0:E]
+        face[FACE + 2 : FACE + 4, 0:16] = table[:, E : E + 16]
+
+
+def unpack_rest(got, place, inner, outer, state):
     pick = place[...]
+    half_sign = 0.5 * odd_sign()
     for v in range(NV):
         for n in range(3):
             rows = placed(got, pick, NV + 3 * v + n)
@@ -188,9 +200,9 @@
             base = v * MODES + 64 * i
             face = slice(64 * v + 8 * i, 64 * v + 8 * i + 8)
             line = [state[base + 8 * j : base + 8 * j + 8, :] for j in range(2, N)]
-            up, low = 0.5 * upper[face, :], 0.5 * lower[face, :]
-            state[base : base + 8, :] = (up + low) - (line[0] + line[2] + line[4])
-            state[base + 8 : base + 16, :] = (up - low) - (line[1] + line[3] + line[5])
+            near, far = inner[face, :], outer[face, :]
+            state[base : base + 8, :] = 0.5 * (near + far) - (line[0] + line[2] + line[4])
+            state[base + 8 : base + 16, :] = half_sign * (near - far) - (line[1] + line[3] + line[5])
 
 
 def couple_one(d, v, first, k):
@@ -229,11 +241,11 @@
         state = refs.pop(8)
     if stage < 2:
         sums_out = refs.pop(7)
-    (degree, upper, lower, metric, near, ztab, out, xsum, zsum, xp, xm, zp, zm, xl, zl, cat, live) = refs
+    (degree, inner, outer, metric, near, ztab, out, xsum, zsum, xp, xm, zp, zm, xl, zl, cat, live) = refs
     row = iota((E, E), 0)
     masks = degree_masks(degree)
     if stage == 0:
-        unpack_rest(got, place, upper, lower, state)
+        unpack_rest(got, place, inner, outer, state)
     for n in range(N):
         live[8 * n : 8 * n + 8, :] = masks[n]
     if stage:
@@ -268,7 +280,7 @@
             odd = (line[1] + line[3]) + (line[5] + line[7])
             write_traces(even, odd, xp, xm, v, j)
 
-    def outer(face, pick):
+    def across(face, pick):
         for v in range(NV):
             high, low = split(face[64 * v : 64 * v + 64, :])
             cat[64 * v : 64 * v + 64, 0:E] = high
@@ -282,8 +294,8 @@
         (xp, xm, (0, 1), 1, 2.0, 1.0, xl),
         (zp, zm, (2, 3), 3, 1.0, 0.5, zl),
     ):
-        d_plus = by_variable(outer(minus, gather[where[0]]) - plus[...])
-        d_minus = by_variable(outer(plus, gather[where[1]]) - minus[...])
+        d_plus = by_variable(across(minus, gather[where[0]]) - plus[...])
+        d_minus = by_variable(across(plus, gather[where[1]]) - minus[...])
         even, odd = halves_of(couple(d_plus, first_v, -1.0), couple(d_minus, first_v, k_minus))
         for v in range(NV):
             result[64 * v : 64 * v + 64, :] = scale * even[v] if scale != 1.0 else even[v]
@@ -294,6 +306,7 @@
     ky = [full[1] * (-0.05 * beta * STEP * (2 * a + 1)) for a in range(N)]
     kz = full[2] * (-beta * STEP) * (2 * iota((8, E), 0) + 1).astype(F32)
     odd_k = (iota((8, E), 0) & 1) == 1
+    even_device = is_even()
 
     def at(ref, start):
         return ref[pl.ds(pl.multiple_of(start, 8), 8), :]
@@ -318,18 +331,20 @@
     lax.fori_loop(0, N, x_pass, 0)
 
     def y_pass(i, carry):
-        d_plus = [-at(upper, 64 * v + 8 * i) for v in range(NV)]
-        d_minus = [-at(lower, 64 * v + 8 * i) for v in range(NV)]
+        near_in = [-at(inner, 64 * v + 8 * i) for v in range(NV)]
+        near_out = [-at(outer, 64 * v + 8 * i) for v in range(NV)]
+        d_plus = [jnp.where(even_device, a, b) for a, b in zip(near_in, near_out)]
+        d_minus = [jnp.where(even_device, b, a) for a, b in zip(near_in, near_out)]
         even, odd = halves_of(couple(d_plus, 2, -1.0), couple(d_minus, 2, 1.1))
         s = [[10.0 * x for x in even], [10.0 * x for x in odd]]
         z_even = [at(zl, 64 * v + 8 * i) for v in range(NV)]
         z_odd = [at(zl, FACE + 64 * v + 8 * i) for v in range(NV)]
         sums = [[None] * NV, [None] * NV]
         for j in range(N - 1, -1, -1):
-            inner = 64 * i + 8 * j
-            rows = [v * MODES + inner for v in range(NV)]
+            offset = 64 * i + 8 * j
+            rows = [v * MODES + offset for v in range(NV)]
             c = [at(state, rows[v]) for v in range(NV)]
-            sw, sp = at(zsum, inner), at(zsum, MODES + inner)
+            sw, sp = at(zsum, offset), at(zsum, MODES + offset)
             zs = (sw, None, None, sp, sw)
             now = s[j % 2]
             mask = at(live, 8 * jnp.maximum(i, j))
@@ -371,8 +386,8 @@
     def own(r):
         return jnp.concatenate([table[r : r + 1, 0:E].astype(F32), table[r : r + 1, E : E + 16].astype(F32), pad], axis=1)
 
-    far_elem = jnp.concatenate([pay[FACE : FACE + 1, :], pay[FACE + 2 : FACE + 3, :]], axis=1)
-    far_half = jnp.concatenate([pay[FACE + 1 : FACE + 2, :], pay[FACE + 3 : FACE + 4, :]], axis=1)
+    far_elem = jnp.concatenate([pay[0:1, :], pay[2:3, :]], axis=1)
+    far_half = jnp.concatenate([pay[1:2, :], pay[3:4, :]], axis=1)
     own_elem, own_half = own(0), own(1)
     far_pick = jnp.where(wide == far_elem, inside, 0.0)
     own_pick = onehot(wide == own_elem).astype(BF16)
@@ -389,11 +404,13 @@
     return [dot_nt((far_pick * w).astype(BF16), own_pick).astype(BF16) for w in weights]
 
 
-def far_side(face, cat, routes):
+def far_side(first, second, cat, routes):
+    even = is_even()
     for v in range(NV):
-        high, low = split(face[64 * v : 64 * v + 64, :])
-        cat[64 * v : 64 * v + 64, 0:E] = high
-        cat[64 * v : 64 * v + 64, E : 2 * E] = low
+        rows = slice(64 * v, 64 * v + 64)
+        high, low = split(jnp.where(even, first[rows, :], second[rows, :]))
+        cat[rows, 0:E] = high
+        cat[rows, E : 2 * E] = low
     return dot(cat[...], routes)
 
 
@@ -410,9 +427,9 @@
     return totals
 
 
-def far_lifts(above, below, cat_up, cat_low, routes):
-    picked_up = far_side(above, cat_up, routes[0 : 2 * E, :])
-    picked_low = far_side(below, cat_low, routes[2 * E : 4 * E, :])
+def far_lifts(from_in, from_out, cat_up, cat_low, routes):
+    picked_up = far_side(from_in, from_out, cat_up, routes[0 : 2 * E, :])
+    picked_low = far_side(from_out, from_in, cat_low, routes[2 * E : 4 * E, :])
     up, low = {}, {}
     for v in (1, 3, 2, 4, 0):
         for n in (2, 4) if v == 2 else (v,):
@@ -429,21 +446,25 @@
 
 def trace_kernel(stage, *refs):
     if stage == 0:
-        (sums, above, below, metric, degree, table_up, table_low, upper, lower, lifts, routes, cat_up, cat_low) = refs
+        (sums, from_in, from_out, metric, degree, table_up, table_low, inner, outer, lifts, routes, cat_up, cat_low) = refs
         place = lax.axis_index("sub")
         last = lax.axis_size("sub") - 1
         inside = (jnp.where(place < last, 1.0, 0.0), jnp.where(place > 0, 1.0, 0.0))
-        for side, (pay, table) in enumerate(((above, table_up), (below, table_low))):
+        tail = slice(FACE, PAY)
+        tail_up = jnp.where(is_even(), from_in[tail, :], from_out[tail, :])
+        tail_low = jnp.where(is_even(), from_out[tail, :], from_in[tail, :])
+        for side, (pay, table) in enumerate(((tail_up, table_up), (tail_low, table_low))):
             for n, route in enumerate(build_routes(pay, table, inside[side])):
                 for part in range(2):
                     start = (side * 2 + part) * E
                     routes[start : start + E, E * n : E * n + E] = route
     else:
-        (sums, above, below, metric, degree, routes, upper, lower, lifts, cat_up, cat_low) = refs
+        (sums, from_in, from_out, metric, degree, routes, inner, outer, lifts, cat_up, cat_low) = refs
+    sign = odd_sign()
     masks = degree_masks(degree)
     kq = lift_weights(metric, stage)
     weights = [[sum(masks[max(i, j)] * kq[j] for j in range(p, N, 2)) for p in range(2)] for i in range(N)]
-    for v, lift_even, lift_odd in far_lifts(above, below, cat_up, cat_low, routes):
+    for v, lift_even, lift_odd in far_lifts(from_in, from_out, cat_up, cat_low, routes):
         for i in range(N):
             rows = slice(64 * v + 8 * i, 64 * v + 8 * i + 8)
             odd_rows = slice(FACE + 64 * v + 8 * i, FACE + 64 * v + 8 * i + 8)
@@ -451,15 +472,15 @@
             lifts[odd_rows, :] = lift_odd[i]
             even = sums[rows, :] + weights[i][0] * lift_even[i]
             odd = sums[odd_rows, :] + weights[i][1] * lift_odd[i]
-            write_traces(even, odd, upper, lower, v, i)
-
-
-def final_kernel(partial, above, below, metric, degree, routes, final, cat_up, cat_low, out, sems):
+            write_traces(even, sign * odd, inner, outer, v, i)
+
+
+def final_kernel(partial, from_in, from_out, metric, degree, routes, final, cat_up, cat_low, out, sems):
     back = 1.0 / jnp.sqrt((2 * iota((8, E), 0) + 1).astype(F32))
     masks = [m * back for m in degree_masks(degree)]
     kq = lift_weights(metric, 2)
     sent = []
-    for v, lift_even, lift_odd in far_lifts(above, below, cat_up, cat_low, routes):
+    for v, lift_even, lift_odd in far_lifts(from_in, from_out, cat_up, cat_low, routes):
         for i in range(N):
             for j in range(N):
                 start = 64 * i + 8 * j
@@ -491,11 +512,18 @@
     return jax.ShapeDtypeStruct(shape, F32)
 
 
-def swap(upper, lower):
+def swap(inner, outer):
     count = lax.axis_size("sub")
-    below = lax.ppermute(upper, "sub", [(i, (i + 1) % count) for i in range(count)])
-    above = lax.ppermute(lower, "sub", [((i + 1) % count, i) for i in range(count)])
-    return above, below
+
+    def partner(c, s):
+        if s in (0, count - 1):
+            return (c ^ 1) * count + s
+        return c * count + (s + 1 if s % 2 else s - 1)
+
+    pairs = [(c * count + s, partner(c, s)) for c in range(lax.axis_size("curve")) for s in range(count)]
+    far = lax.ppermute(outer, ("curve", "sub"), pairs)
+    near = lax.ppermute(inner, "sub", [(s, s ^ 1) for s in range(count)])
+    return near, far
 
 
 def shards(coefficients, old_degree, new_degree, destination, metric, near, mortar_up, mortar_low):
@@ -511,7 +539,7 @@
     packed = packed.reshape(E, 1, BLOCK * E)
     got = lax.all_to_all(packed, ("curve", "sub"), split_axis=0, concat_axis=0, tiled=True)
     got = got.reshape(E * BLOCK, E)
-    place, degree, upper, lower = call(
+    place, degree, inner, outer = call(
         unpack_kernel,
         (jax.ShapeDtypeStruct((E, 2 * E), BF16), f32(8, E), f32(PAY, E), f32(PAY, E)),
         [],
@@ -520,7 +548,7 @@
     faces = (f32(FACE, E), f32(FACE, E))
     cats = [pltpu.VMEM((FACE, 2 * E), BF16)] * 2
     for stage in range(3):
-        above, below = swap(upper, lower)
+        from_in, from_out = swap(inner, outer)
         given = (got, place) if stage == 0 else (first, partial, lifts)
         partial, *sums = call(
             functools.partial(volume_kernel, stage),
@@ -530,24 +558,24 @@
             + [pltpu.VMEM((2 * FACE, E), F32)] * 2
             + [pltpu.VMEM((FACE, 2 * E), BF16), pltpu.VMEM((8 * N, E), F32)]
             + ([pltpu.VMEM((ROWS, E), F32)] if stage else []),
-            given + (degree, upper, lower, metric, near, ztab),
+            given + (degree, inner, outer, metric, near, ztab),
         )
         if stage == 0:
             first = sums.pop()
         body = functools.partial(trace_kernel, stage)
         outs = faces + (f32(2 * FACE, E),)
         if stage == 0:
-            upper, lower, lifts, routes = call(
+            inner, outer, lifts, routes = call(
                 body,
                 outs + (jax.ShapeDtypeStruct((4 * E, 5 * E), BF16),),
                 cats,
-                (*sums, above, below, metric, degree, mortar_up, mortar_low),
+                (*sums, from_in, from_out, metric, degree, mortar_up, mortar_low),
             )
         elif stage == 1:
-            upper, lower, lifts = call(body, outs, cats, (*sums, above, below, metric, degree, routes))
+            inner, outer, lifts = call(body, outs, cats, (*sums, from_in, from_out, metric, degree, routes))
         else:
             scratch = cats + [pltpu.VMEM((NV, MODES, E), F32), pltpu.SemaphoreType.DMA((NV * N,))]
-            args = (partial, above, below, metric, degree, routes)
+            args = (partial, from_in, from_out, metric, degree, routes)
             return call(final_kernel, f32(NV, MODES, E), scratch, args, result=HBM)
 
 

time: 71.4 us -> 71 us (level); the launches traced: 71.3 us -> 69.8 us
  waiting for transfers between devices: 10.4 us -> 7.73 us
  starting transfers between devices: 1.54 us -> 2.75 us
    ppermute x6, waiting for transfers between devices: 10.4 us -> 7.73 us  [the longest x3 7.72 us: swap(): far = lax.ppermute(outer, ('curve', 'sub'), pairs)]
    ppermute x6, starting transfers between devices: 1.54 us -> 2.75 us  [the longest x3 2.28 us: swap(): far = lax.ppermute(outer, ('curve', 'sub'), pairs)]
  transfers between devices with their start and end apart: 6 -> 6, of which waited for: 6 -> 3; matrix products, arithmetic and copies ran while one was open for 0% -> 0% of each run, Pallas kernels for 8% -> 9%
where the time goes in v5:
time: 71 us; the launch traced here: 69.8 us
  blocking collectives  47.7 us (67%)
  Pallas kernels  10.5 us (15%)
  waiting for transfers between devices  7.73 us (11%)
  starting transfers between devices  2.75 us (4%)
  other arithmetic  0.8 us (1%)
    all_to_all x1, blocking collectives, shards(): lax.all_to_all(packed, ('curve', 'sub'), split_axis=0, concat_axis=0, til...  47.7 us
    pallas_call x9, Pallas kernels, call(): pl.pallas_call(kernel, out_shape=outs, in_specs=[VMEM] * len(args), out_s...  10.5 us
    ppermute x3, waiting for transfers between devices, swap(): far = lax.ppermute(outer, ('curve', 'sub'), pairs)  7.72 us
    ppermute x3, starting transfers between devices, swap(): far = lax.ppermute(outer, ('curve', 'sub'), pairs)  2.28 us
  transfers between devices with their start and end apart: 6, of which 3 were waited for; matrix products, arithmetic and copies ran while one was open for 0% of the time, Pallas kernels for 9%

profile of v5, /device:TPU:0, one launch (start us, length us, event | category | flops | bytes accessed | tf_op | source)
XLA Modules:
  0.0 69.8 jit_solution(6243699960379312270)
XLA Ops:
  0.0 0.0 copy-start.1
  0.0 0.8 %pad_add_fusion.index = s32[3,128]{1,0:T(4,128)S(1)} fusion(s32[1,128]{1,0:T(1,128)} %bitcast.8, s32[1,128]{1,0:T(1,128)} %bitcast.9, s32[1,128]{1,0:T(1,128)} %bitcast.10), kind=kLoop, calls=%fused_computation | loop fusion | flops 768 | bytes 3072 | tf_op jit(solution)/shard_map/stack | solution.py:535
  0.8 0.4 shard_map.91
  1.2 0.2 copy-done.1
  1.4 0.6 shard_map.92
  1.9 0.0 copy-start.4
  2.0 0.0 copy-start.5
  2.0 47.7 %all_to_all.5 = f32[128,1,5248]{2,1,0:T(1,128)S(1)} all-to-all(f32[128,1,5248]{2,1,0:T(1,128)S(1)} %bitcast.7), channel_id=1, replica_groups=mesh['curve'=16,'sub'=8] {'curve','sub'}, dimensions={0} | all-to-all | bytes 5373952 | tf_op jit(solution)/shard_map/all_to_all | solution.py:540
  49.7 0.0 copy-done.4
  49.7 0.0 copy-done.5
  49.7 0.0 copy-start
  49.7 0.0 copy-start.2
  49.7 0.0 copy-start.3
  49.7 0.4 shard_map.93
  50.1 0.1 collective-permute-start
  50.2 0.8 %collective-permute-start.1 = (f32[328,128]{1,0:T(8,128)S(1)}, f32[328,128]{1,0:T(8,128)S(1)}, u32[]{:S(2)}, u32[]{:S(2)}) collective-permute-start(f32[328,128]{1,0:T(8,128)S(1)} %get-tuple-element.30.refs_4_), channel_id=1, source_target_pairs={{0,8},{1,2},{2,1},{3,4},{4,3},{5,6},{6,5},{7,15},{8,0},{9,10},{10,... | collective-permute-start | bytes 503816 | tf_op jit(solution)/shard_map/ppermute | solution.py:524
  51.0 0.0 copy-done
  51.0 0.0 copy-done.2
  51.0 0.0 copy-done.3
  51.0 2.0 %shard_map.94 = (f32[2560,128]{1,0:T(8,128)S(1)}, f32[640,128]{1,0:T(8,128)S(1)}, f32[2560,128]{1,0:T(8,128)S(1)}) custom-call(f32[5248,128]{1,0:T(8,128)S(1)} %bitcast.6, bf16[128,256]{1,0:T(8,128)(2,1)S(1)} %get-tuple-element.27.refs_1_, f32[8,128]{1,0:T(8,128)S(1)} %get-tuple-element.28.refs_2_.refs_4_.refs_3_.degree, ...), custom_call_target="tpu_custom_call" | custom-call | tf_op jit(solution)/shard_map/pallas_call | solution.py:500
  53.0 0.0 collective-permute-done.refs_1_
  53.0 2.6 %collective-permute-done.1.refs_2_ = f32[328,128]{1,0:T(8,128)S(1)} collective-permute-done((f32[328,128]{1,0:T(8,128)S(1)}, f32[328,128]{1,0:T(8,128)S(1)}, u32[]{:S(2)}, u32[]{:S(2)}) %collective-permute-start.1) | collective-permute-done | bytes 167968 | tf_op jit(solution)/shard_map/ppermute | solution.py:524
  55.7 0.8 %shard_map.95 = (f32[320,128]{1,0:T(8,128)S(1)}, f32[320,128]{1,0:T(8,128)S(1)}, f32[640,128]{1,0:T(8,128)S(1)}, bf16[512,640]{1,0:T(8,128)(2,1)S(1)}) custom-call(f32[640,128]{1,0:T(8,128)S(1)} %get-tuple-element.33.refs_0_, f32[328,128]{1,0:T(8,128)S(1)} %collective-permute-done.refs_1_, f32[328,128]{1,0:T(8,128)S(1)} %collective-permute-done.1.refs_2_, ...), custom_call_target="tpu_custom_call" | custom-call | tf_op jit(solution)/shard_map/pallas_call | solution.py:500
  56.4 0.2 collective-permute-start.2
  56.6 0.7 %collective-permute-start.3 = (f32[320,128]{1,0:T(8,128)S(1)}, f32[320,128]{1,0:T(8,128)S(1)}, u32[]{:S(2)}, u32[]{:S(2)}) collective-permute-start(f32[320,128]{1,0:T(8,128)S(1)} %get-tuple-element.36.refs_5_), channel_id=1, source_target_pairs={{0,8},{1,2},{2,1},{3,4},{4,3},{5,6},{6,5},{7,15},{8,0},{9,10},{10,... | collective-permute-start | bytes 491528 | tf_op jit(solution)/shard_map/ppermute | solution.py:524
  57.3 2.0 %shard_map.96 = (f32[2560,128]{1,0:T(8,128)S(1)}, f32[640,128]{1,0:T(8,128)S(1)}) custom-call(f32[2560,128]{1,0:T(8,128)S(1)} %get-tuple-element.31.refs_0_, f32[2560,128]{1,0:T(8,128)S(1)} %get-tuple-element.32.refs_1_, f32[640,128]{1,0:T(8,128)S(1)} %get-tuple-element.34.refs_2_, f32[8,128]{1,0:T(8,128)S(1)} %get-tuple-element.28.refs_2_.refs_4_.refs_3_.degree, ...), custom_call_target="tpu_custom_call" | custom-call | tf_op jit(solution)/shard_map/pallas_call | solution.py:500
  59.4 0.0 collective-permute-done.2.refs_1_
  59.4 2.5 %collective-permute-done.3.refs_2_ = f32[320,128]{1,0:T(8,128)S(1)} collective-permute-done((f32[320,128]{1,0:T(8,128)S(1)}, f32[320,128]{1,0:T(8,128)S(1)}, u32[]{:S(2)}, u32[]{:S(2)}) %collective-permute-start.3) | collective-permute-done | bytes 163872 | tf_op jit(solution)/shard_map/ppermute | solution.py:524
  61.9 0.5 shard_map.97
  62.5 0.2 collective-permute-start.4
  62.7 0.7 %collective-permute-start.5 = (f32[320,128]{1,0:T(8,128)S(1)}, f32[320,128]{1,0:T(8,128)S(1)}, u32[]{:S(2)}, u32[]{:S(2)}) collective-permute-start(f32[320,128]{1,0:T(8,128)S(1)} %get-tuple-element.42.refs_5_), channel_id=1, source_target_pairs={{0,8},{1,2},{2,1},{3,4},{4,3},{5,6},{6,5},{7,15},{8,0},{9,10},{10,... | collective-permute-start | bytes 491528 | tf_op jit(solution)/shard_map/ppermute | solution.py:524
  63.4 2.0 %shard_map.98.partial = f32[2560,128]{1,0:T(8,128)S(1)} custom-call(f32[2560,128]{1,0:T(8,128)S(1)} %get-tuple-element.31.refs_0_, f32[2560,128]{1,0:T(8,128)S(1)} %get-tuple-element.37.refs_1_, f32[640,128]{1,0:T(8,128)S(1)} %get-tuple-element.40.refs_2_, f32[8,128]{1,0:T(8,128)S(1)} %get-tuple-element.28.refs_2_.refs_4_.refs_3_.degree, ...), custom_call_target="tpu_custom_call" | custom-call | tf_op jit(solution)/shard_map/pallas_call | solution.py:500
  65.4 0.0 collective-permute-done.4.from_in
  65.4 2.6 %collective-permute-done.5.from_out = f32[320,128]{1,0:T(8,128)S(1)} collective-permute-done((f32[320,128]{1,0:T(8,128)S(1)}, f32[320,128]{1,0:T(8,128)S(1)}, u32[]{:S(2)}, u32[]{:S(2)}) %collective-permute-start.5) | collective-permute-done | bytes 163872 | tf_op jit(solution)/shard_map/ppermute | solution.py:524
  68.0 1.9 %shard_map.99 = f32[5,512,128]{2,1,0:T(8,128)} custom-call(f32[2560,128]{1,0:T(8,128)S(1)} %shard_map.98.partial, f32[320,128]{1,0:T(8,128)S(1)} %collective-permute-done.4.from_in, f32[320,128]{1,0:T(8,128)S(1)} %collective-permute-done.5.from_out, f32[3,128]{1,0:T(4,128)S(1)} %copy-done.2, f32[8,128]{1,0:T(8,128)S(1)} %get-tuple-element.28.refs_2_.refs_4_.refs_3_.degree, ...), custom_call_target="tpu_custom_call" | custom-call | tf_op jit(solution)/shard_map/pallas_call | solution.py:500
Async XLA Ops:
  0.0 1.4 %copy-start.1 = (f32[5,512,128]{2,1,0:T(8,128)S(1)}, f32[5,512,128]{2,1,0:T(8,128)}, u32[]{:S(2)}) copy-start(f32[5,512,128]{2,1,0:T(8,128)} %coef.1) | copy-start | bytes 3932164
  1.9 47.8 %copy-start.4 = (s32[2,144]{1,0:T(2,128)S(1)}, s32[2,144]{1,0:T(2,128)}, u32[]{:S(2)}) copy-start(s32[2,144]{1,0:T(2,128)} %refs_5_.3) | copy-start | bytes 3460
  2.0 47.7 %copy-start.5 = (s32[2,144]{1,0:T(2,128)S(1)}, s32[2,144]{1,0:T(2,128)}, u32[]{:S(2)}) copy-start(s32[2,144]{1,0:T(2,128)} %refs_6_.5) | copy-start | bytes 3460
  49.7 1.3 %copy-start = (bf16[320,256]{1,0:T(8,128)(2,1)S(1)}, bf16[320,256]{1,0:T(8,128)(2,1)}, u32[]{:S(2)}) copy-start(bf16[320,256]{1,0:T(8,128)(2,1)} %constant.2.clone.refs_7_.refs_8_) | copy-start | bytes 491524
  49.7 1.3 %copy-start.2 = (f32[3,128]{1,0:T(4,128)S(1)}, f32[3,128]{1,0:T(4,128)}, u32[]{:S(2)}) copy-start(f32[3,128]{1,0:T(4,128)} %metric.1) | copy-start | bytes 4612
  49.7 1.3 %copy-start.3 = (s32[4,128]{1,0:T(4,128)S(1)}, s32[4,128]{1,0:T(4,128)}, u32[]{:S(2)}) copy-start(s32[4,128]{1,0:T(4,128)} %refs_7_.4) | copy-start | bytes 6148
  50.1 2.9 %collective-permute-start = (f32[328,128]{1,0:T(8,128)S(1)}, f32[328,128]{1,0:T(8,128)S(1)}, u32[]{:S(2)}, u32[]{:S(2)}) collective-permute-start(f32[328,128]{1,0:T(8,128)S(1)} %get-tuple-element.29.refs_3_), channel_id=1, source_target_pairs={{0,1},{1,0},{2,3},{3,2},{4,5},{5,4},{6,7},{7,6},{8,9},{9,8},{10,11... | collective-permute-start | bytes 503816 | tf_op jit(solution)/shard_map/ppermute | solution.py:525
  50.2 5.4 %collective-permute-start.1 = (f32[328,128]{1,0:T(8,128)S(1)}, f32[328,128]{1,0:T(8,128)S(1)}, u32[]{:S(2)}, u32[]{:S(2)}) collective-permute-start(f32[328,128]{1,0:T(8,128)S(1)} %get-tuple-element.30.refs_4_), channel_id=1, source_target_pairs={{0,8},{1,2},{2,1},{3,4},{4,3},{5,6},{6,5},{7,15},{8,0},{9,10},{10,... | collective-permute-start | bytes 503816 | tf_op jit(solution)/shard_map/ppermute | solution.py:524
  56.4 3.0 %collective-permute-start.2 = (f32[320,128]{1,0:T(8,128)S(1)}, f32[320,128]{1,0:T(8,128)S(1)}, u32[]{:S(2)}, u32[]{:S(2)}) collective-permute-start(f32[320,128]{1,0:T(8,128)S(1)} %get-tuple-element.35.refs_4_), channel_id=1, source_target_pairs={{0,1},{1,0},{2,3},{3,2},{4,5},{5,4},{6,7},{7,6},{8,9},{9,8},{10,11... | collective-permute-start | bytes 491528 | tf_op jit(solution)/shard_map/ppermute | solution.py:525
  56.6 5.3 %collective-permute-start.3 = (f32[320,128]{1,0:T(8,128)S(1)}, f32[320,128]{1,0:T(8,128)S(1)}, u32[]{:S(2)}, u32[]{:S(2)}) collective-permute-start(f32[320,128]{1,0:T(8,128)S(1)} %get-tuple-element.36.refs_5_), channel_id=1, source_target_pairs={{0,8},{1,2},{2,1},{3,4},{4,3},{5,6},{6,5},{7,15},{8,0},{9,10},{10,... | collective-permute-start | bytes 491528 | tf_op jit(solution)/shard_map/ppermute | solution.py:524
  62.5 2.9 %collective-permute-start.4 = (f32[320,128]{1,0:T(8,128)S(1)}, f32[320,128]{1,0:T(8,128)S(1)}, u32[]{:S(2)}, u32[]{:S(2)}) collective-permute-start(f32[320,128]{1,0:T(8,128)S(1)} %get-tuple-element.41.refs_4_), channel_id=1, source_target_pairs={{0,1},{1,0},{2,3},{3,2},{4,5},{5,4},{6,7},{7,6},{8,9},{9,8},{10,11... | collective-permute-start | bytes 491528 | tf_op jit(solution)/shard_map/ppermute | solution.py:525
  62.7 5.3 %collective-permute-start.5 = (f32[320,128]{1,0:T(8,128)S(1)}, f32[320,128]{1,0:T(8,128)S(1)}, u32[]{:S(2)}, u32[]{:S(2)}) collective-permute-start(f32[320,128]{1,0:T(8,128)S(1)} %get-tuple-element.42.refs_5_), channel_id=1, source_target_pairs={{0,8},{1,2},{2,1},{3,4},{4,3},{5,6},{6,5},{7,15},{8,0},{9,10},{10,... | collective-permute-start | bytes 491528 | tf_op jit(solution)/shard_map/ppermute | solution.py:524

commit v6 on v5

--- a/solution.py
+++ b/solution.py
@@ -390,18 +390,14 @@
     far_half = jnp.concatenate([pay[1:2, :], pay[3:4, :]], axis=1)
     own_elem, own_half = own(0), own(1)
     far_pick = jnp.where(wide == far_elem, inside, 0.0)
-    own_pick = onehot(wide == own_elem).astype(BF16)
-    far_whole, own_whole = onehot(far_half == 0.0), onehot(own_half == 0.0)
+    own_pick = onehot(wide == own_elem)
     far_1, far_2 = onehot(far_half == 1.0), onehot(far_half == 2.0)
     own_1, own_2 = onehot(own_half == 1.0), onehot(own_half == 2.0)
-    weights = (
-        far_whole * own_whole,
-        own_whole * (far_1 + far_2),
-        own_whole * (far_1 - far_2),
-        far_whole * (own_1 + own_2),
-        far_whole * (own_1 - own_2),
-    )
-    return [dot_nt((far_pick * w).astype(BF16), own_pick).astype(BF16) for w in weights]
+    far_kinds = [(far_pick * w).astype(BF16) for w in (onehot(far_half == 0.0), far_1 + far_2, far_1 - far_2)]
+    own_kinds = [(own_pick * w).astype(BF16) for w in (onehot(own_half == 0.0), own_1 + own_2, own_1 - own_2)]
+    whole = dot_nt(jnp.concatenate(far_kinds, axis=0), own_kinds[0]).astype(BF16)
+    halves = dot_nt(far_kinds[0], jnp.concatenate(own_kinds[1:], axis=0)).astype(BF16)
+    return [whole[E * n : E * n + E] for n in range(3)] + [halves[:, E * n : E * n + E] for n in range(2)]
 
 
 def far_side(first, second, cat, routes):
@@ -479,6 +475,7 @@
     back = 1.0 / jnp.sqrt((2 * iota((8, E), 0) + 1).astype(F32))
     masks = [m * back for m in degree_masks(degree)]
     kq = lift_weights(metric, 2)
+    scales = [[masks[max(i, j)] * (1.0 / math.sqrt((2 * i + 1) * (2 * j + 1))) for j in range(N)] for i in range(N)]
     sent = []
     for v, lift_even, lift_odd in far_lifts(from_in, from_out, cat_up, cat_low, routes):
         for i in range(N):
@@ -486,7 +483,7 @@
                 start = 64 * i + 8 * j
                 lift = (lift_even, lift_odd)[j % 2][i]
                 value = partial[v * MODES + start : v * MODES + start + 8, :] + kq[j] * lift
-                value = (masks[max(i, j)] * (1.0 / math.sqrt((2 * i + 1) * (2 * j + 1)))) * value
+                value = scales[i][j] * value
                 out[v, start : start + 8, :] = value
             part = pl.ds(64 * i, 64)
             copy = pltpu.make_async_copy(out.at[v, part, :], final.at[v, part, :], sems.at[v * N + i])
@@ -521,8 +518,8 @@
         return c * count + (s + 1 if s % 2 else s - 1)
 
     pairs = [(c * count + s, partner(c, s)) for c in range(lax.axis_size("curve")) for s in range(count)]
+    near = lax.ppermute(inner, "sub", [(s, s ^ 1) for s in range(count)])
     far = lax.ppermute(outer, ("curve", "sub"), pairs)
-    near = lax.ppermute(inner, "sub", [(s, s ^ 1) for s in range(count)])
     return near, far
 
 

time: 71 us -> 71 us (level)
  no operation moved by 1% of the time
where the time goes in v6:
time: 71 us; the launch traced here: 69.8 us
  blocking collectives  47.7 us (67%)
  Pallas kernels  10.5 us (15%)
  waiting for transfers between devices  7.73 us (11%)
  starting transfers between devices  2.75 us (4%)
  other arithmetic  0.8 us (1%)
    all_to_all x1, blocking collectives, shards(): lax.all_to_all(packed, ('curve', 'sub'), split_axis=0, concat_axis=0, til...  47.7 us
    pallas_call x9, Pallas kernels, call(): pl.pallas_call(kernel, out_shape=outs, in_specs=[VMEM] * len(args), out_s...  10.5 us
    ppermute x3, waiting for transfers between devices, swap(): far = lax.ppermute(outer, ('curve', 'sub'), pairs)  7.73 us
    ppermute x3, starting transfers between devices, swap(): far = lax.ppermute(outer, ('curve', 'sub'), pairs)  2.28 us
  transfers between devices with their start and end apart: 6, of which 3 were waited for; matrix products, arithmetic and copies ran while one was open for 0% of the time, Pallas kernels for 9%

profile of v6, /device:TPU:0, one launch (start us, length us, event | category | flops | bytes accessed | tf_op | source)
XLA Modules:
  0.0 69.8 jit_solution(12489720262231929405)
XLA Ops:
  0.0 0.0 copy-start.1
  0.0 0.8 %pad_add_fusion.index = s32[3,128]{1,0:T(4,128)S(1)} fusion(s32[1,128]{1,0:T(1,128)} %bitcast.8, s32[1,128]{1,0:T(1,128)} %bitcast.9, s32[1,128]{1,0:T(1,128)} %bitcast.10), kind=kLoop, calls=%fused_computation | loop fusion | flops 768 | bytes 3072 | tf_op jit(solution)/shard_map/stack | solution.py:532
  0.8 0.4 shard_map.91
  1.2 0.2 copy-done.1
  1.4 0.6 shard_map.92
  1.9 0.0 copy-start.4
  2.0 0.0 copy-start.5
  2.0 47.7 %all_to_all.5 = f32[128,1,5248]{2,1,0:T(1,128)S(1)} all-to-all(f32[128,1,5248]{2,1,0:T(1,128)S(1)} %bitcast.7), channel_id=1, replica_groups=mesh['curve'=16,'sub'=8] {'curve','sub'}, dimensions={0} | all-to-all | bytes 5373952 | tf_op jit(solution)/shard_map/all_to_all | solution.py:537
  49.7 0.0 copy-done.4
  49.7 0.0 copy-done.5
  49.7 0.0 copy-start
  49.7 0.0 copy-start.2
  49.7 0.0 copy-start.3
  49.7 0.4 shard_map.93
  50.1 0.1 collective-permute-start
  50.2 0.8 %collective-permute-start.1 = (f32[328,128]{1,0:T(8,128)S(1)}, f32[328,128]{1,0:T(8,128)S(1)}, u32[]{:S(2)}, u32[]{:S(2)}) collective-permute-start(f32[328,128]{1,0:T(8,128)S(1)} %get-tuple-element.30.refs_4_), channel_id=1, source_target_pairs={{0,8},{1,2},{2,1},{3,4},{4,3},{5,6},{6,5},{7,15},{8,0},{9,10},{10,... | collective-permute-start | bytes 503816 | tf_op jit(solution)/shard_map/ppermute | solution.py:522
  51.0 0.0 copy-done
  51.0 0.0 copy-done.2
  51.0 0.0 copy-done.3
  51.0 2.0 %shard_map.94 = (f32[2560,128]{1,0:T(8,128)S(1)}, f32[640,128]{1,0:T(8,128)S(1)}, f32[2560,128]{1,0:T(8,128)S(1)}) custom-call(f32[5248,128]{1,0:T(8,128)S(1)} %bitcast.6, bf16[128,256]{1,0:T(8,128)(2,1)S(1)} %get-tuple-element.27.refs_1_, f32[8,128]{1,0:T(8,128)S(1)} %get-tuple-element.28.refs_2_.refs_4_.refs_3_.degree, ...), custom_call_target="tpu_custom_call" | custom-call | tf_op jit(solution)/shard_map/pallas_call | solution.py:497
  53.0 0.0 collective-permute-done.refs_1_
  53.0 2.6 %collective-permute-done.1.refs_2_ = f32[328,128]{1,0:T(8,128)S(1)} collective-permute-done((f32[328,128]{1,0:T(8,128)S(1)}, f32[328,128]{1,0:T(8,128)S(1)}, u32[]{:S(2)}, u32[]{:S(2)}) %collective-permute-start.1) | collective-permute-done | bytes 167968 | tf_op jit(solution)/shard_map/ppermute | solution.py:522
  55.7 0.8 %shard_map.95 = (f32[320,128]{1,0:T(8,128)S(1)}, f32[320,128]{1,0:T(8,128)S(1)}, f32[640,128]{1,0:T(8,128)S(1)}, bf16[512,640]{1,0:T(8,128)(2,1)S(1)}) custom-call(f32[640,128]{1,0:T(8,128)S(1)} %get-tuple-element.33.refs_0_, f32[328,128]{1,0:T(8,128)S(1)} %collective-permute-done.refs_1_, f32[328,128]{1,0:T(8,128)S(1)} %collective-permute-done.1.refs_2_, ...), custom_call_target="tpu_custom_call" | custom-call | tf_op jit(solution)/shard_map/pallas_call | solution.py:497
  56.4 0.2 collective-permute-start.2
  56.6 0.7 %collective-permute-start.3 = (f32[320,128]{1,0:T(8,128)S(1)}, f32[320,128]{1,0:T(8,128)S(1)}, u32[]{:S(2)}, u32[]{:S(2)}) collective-permute-start(f32[320,128]{1,0:T(8,128)S(1)} %get-tuple-element.36.refs_5_), channel_id=1, source_target_pairs={{0,8},{1,2},{2,1},{3,4},{4,3},{5,6},{6,5},{7,15},{8,0},{9,10},{10,... | collective-permute-start | bytes 491528 | tf_op jit(solution)/shard_map/ppermute | solution.py:522
  57.4 2.0 %shard_map.96 = (f32[2560,128]{1,0:T(8,128)S(1)}, f32[640,128]{1,0:T(8,128)S(1)}) custom-call(f32[2560,128]{1,0:T(8,128)S(1)} %get-tuple-element.31.refs_0_, f32[2560,128]{1,0:T(8,128)S(1)} %get-tuple-element.32.refs_1_, f32[640,128]{1,0:T(8,128)S(1)} %get-tuple-element.34.refs_2_, f32[8,128]{1,0:T(8,128)S(1)} %get-tuple-element.28.refs_2_.refs_4_.refs_3_.degree, ...), custom_call_target="tpu_custom_call" | custom-call | tf_op jit(solution)/shard_map/pallas_call | solution.py:497
  59.4 0.0 collective-permute-done.2.refs_1_
  59.4 2.5 %collective-permute-done.3.refs_2_ = f32[320,128]{1,0:T(8,128)S(1)} collective-permute-done((f32[320,128]{1,0:T(8,128)S(1)}, f32[320,128]{1,0:T(8,128)S(1)}, u32[]{:S(2)}, u32[]{:S(2)}) %collective-permute-start.3) | collective-permute-done | bytes 163872 | tf_op jit(solution)/shard_map/ppermute | solution.py:522
  62.0 0.5 shard_map.97
  62.5 0.2 collective-permute-start.4
  62.7 0.7 %collective-permute-start.5 = (f32[320,128]{1,0:T(8,128)S(1)}, f32[320,128]{1,0:T(8,128)S(1)}, u32[]{:S(2)}, u32[]{:S(2)}) collective-permute-start(f32[320,128]{1,0:T(8,128)S(1)} %get-tuple-element.42.refs_5_), channel_id=1, source_target_pairs={{0,8},{1,2},{2,1},{3,4},{4,3},{5,6},{6,5},{7,15},{8,0},{9,10},{10,... | collective-permute-start | bytes 491528 | tf_op jit(solution)/shard_map/ppermute | solution.py:522
  63.4 2.0 %shard_map.98.partial = f32[2560,128]{1,0:T(8,128)S(1)} custom-call(f32[2560,128]{1,0:T(8,128)S(1)} %get-tuple-element.31.refs_0_, f32[2560,128]{1,0:T(8,128)S(1)} %get-tuple-element.37.refs_1_, f32[640,128]{1,0:T(8,128)S(1)} %get-tuple-element.40.refs_2_, f32[8,128]{1,0:T(8,128)S(1)} %get-tuple-element.28.refs_2_.refs_4_.refs_3_.degree, ...), custom_call_target="tpu_custom_call" | custom-call | tf_op jit(solution)/shard_map/pallas_call | solution.py:497
  65.4 0.0 collective-permute-done.4.from_in
  65.4 2.6 %collective-permute-done.5.from_out = f32[320,128]{1,0:T(8,128)S(1)} collective-permute-done((f32[320,128]{1,0:T(8,128)S(1)}, f32[320,128]{1,0:T(8,128)S(1)}, u32[]{:S(2)}, u32[]{:S(2)}) %collective-permute-start.5) | collective-permute-done | bytes 163872 | tf_op jit(solution)/shard_map/ppermute | solution.py:522
  68.0 1.8 %shard_map.99 = f32[5,512,128]{2,1,0:T(8,128)} custom-call(f32[2560,128]{1,0:T(8,128)S(1)} %shard_map.98.partial, f32[320,128]{1,0:T(8,128)S(1)} %collective-permute-done.4.from_in, f32[320,128]{1,0:T(8,128)S(1)} %collective-permute-done.5.from_out, f32[3,128]{1,0:T(4,128)S(1)} %copy-done.2, f32[8,128]{1,0:T(8,128)S(1)} %get-tuple-element.28.refs_2_.refs_4_.refs_3_.degree, ...), custom_call_target="tpu_custom_call" | custom-call | tf_op jit(solution)/shard_map/pallas_call | solution.py:497
Async XLA Ops:
  0.0 1.4 %copy-start.1 = (f32[5,512,128]{2,1,0:T(8,128)S(1)}, f32[5,512,128]{2,1,0:T(8,128)}, u32[]{:S(2)}) copy-start(f32[5,512,128]{2,1,0:T(8,128)} %coef.1) | copy-start | bytes 3932164
  1.9 47.8 %copy-start.4 = (s32[2,144]{1,0:T(2,128)S(1)}, s32[2,144]{1,0:T(2,128)}, u32[]{:S(2)}) copy-start(s32[2,144]{1,0:T(2,128)} %refs_5_.3) | copy-start | bytes 3460
  2.0 47.7 %copy-start.5 = (s32[2,144]{1,0:T(2,128)S(1)}, s32[2,144]{1,0:T(2,128)}, u32[]{:S(2)}) copy-start(s32[2,144]{1,0:T(2,128)} %refs_6_.5) | copy-start | bytes 3460
  49.7 1.3 %copy-start = (bf16[320,256]{1,0:T(8,128)(2,1)S(1)}, bf16[320,256]{1,0:T(8,128)(2,1)}, u32[]{:S(2)}) copy-start(bf16[320,256]{1,0:T(8,128)(2,1)} %constant.2.clone.refs_7_.refs_8_) | copy-start | bytes 491524
  49.7 1.3 %copy-start.2 = (f32[3,128]{1,0:T(4,128)S(1)}, f32[3,128]{1,0:T(4,128)}, u32[]{:S(2)}) copy-start(f32[3,128]{1,0:T(4,128)} %metric.1) | copy-start | bytes 4612
  49.7 1.3 %copy-start.3 = (s32[4,128]{1,0:T(4,128)S(1)}, s32[4,128]{1,0:T(4,128)}, u32[]{:S(2)}) copy-start(s32[4,128]{1,0:T(4,128)} %refs_7_.4) | copy-start | bytes 6148
  50.1 2.9 %collective-permute-start = (f32[328,128]{1,0:T(8,128)S(1)}, f32[328,128]{1,0:T(8,128)S(1)}, u32[]{:S(2)}, u32[]{:S(2)}) collective-permute-start(f32[328,128]{1,0:T(8,128)S(1)} %get-tuple-element.29.refs_3_), channel_id=1, source_target_pairs={{0,1},{1,0},{2,3},{3,2},{4,5},{5,4},{6,7},{7,6},{8,9},{9,8},{10,11... | collective-permute-start | bytes 503816 | tf_op jit(solution)/shard_map/ppermute | solution.py:521
  50.2 5.4 %collective-permute-start.1 = (f32[328,128]{1,0:T(8,128)S(1)}, f32[328,128]{1,0:T(8,128)S(1)}, u32[]{:S(2)}, u32[]{:S(2)}) collective-permute-start(f32[328,128]{1,0:T(8,128)S(1)} %get-tuple-element.30.refs_4_), channel_id=1, source_target_pairs={{0,8},{1,2},{2,1},{3,4},{4,3},{5,6},{6,5},{7,15},{8,0},{9,10},{10,... | collective-permute-start | bytes 503816 | tf_op jit(solution)/shard_map/ppermute | solution.py:522
  56.4 3.0 %collective-permute-start.2 = (f32[320,128]{1,0:T(8,128)S(1)}, f32[320,128]{1,0:T(8,128)S(1)}, u32[]{:S(2)}, u32[]{:S(2)}) collective-permute-start(f32[320,128]{1,0:T(8,128)S(1)} %get-tuple-element.35.refs_4_), channel_id=1, source_target_pairs={{0,1},{1,0},{2,3},{3,2},{4,5},{5,4},{6,7},{7,6},{8,9},{9,8},{10,11... | collective-permute-start | bytes 491528 | tf_op jit(solution)/shard_map/ppermute | solution.py:521
  56.6 5.3 %collective-permute-start.3 = (f32[320,128]{1,0:T(8,128)S(1)}, f32[320,128]{1,0:T(8,128)S(1)}, u32[]{:S(2)}, u32[]{:S(2)}) collective-permute-start(f32[320,128]{1,0:T(8,128)S(1)} %get-tuple-element.36.refs_5_), channel_id=1, source_target_pairs={{0,8},{1,2},{2,1},{3,4},{4,3},{5,6},{6,5},{7,15},{8,0},{9,10},{10,... | collective-permute-start | bytes 491528 | tf_op jit(solution)/shard_map/ppermute | solution.py:522
  62.5 2.9 %collective-permute-start.4 = (f32[320,128]{1,0:T(8,128)S(1)}, f32[320,128]{1,0:T(8,128)S(1)}, u32[]{:S(2)}, u32[]{:S(2)}) collective-permute-start(f32[320,128]{1,0:T(8,128)S(1)} %get-tuple-element.41.refs_4_), channel_id=1, source_target_pairs={{0,1},{1,0},{2,3},{3,2},{4,5},{5,4},{6,7},{7,6},{8,9},{9,8},{10,11... | collective-permute-start | bytes 491528 | tf_op jit(solution)/shard_map/ppermute | solution.py:521
  62.7 5.3 %collective-permute-start.5 = (f32[320,128]{1,0:T(8,128)S(1)}, f32[320,128]{1,0:T(8,128)S(1)}, u32[]{:S(2)}, u32[]{:S(2)}) collective-permute-start(f32[320,128]{1,0:T(8,128)S(1)} %get-tuple-element.42.refs_5_), channel_id=1, source_target_pairs={{0,8},{1,2},{2,1},{3,4},{4,3},{5,6},{6,5},{7,15},{8,0},{9,10},{10,... | collective-permute-start | bytes 491528 | tf_op jit(solution)/shard_map/ppermute | solution.py:522

commit v7 on v5

--- a/solution.py
+++ b/solution.py
@@ -517,7 +517,7 @@
 
     def partner(c, s):
         if s in (0, count - 1):
-            return (c ^ 1) * count + s
+            return (c ^ 4) * count + s
         return c * count + (s + 1 if s % 2 else s - 1)
 
     pairs = [(c * count + s, partner(c, s)) for c in range(lax.axis_size("curve")) for s in range(count)]

time: 71 us -> 71 us (level)
  no operation moved by 1% of the time
where the time goes in v7:
time: 71 us; the launch traced here: 69.8 us
  blocking collectives  47.7 us (67%)
  Pallas kernels  10.5 us (15%)
  waiting for transfers between devices  8.34 us (12%)
  starting transfers between devices  2.14 us (3%)
  other arithmetic  0.8 us (1%)
    all_to_all x1, blocking collectives, shards(): lax.all_to_all(packed, ('curve', 'sub'), split_axis=0, concat_axis=0, til...  47.7 us
    pallas_call x9, Pallas kernels, call(): pl.pallas_call(kernel, out_shape=outs, in_specs=[VMEM] * len(args), out_s...  10.5 us
    ppermute x3, waiting for transfers between devices, swap(): far = lax.ppermute(outer, ('curve', 'sub'), pairs)  8.33 us
    ppermute x3, starting transfers between devices, swap(): far = lax.ppermute(outer, ('curve', 'sub'), pairs)  1.67 us
  transfers between devices with their start and end apart: 6, of which 3 were waited for; matrix products, arithmetic and copies ran while one was open for 0% of the time, Pallas kernels for 9%

profile of v7, /device:TPU:0, one launch (start us, length us, event | category | flops | bytes accessed | tf_op | source)
XLA Modules:
  0.0 69.8 jit_solution(4886445458165675041)
XLA Ops:
  0.0 0.0 copy-start.1
  0.0 0.8 %pad_add_fusion.index = s32[3,128]{1,0:T(4,128)S(1)} fusion(s32[1,128]{1,0:T(1,128)} %bitcast.8, s32[1,128]{1,0:T(1,128)} %bitcast.9, s32[1,128]{1,0:T(1,128)} %bitcast.10), kind=kLoop, calls=%fused_computation | loop fusion | flops 768 | bytes 3072 | tf_op jit(solution)/shard_map/stack | solution.py:535
  0.8 0.4 shard_map.91
  1.2 0.2 copy-done.1
  1.4 0.6 shard_map.92
  1.9 0.0 copy-start.4
  2.0 0.0 copy-start.5
  2.0 47.7 %all_to_all.5 = f32[128,1,5248]{2,1,0:T(1,128)S(1)} all-to-all(f32[128,1,5248]{2,1,0:T(1,128)S(1)} %bitcast.7), channel_id=1, replica_groups=mesh['curve'=16,'sub'=8] {'curve','sub'}, dimensions={0} | all-to-all | bytes 5373952 | tf_op jit(solution)/shard_map/all_to_all | solution.py:540
  49.7 0.0 copy-done.4
  49.7 0.0 copy-done.5
  49.7 0.0 copy-start
  49.7 0.0 copy-start.2
  49.7 0.0 copy-start.3
  49.7 0.4 shard_map.93
  50.1 0.1 collective-permute-start
  50.2 0.6 collective-permute-start.1
  50.8 0.0 copy-done
  50.8 0.0 copy-done.2
  50.8 0.0 copy-done.3
  50.8 2.0 %shard_map.94 = (f32[2560,128]{1,0:T(8,128)S(1)}, f32[640,128]{1,0:T(8,128)S(1)}, f32[2560,128]{1,0:T(8,128)S(1)}) custom-call(f32[5248,128]{1,0:T(8,128)S(1)} %bitcast.6, bf16[128,256]{1,0:T(8,128)(2,1)S(1)} %get-tuple-element.27.refs_1_, f32[8,128]{1,0:T(8,128)S(1)} %get-tuple-element.28.refs_2_.refs_4_.refs_3_.degree, ...), custom_call_target="tpu_custom_call" | custom-call | tf_op jit(solution)/shard_map/pallas_call | solution.py:500
  52.8 0.0 collective-permute-done.refs_1_
  52.8 2.8 %collective-permute-done.1.refs_2_ = f32[328,128]{1,0:T(8,128)S(1)} collective-permute-done((f32[328,128]{1,0:T(8,128)S(1)}, f32[328,128]{1,0:T(8,128)S(1)}, u32[]{:S(2)}, u32[]{:S(2)}) %collective-permute-start.1) | collective-permute-done | bytes 167968 | tf_op jit(solution)/shard_map/ppermute | solution.py:524
  55.7 0.8 %shard_map.95 = (f32[320,128]{1,0:T(8,128)S(1)}, f32[320,128]{1,0:T(8,128)S(1)}, f32[640,128]{1,0:T(8,128)S(1)}, bf16[512,640]{1,0:T(8,128)(2,1)S(1)}) custom-call(f32[640,128]{1,0:T(8,128)S(1)} %get-tuple-element.33.refs_0_, f32[328,128]{1,0:T(8,128)S(1)} %collective-permute-done.refs_1_, f32[328,128]{1,0:T(8,128)S(1)} %collective-permute-done.1.refs_2_, ...), custom_call_target="tpu_custom_call" | custom-call | tf_op jit(solution)/shard_map/pallas_call | solution.py:500
  56.4 0.2 collective-permute-start.2
  56.6 0.5 collective-permute-start.3
  57.1 2.0 %shard_map.96 = (f32[2560,128]{1,0:T(8,128)S(1)}, f32[640,128]{1,0:T(8,128)S(1)}) custom-call(f32[2560,128]{1,0:T(8,128)S(1)} %get-tuple-element.31.refs_0_, f32[2560,128]{1,0:T(8,128)S(1)} %get-tuple-element.32.refs_1_, f32[640,128]{1,0:T(8,128)S(1)} %get-tuple-element.34.refs_2_, f32[8,128]{1,0:T(8,128)S(1)} %get-tuple-element.28.refs_2_.refs_4_.refs_3_.degree, ...), custom_call_target="tpu_custom_call" | custom-call | tf_op jit(solution)/shard_map/pallas_call | solution.py:500
  59.2 0.0 collective-permute-done.2.refs_1_
  59.2 2.7 %collective-permute-done.3.refs_2_ = f32[320,128]{1,0:T(8,128)S(1)} collective-permute-done((f32[320,128]{1,0:T(8,128)S(1)}, f32[320,128]{1,0:T(8,128)S(1)}, u32[]{:S(2)}, u32[]{:S(2)}) %collective-permute-start.3) | collective-permute-done | bytes 163872 | tf_op jit(solution)/shard_map/ppermute | solution.py:524
  61.9 0.5 shard_map.97
  62.5 0.2 collective-permute-start.4
  62.7 0.5 collective-permute-start.5
  63.2 2.0 %shard_map.98.partial = f32[2560,128]{1,0:T(8,128)S(1)} custom-call(f32[2560,128]{1,0:T(8,128)S(1)} %get-tuple-element.31.refs_0_, f32[2560,128]{1,0:T(8,128)S(1)} %get-tuple-element.37.refs_1_, f32[640,128]{1,0:T(8,128)S(1)} %get-tuple-element.40.refs_2_, f32[8,128]{1,0:T(8,128)S(1)} %get-tuple-element.28.refs_2_.refs_4_.refs_3_.degree, ...), custom_call_target="tpu_custom_call" | custom-call | tf_op jit(solution)/shard_map/pallas_call | solution.py:500
  65.2 0.0 collective-permute-done.4.from_in
  65.2 2.8 %collective-permute-done.5.from_out = f32[320,128]{1,0:T(8,128)S(1)} collective-permute-done((f32[320,128]{1,0:T(8,128)S(1)}, f32[320,128]{1,0:T(8,128)S(1)}, u32[]{:S(2)}, u32[]{:S(2)}) %collective-permute-start.5) | collective-permute-done | bytes 163872 | tf_op jit(solution)/shard_map/ppermute | solution.py:524
  68.0 1.9 %shard_map.99 = f32[5,512,128]{2,1,0:T(8,128)} custom-call(f32[2560,128]{1,0:T(8,128)S(1)} %shard_map.98.partial, f32[320,128]{1,0:T(8,128)S(1)} %collective-permute-done.4.from_in, f32[320,128]{1,0:T(8,128)S(1)} %collective-permute-done.5.from_out, f32[3,128]{1,0:T(4,128)S(1)} %copy-done.2, f32[8,128]{1,0:T(8,128)S(1)} %get-tuple-element.28.refs_2_.refs_4_.refs_3_.degree, ...), custom_call_target="tpu_custom_call" | custom-call | tf_op jit(solution)/shard_map/pallas_call | solution.py:500
Async XLA Ops:
  0.0 1.4 %copy-start.1 = (f32[5,512,128]{2,1,0:T(8,128)S(1)}, f32[5,512,128]{2,1,0:T(8,128)}, u32[]{:S(2)}) copy-start(f32[5,512,128]{2,1,0:T(8,128)} %coef.1) | copy-start | bytes 3932164
  1.9 47.8 %copy-start.4 = (s32[2,144]{1,0:T(2,128)S(1)}, s32[2,144]{1,0:T(2,128)}, u32[]{:S(2)}) copy-start(s32[2,144]{1,0:T(2,128)} %refs_5_.3) | copy-start | bytes 3460
  2.0 47.7 %copy-start.5 = (s32[2,144]{1,0:T(2,128)S(1)}, s32[2,144]{1,0:T(2,128)}, u32[]{:S(2)}) copy-start(s32[2,144]{1,0:T(2,128)} %refs_6_.5) | copy-start | bytes 3460
  49.7 1.1 %copy-start = (bf16[320,256]{1,0:T(8,128)(2,1)S(1)}, bf16[320,256]{1,0:T(8,128)(2,1)}, u32[]{:S(2)}) copy-start(bf16[320,256]{1,0:T(8,128)(2,1)} %constant.2.clone.refs_7_.refs_8_) | copy-start | bytes 491524
  49.7 1.1 %copy-start.2 = (f32[3,128]{1,0:T(4,128)S(1)}, f32[3,128]{1,0:T(4,128)}, u32[]{:S(2)}) copy-start(f32[3,128]{1,0:T(4,128)} %metric.1) | copy-start | bytes 4612
  49.7 1.1 %copy-start.3 = (s32[4,128]{1,0:T(4,128)S(1)}, s32[4,128]{1,0:T(4,128)}, u32[]{:S(2)}) copy-start(s32[4,128]{1,0:T(4,128)} %refs_7_.4) | copy-start | bytes 6148
  50.1 2.7 %collective-permute-start = (f32[328,128]{1,0:T(8,128)S(1)}, f32[328,128]{1,0:T(8,128)S(1)}, u32[]{:S(2)}, u32[]{:S(2)}) collective-permute-start(f32[328,128]{1,0:T(8,128)S(1)} %get-tuple-element.29.refs_3_), channel_id=1, source_target_pairs={{0,1},{1,0},{2,3},{3,2},{4,5},{5,4},{6,7},{7,6},{8,9},{9,8},{10,11... | collective-permute-start | bytes 503816 | tf_op jit(solution)/shard_map/ppermute | solution.py:525
  50.2 5.4 %collective-permute-start.1 = (f32[328,128]{1,0:T(8,128)S(1)}, f32[328,128]{1,0:T(8,128)S(1)}, u32[]{:S(2)}, u32[]{:S(2)}) collective-permute-start(f32[328,128]{1,0:T(8,128)S(1)} %get-tuple-element.30.refs_4_), channel_id=1, source_target_pairs={{0,32},{1,2},{2,1},{3,4},{4,3},{5,6},{6,5},{7,39},{8,40},{9,10},{1... | collective-permute-start | bytes 503816 | tf_op jit(solution)/shard_map/ppermute | solution.py:524
  56.4 2.8 %collective-permute-start.2 = (f32[320,128]{1,0:T(8,128)S(1)}, f32[320,128]{1,0:T(8,128)S(1)}, u32[]{:S(2)}, u32[]{:S(2)}) collective-permute-start(f32[320,128]{1,0:T(8,128)S(1)} %get-tuple-element.35.refs_4_), channel_id=1, source_target_pairs={{0,1},{1,0},{2,3},{3,2},{4,5},{5,4},{6,7},{7,6},{8,9},{9,8},{10,11... | collective-permute-start | bytes 491528 | tf_op jit(solution)/shard_map/ppermute | solution.py:525
  56.6 5.3 %collective-permute-start.3 = (f32[320,128]{1,0:T(8,128)S(1)}, f32[320,128]{1,0:T(8,128)S(1)}, u32[]{:S(2)}, u32[]{:S(2)}) collective-permute-start(f32[320,128]{1,0:T(8,128)S(1)} %get-tuple-element.36.refs_5_), channel_id=1, source_target_pairs={{0,32},{1,2},{2,1},{3,4},{4,3},{5,6},{6,5},{7,39},{8,40},{9,10},{1... | collective-permute-start | bytes 491528 | tf_op jit(solution)/shard_map/ppermute | solution.py:524
  62.5 2.7 %collective-permute-start.4 = (f32[320,128]{1,0:T(8,128)S(1)}, f32[320,128]{1,0:T(8,128)S(1)}, u32[]{:S(2)}, u32[]{:S(2)}) collective-permute-start(f32[320,128]{1,0:T(8,128)S(1)} %get-tuple-element.41.refs_4_), channel_id=1, source_target_pairs={{0,1},{1,0},{2,3},{3,2},{4,5},{5,4},{6,7},{7,6},{8,9},{9,8},{10,11... | collective-permute-start | bytes 491528 | tf_op jit(solution)/shard_map/ppermute | solution.py:525
  62.7 5.3 %collective-permute-start.5 = (f32[320,128]{1,0:T(8,128)S(1)}, f32[320,128]{1,0:T(8,128)S(1)}, u32[]{:S(2)}, u32[]{:S(2)}) collective-permute-start(f32[320,128]{1,0:T(8,128)S(1)} %get-tuple-element.42.refs_5_), channel_id=1, source_target_pairs={{0,32},{1,2},{2,1},{3,4},{4,3},{5,6},{6,5},{7,39},{8,40},{9,10},{1... | collective-permute-start | bytes 491528 | tf_op jit(solution)/shard_map/ppermute | solution.py:524
